TPU v7x, 256 devices: a whole 4x4x8 slice. The times are simulated.
256 devices in a mesh: dp: 16 (over x, z_lo), seq: 16 (over y, z_hi, core).
Axes of the slice: x: 4, y: 4, z: 8 (z_hi: 2, z_lo: 4; z = z_hi * 4 + z_lo), core: 2. Of those that a mesh axis runs over, the one named last changes fastest.
Arguments:
- frames_in: bfloat16 [16, 4096, 1536], P('dp', 'seq'), may hold values from -6 to 6
- cotangent: bfloat16 [16, 4096, 1536], P('dp', 'seq'), may hold values from -0.09375 to 0.09375
- lengths: int32 [16], P('dp'), may hold values from 1024 to 4096, as said below
- out_weight: bfloat16 [1536, 1536], replicated, may hold values from -0.15625 to 0.15625
- conv_kernel: float32 [32, 1536], replicated, may hold values from -1 to 1
- layer_norm_gain: float32 [1536], replicated, may hold values from 0.5 to 1.5
Outputs:
- input_grad: bfloat16 [16, 4096, 1536], P('dp', 'seq')
- fisher_out: float32 [1536, 1536], P('seq', 'dp')
- fisher_kernel: float32 [32, 1536], P('dp', 'seq')
- fisher_gain: float32 [1536], P('seq')
Inputs may be any that keep to these rules, and one draw needn't show every extreme that they name: `lengths`: every recording has at least 1024 valid frames, and at least one recording is valid over all 4096 frames.
All inputs are finite; a program needn't handle non-finite values.
Results may differ from a plain program's by a relative error of at most 0.0049.
Values may be sent and summed in bfloat16 or wider, within the bound.
No kernel may reach another device: no remote copies, remote signals or barrier semaphores. Data moves between devices by JAX's collectives and lax.ppermute only.
A program may use at most 64 MiB of HBM per device.

v0:
```python
import jax
import jax.numpy as jnp
from jax import lax
from jax.sharding import PartitionSpec as P

KW = 32


def with_halo(block, sides, width):
    for axis, dim in sides:
        count = lax.axis_size(axis)
        forward = [(i, i + 1) for i in range(count - 1)]
        backward = [(target, source) for source, target in forward]
        low = lax.ppermute(
            lax.slice_in_dim(block, block.shape[dim] - width, None, axis=dim), axis, forward
        )
        high = lax.ppermute(lax.slice_in_dim(block, 0, width, axis=dim), axis, backward)
        block = jnp.concatenate([low, block, high], axis=dim)
    return block


def on_device(frames_in, cotangent, lengths, out_weight, conv_kernel, layer_norm_gain):
    frame_count = frames_in.shape[1]
    width = out_weight.shape[0]
    half_width = KW // 2
    first_frame = lax.axis_index("seq") * frame_count
    position = first_frame + jnp.arange(frame_count, dtype=jnp.int32)
    valid_mask = (position < lengths[0]).astype(jnp.float32)[:, None]
    masked = (frames_in[0].astype(jnp.float32) * valid_mask).astype(jnp.bfloat16)
    padded = with_halo(masked, (("seq", 0),), half_width)
    padded_wide = padded.astype(jnp.float32)
    conv_out = jnp.zeros((frame_count, width), jnp.float32)
    for offset in range(KW):
        conv_out = conv_out + conv_kernel[offset] * padded_wide[offset : offset + frame_count]
    row_mean = jnp.mean(conv_out, axis=1, keepdims=True)
    centered_input = conv_out - row_mean
    inverse_deviation = lax.rsqrt(
        jnp.mean(centered_input * centered_input, axis=1, keepdims=True) + 1e-05
    )
    standardized_input = centered_input * inverse_deviation
    normalized_input = standardized_input * layer_norm_gain
    sigma = jax.nn.sigmoid(normalized_input)
    hidden = (normalized_input * sigma).astype(jnp.bfloat16)
    grad_out = (cotangent[0].astype(jnp.float32) * valid_mask).astype(jnp.bfloat16)
    out_grad = lax.dot_general(
        hidden, grad_out, (((0,), (0,)), ((), ())), preferred_element_type=jnp.float32
    )
    hidden_grad = lax.dot_general(
        grad_out, out_weight, (((1,), (1,)), ((), ())), preferred_element_type=jnp.float32
    )
    normalized_gradient = hidden_grad * (sigma + normalized_input * sigma * (1.0 - sigma))
    gain_gradient = jnp.sum(normalized_gradient * standardized_input, axis=0)
    scaled_output = normalized_gradient * layer_norm_gain
    convolved_gradient = inverse_deviation * (
        scaled_output
        - jnp.mean(scaled_output, axis=1, keepdims=True)
        - standardized_input * jnp.mean(scaled_output * standardized_input, axis=1, keepdims=True)
    )
    convolved_gradient = convolved_gradient.astype(jnp.bfloat16)
    conv_wide = convolved_gradient.astype(jnp.float32)
    kernel_rows = []
    for offset in range(KW):
        kernel_rows.append(jnp.sum(conv_wide * padded_wide[offset : offset + frame_count], axis=0))
    kernel_grad = jnp.stack(kernel_rows)
    grad_padded = with_halo(convolved_gradient, (("seq", 0),), half_width)
    grad_padded = grad_padded.astype(jnp.float32)
    summed = jnp.zeros((frame_count, width), jnp.float32)
    for offset in range(KW):
        begin = 2 * half_width - offset
        summed = summed + conv_kernel[offset] * grad_padded[begin : begin + frame_count]
    input_grad = (summed * valid_mask).astype(jnp.bfloat16)[None]
    share = width // lax.axis_size("seq")
    seq_place = lax.axis_index("seq") * share
    out_total = lax.psum_scatter(out_grad, "seq", scatter_dimension=0, tiled=True)
    kernel_total, gain_total = lax.psum((kernel_grad, gain_gradient), "seq")
    kernel_square = kernel_total * kernel_total
    gain_square = gain_total * gain_total
    kernel_square = lax.dynamic_slice_in_dim(kernel_square, seq_place, share, 1)
    gain_square = lax.dynamic_slice_in_dim(gain_square, seq_place, share, 0)
    out_square = out_total * out_total
    out_whole, kernel_whole = lax.psum((out_square, kernel_square), "dp")
    column_share = width // lax.axis_size("dp")
    kernel_rows_share = KW // lax.axis_size("dp")
    fisher_out = lax.dynamic_slice_in_dim(
        out_whole, lax.axis_index("dp") * column_share, column_share, 1
    )
    fisher_kernel = lax.dynamic_slice_in_dim(
        kernel_whole, lax.axis_index("dp") * kernel_rows_share, kernel_rows_share, 0
    )
    fisher_gain = lax.psum(gain_square, "dp")
    record_count = frames_in.shape[0] * lax.axis_size("dp")
    return (
        input_grad,
        fisher_out / record_count,
        fisher_kernel / record_count,
        fisher_gain / record_count,
    )


def solution(mesh):
    return jax.shard_map(
        on_device,
        mesh=mesh,
        in_specs=(P("dp", "seq", None), P("dp", "seq", None), P("dp"), P(), P(), P()),
        out_specs=(P("dp", "seq", None), P("seq", "dp"), P("dp", "seq"), P("seq")),
        check_vma=False,
    )
```

profile of v0, /device:TPU:6, one launch (start us, length us, event | category | flops | bytes accessed | tf_op | source)
XLA Modules:
  0.0 524.3 jit_solution(6748945795130323513)
XLA Ops:
  7.2 0.0 reduce-scatter.2.cloned.1.call-start
  7.9 0.0 copy-start.40
  7.9 1.3 fusion.66
  9.3 1.7 collective-permute-start
  11.0 1.3 collective-permute-start.1
  12.3 0.3 slice_reduce_fusion.31
  12.7 0.2 slice_reduce_fusion.30
  12.9 0.0 collective-permute-done
  13.0 8.2 %collective-permute-done.1 = bf16[16,1536]{1,0:T(8,128)(2,1)S(1)} collective-permute-done((bf16[16,1536]{1,0:T(8,128)(2,1)S(1)}, bf16[16,1536]{1,0:T(8,128)(2,1)S(1)}, u32[]{:S(2)}, u32[]{:S(2)}) %collective-permute-start.1) | collective-permute-done | bytes 49184 | tf_op jit(solution)/shard_map/ppermute | solution.py:17
  21.1 0.2 maximum_convert_fusion
  21.3 8.3 %fusion.78 = (f32[256]{0:T(256)S(1)}, f32[256,1536]{1,0:T(8,128)S(1)}) fusion(f32[288,1536]{1,0:T(8,128)S(1)} %maximum_convert_fusion, f32[1536]{0:T(1024)S(1)} %get-tuple-element.69, f32[1536]{0:T(1024)S(1)} %get-tuple-element.70, f32[1536]{0:T(1024)S(1)} %get-tuple-element.40, f32[1536]{0:T(1024)S(1)} %get-tuple-element.41, ...), kind=kLoop, calls=%fused_computation.195 | loop fusion | flops 25165568 | bytes 52102144 | tf_op jit(solution)/shard_map/reduce_sum | solution.py:35
  29.7 0.0 copy-start.2
  29.7 0.0 copy-start.16
  29.7 0.0 copy-start.36
  29.7 0.3 multiply_reduce_fusion.2
  30.0 0.2 copy-done.36
  30.3 0.6 copy-done.38
  30.8 5.4 %fusion.68 = f32[1536,1536]{1,0:T(8,128)} fusion(f32[256,1536]{1,0:T(8,128)S(1)} %get-tuple-element.75, f32[1536]{0:T(1024)S(1)} %copy-done.16, f32[256]{0:T(256)S(1)} %add_rsqrt_fusion, f32[256]{0:T(256)S(1)} %broadcast_multiply_fusion.2, bf16[1,256,1536]{2,1,0:T(8,128)(2,1)S(1)} %copy-done.2, f32[256]{0:T(256)S(1)} %compare_convert_fusion), kind=kOutput, calls=%fused_computation.146 | convolution fusion | flops 1212284928 | bytes 11805696 | tf_op jit(solution)/shard_map/dot_general | solution.py:45
  36.3 0.0 reduce-scatter.2.cloned.1.call-update
  36.3 0.0 all-reduce.6.cloned.1.call-start
  36.4 0.0 copy-start.17
  36.4 0.0 copy-start.39
  36.4 5.2 multiply_reduce_fusion
  41.6 0.0 copy-done.37
  41.6 0.0 copy-done.39
  41.6 5.5 %fusion.31 = (f32[1536]{0:T(1024)}, f32[1536]{0:T(1024)}, f32[1536]{0:T(1024)}, f32[1536]{0:T(1024)}, f32[1536]{0:T(1024)}, /*index=5*/f32[1536]{0:T(1024)}, f32...) fusion(f32[288,1536]{1,0:T(8,128)S(1)} %maximum_convert_fusion,, ...), kind=kLoop, calls=%fused_computation.64 | loop fusion | flops 17667072 | bytes 32364544 | tf_op jit(solution)/shard_map/reduce_sum | solution.py:63
  47.1 0.9 copy-done
  48.0 8.6 %collective-permute-start.2 = (bf16[16,1536]{1,0:T(8,128)(2,1)S(1)}, bf16[16,1536]{1,0:T(8,128)(2,1)S(1)}, u32[]{:S(2)}, u32[]{:S(2)}) collective-permute-start(bf16[16,1536]{1,0:T(8,128)(2,1)S(1)} %get-tuple-element.76), channel_id=1, source_target_pairs={{0,1},{1,2},{2,3},{3,4},{4,5},{5,6},{6,7},{7,8},{8,9},{9,10},{10,1... | collective-permute-start | bytes 147464 | tf_op jit(solution)/shard_map/ppermute | solution.py:14
  56.6 1.3 collective-permute-start.3
  57.9 50.4 %psum.38 = f32[1536]{0:T(1024)S(1)} all-reduce(f32[1536]{0:T(1024)} %get-tuple-element.4), channel_id=1, replica_groups=mesh['dp'=16,'seq'=16] {'seq'}, use_global_device_ids=true, to_apply=%region_41.0 | all-reduce | flops 1536 | bytes 12288 | tf_op jit(solution)/shard_map/psum | solution.py:75
  108.3 0.0 copy-start.35
  108.3 0.0 copy-start.34
  108.4 0.0 copy-start.33
  108.4 0.0 copy-start.32
  108.4 0.0 copy-start.31
  108.4 0.0 copy-start.30
  108.4 0.0 copy-start.29
  108.4 0.0 copy-start.28
  108.4 0.0 copy-start.27
  108.4 0.0 copy-start.26
  108.4 0.0 copy-start.25
  108.4 0.0 copy-start.24
  108.5 0.0 copy-start.23
  108.5 4.0 fusion.30
  112.5 0.0 copy-start.1
  112.5 0.1 dynamic-slice_multiply_fusion.3
  113.2 2.8 stack.131
  116.0 0.0 all-reduce.6.cloned.1.call-update
  116.0 0.2 all-reduce.4.cloned.1.call-start
  116.2 0.0 collective-permute-done.2
  116.3 0.0 collective-permute-done.3
  116.3 0.2 maximum_convert_fusion.1
  116.5 0.0 copy-start.41
  116.6 73.7 %reduce-scatter.2.cloned.1.call-done = f32[96,1536]{1,0:T(8,128)} async-done(((f32[1536,1536]{1,0:T(8,128)}), f32[96,1536]{1,0:T(8,128)}) %reduce-scatter.2.cloned.1.call-update) | async-done | bytes 589840 | tf_op jit(solution)/shard_map/reduce_scatter | solution.py:74
  190.3 2.1 mul.850
  192.4 0.0 all-reduce.4.cloned.1.call-update
  192.5 7.1 %fusion.74 = bf16[1,256,1536]{2,1,0:T(8,128)(2,1)} fusion(f32[256]{0:T(256)S(1)} %copy-done.41, f32[288,1536]{1,0:T(8,128)S(1)} %maximum_convert_fusion.1, f32[1536]{0:T(1024)S(1)} %copy-done.13, f32[1536]{0:T(1024)S(1)} %copy-done.15, f32[1536]{0:T(1024)S(1)} %get-tuple-element.40, f32[1536]{0:T(1024)S(1)} %get-tuple-element.41, ...), kind=kLoop, calls=%fused_computation.151 | loop fusion | flops 25559040 | bytes 51315712 | tf_op jit(solution)/shard_map/broadcast_in_dim | solution.py:71
  199.6 159.8 %all-reduce.6.cloned.1.call-done = f32[32,1536]{1,0:T(8,128)} async-done(((f32[32,1536]{1,0:T(8,128)}), f32[32,1536]{1,0:T(8,128)}) %all-reduce.6.cloned.1.call-update) | async-done | bytes 196624 | tf_op jit(solution)/shard_map/psum | solution.py:75
  359.4 0.8 dynamic-slice_multiply_fusion.1
  360.2 72.1 %all-reduce = (f32[32,96]{1,0:T(8,128)S(1)}, f32[96]{0:T(128)S(1)}) all-reduce(f32[32,96]{1,0:T(8,128)S(1)} %dynamic-slice_multiply_fusion.1, f32[96]{0:T(128)S(1)} %dynamic-slice_multiply_fusion.3), channel_id=1, replica_groups=mesh['dp'=16,'seq'=16] {'dp'}, use_global_device_ids=true, to_apply=%region_39.0 | all-reduce | flops 3168 | bytes 25344 | tf_op jit(solution)/shard_map/psum | solution.py:81
  432.3 0.6 dynamic-slice_multiply_fusion.2
  432.9 0.5 broadcast_multiply_fusion.3
  433.4 82.8 %all-reduce.4.cloned.1.call-done = f32[96,1536]{1,0:T(8,128)} async-done(((f32[96,1536]{1,0:T(8,128)}), f32[96,1536]{1,0:T(8,128)}) %all-reduce.4.cloned.1.call-update) | async-done | bytes 589840 | tf_op jit(solution)/shard_map/psum | solution.py:81
  516.2 1.6 dynamic-slice_multiply_fusion
  (96 shorter events, 0.4 us)
Async XLA Ops:
  7.2 5.2 copy-start.3
  7.2 183.1 %reduce-scatter.2.cloned.1.call-start = ((), (), s32[]{:S(2)}) async-start(), calls=%async_computation.1 | async-start | bytes 10027008 | tf_op jit(solution)/shard_map/reduce_scatter | solution.py:74
  7.9 22.1 %copy-start.40 = (f32[256]{0:T(256)}, f32[256]{0:T(256)S(1)}, u32[]{:S(2)}) copy-start(f32[256]{0:T(256)S(1)} %compare_convert_fusion) | copy-start | bytes 3076
  9.3 3.7 collective-permute-start
  11.0 10.1 %collective-permute-start.1 = (bf16[16,1536]{1,0:T(8,128)(2,1)S(1)}, bf16[16,1536]{1,0:T(8,128)(2,1)S(1)}, u32[]{:S(2)}, u32[]{:S(2)}) collective-permute-start(bf16[16,1536]{1,0:T(8,128)(2,1)S(1)} %get-tuple-element.79), channel_id=1, source_target_pairs={{1,0},{2,1},{3,2},{4,3},{5,4},{6,5},{7,6},{8,7},{9,8},{10,9},{11,1... | collective-permute-start | bytes 147464 | tf_op jit(solution)/shard_map/ppermute | solution.py:17
  12.9 16.7 %copy-start.4 = (f32[1536]{0:T(1024)}, f32[1536]{0:T(1024)S(1)}, u32[]{:S(2)}) copy-start(f32[1536]{0:T(1024)S(1)} %get-tuple-element.65) | copy-start | bytes 18436
  12.9 16.7 %copy-start.6 = (f32[1536]{0:T(1024)}, f32[1536]{0:T(1024)S(1)}, u32[]{:S(2)}) copy-start(f32[1536]{0:T(1024)S(1)} %get-tuple-element.66) | copy-start | bytes 18436
  12.9 16.7 %copy-start.8 = (f32[1536]{0:T(1024)}, f32[1536]{0:T(1024)S(1)}, u32[]{:S(2)}) copy-start(f32[1536]{0:T(1024)S(1)} %get-tuple-element.67) | copy-start | bytes 18436
  12.9 16.7 %copy-start.10 = (f32[1536]{0:T(1024)}, f32[1536]{0:T(1024)S(1)}, u32[]{:S(2)}) copy-start(f32[1536]{0:T(1024)S(1)} %get-tuple-element.68) | copy-start | bytes 18436
  12.9 16.7 %copy-start.12 = (f32[1536]{0:T(1024)}, f32[1536]{0:T(1024)S(1)}, u32[]{:S(2)}) copy-start(f32[1536]{0:T(1024)S(1)} %get-tuple-element.69) | copy-start | bytes 18436
  12.9 16.7 %copy-start.14 = (f32[1536]{0:T(1024)}, f32[1536]{0:T(1024)S(1)}, u32[]{:S(2)}) copy-start(f32[1536]{0:T(1024)S(1)} %get-tuple-element.70) | copy-start | bytes 18436
  29.7 1.2 copy-start.2
  29.7 1.2 copy-start.16
  29.7 0.6 copy-start.36
  30.3 0.6 copy-start.38
  36.3 323.1 %all-reduce.6.cloned.1.call-start = ((), (), s32[]{:S(2)}) async-start(), calls=%async_computation.3 | async-start | bytes 393216 | tf_op jit(solution)/shard_map/psum | solution.py:75
  36.4 5.3 %copy-start.17 = (f32[1536]{0:T(1024)S(1)}, f32[1536]{0:T(1024)}, u32[]{:S(2)}) copy-start(f32[1536]{0:T(1024)} %param.11) | copy-start | bytes 18436
  36.4 5.3 %copy-start.37 = (f32[256]{0:T(256)S(1)}, f32[256]{0:T(256)}, u32[]{:S(2)}) copy-start(f32[256]{0:T(256)} %copy-done.36) | copy-start | bytes 3076
  36.4 5.3 %copy-start.39 = (f32[256]{0:T(256)S(1)}, f32[256]{0:T(256)}, u32[]{:S(2)}) copy-start(f32[256]{0:T(256)} %copy-done.38) | copy-start | bytes 3076
  47.1 0.9 copy-start
  48.0 68.2 %collective-permute-start.2 = (bf16[16,1536]{1,0:T(8,128)(2,1)S(1)}, bf16[16,1536]{1,0:T(8,128)(2,1)S(1)}, u32[]{:S(2)}, u32[]{:S(2)}) collective-permute-start(bf16[16,1536]{1,0:T(8,128)(2,1)S(1)} %get-tuple-element.76), channel_id=1, source_target_pairs={{0,1},{1,2},{2,3},{3,4},{4,5},{5,6},{6,7},{7,8},{8,9},{9,10},{10,1... | collective-permute-start | bytes 147464 | tf_op jit(solution)/shard_map/ppermute | solution.py:14
  56.6 59.7 %collective-permute-start.3 = (bf16[16,1536]{1,0:T(8,128)(2,1)S(1)}, bf16[16,1536]{1,0:T(8,128)(2,1)S(1)}, u32[]{:S(2)}, u32[]{:S(2)}) collective-permute-start(bf16[16,1536]{1,0:T(8,128)(2,1)S(1)} %get-tuple-element.77), channel_id=1, source_target_pairs={{1,0},{2,1},{3,2},{4,3},{5,4},{6,5},{7,6},{8,7},{9,8},{10,9},{11,1... | collective-permute-start | bytes 147464 | tf_op jit(solution)/shard_map/ppermute | solution.py:17
  108.3 4.3 copy-start.35
  108.3 4.3 copy-start.34
  108.4 4.3 copy-start.33
  108.4 4.3 copy-start.32
  108.4 4.3 copy-start.31
  108.4 4.3 copy-start.30
  108.4 4.3 copy-start.29
  108.4 4.4 copy-start.28
  108.4 4.4 copy-start.27
  108.4 4.4 copy-start.26
  108.4 4.4 copy-start.25
  108.4 4.4 copy-start.24
  108.5 4.4 copy-start.23
  108.5 4.4 copy-start.22
  108.5 4.5 copy-start.21
  108.5 4.5 copy-start.20
  108.5 4.5 copy-start.19
  108.5 4.5 copy-start.18
  112.5 3.8 copy-start.1
  116.0 400.2 %all-reduce.4.cloned.1.call-start = ((), (), s32[]{:S(2)}) async-start(), calls=%async_computation.2 | async-start | bytes 1179648 | tf_op jit(solution)/shard_map/psum | solution.py:81
  116.5 75.9 %copy-start.5 = (f32[1536]{0:T(1024)S(1)}, f32[1536]{0:T(1024)}, u32[]{:S(2)}) copy-start(f32[1536]{0:T(1024)} %copy-done.4) | copy-start | bytes 18436
  116.5 75.9 %copy-start.7 = (f32[1536]{0:T(1024)S(1)}, f32[1536]{0:T(1024)}, u32[]{:S(2)}) copy-start(f32[1536]{0:T(1024)} %copy-done.6) | copy-start | bytes 18436
  116.5 75.9 %copy-start.9 = (f32[1536]{0:T(1024)S(1)}, f32[1536]{0:T(1024)}, u32[]{:S(2)}) copy-start(f32[1536]{0:T(1024)} %copy-done.8) | copy-start | bytes 18436
  116.5 75.9 %copy-start.11 = (f32[1536]{0:T(1024)S(1)}, f32[1536]{0:T(1024)}, u32[]{:S(2)}) copy-start(f32[1536]{0:T(1024)} %copy-done.10) | copy-start | bytes 18436
  116.5 75.9 %copy-start.13 = (f32[1536]{0:T(1024)S(1)}, f32[1536]{0:T(1024)}, u32[]{:S(2)}) copy-start(f32[1536]{0:T(1024)} %copy-done.12) | copy-start | bytes 18436
  116.5 75.9 %copy-start.15 = (f32[1536]{0:T(1024)S(1)}, f32[1536]{0:T(1024)}, u32[]{:S(2)}) copy-start(f32[1536]{0:T(1024)} %copy-done.14) | copy-start | bytes 18436
  116.5 75.9 %copy-start.41 = (f32[256]{0:T(256)S(1)}, f32[256]{0:T(256)}, u32[]{:S(2)}) copy-start(f32[256]{0:T(256)} %copy-done.40) | copy-start | bytes 3076
Sparse Core Ops, SparseCore 0:
  36.4 153.8 reduce-scatter.1
  192.9 166.4 all-reduce.5
  362.2 153.9 all-reduce.3
where the time goes:
time: 532 us; the launch traced here: 524 us
  waiting for transfers between devices  325 us (61%)
  blocking collectives  123 us (23%)
  other arithmetic  32.5 us (6%)
  between operations  15.4 us (3%)
  starting transfers between devices  13.2 us (2%)
  matrix products  10.7 us (2%)
  local copies, waits for them, and re-layouts  5.37 us (1%)
    psum x1, waiting for transfers between devices, on_device(): kernel_total, gain_total = lax.psum((kernel_grad, gain_gradient), 'seq')  160 us
    psum x1, waiting for transfers between devices, on_device(): out_whole, kernel_whole = lax.psum((out_square, kernel_square), 'dp')  82.8 us
    reduce_scatter x1, waiting for transfers between devices, on_device(): lax.psum_scatter(out_grad, 'seq', scatter_dimension=0, tiled=True)  73.7 us
    psum x1, blocking collectives, on_device(): out_whole, kernel_whole = lax.psum((out_square, kernel_square), 'dp')  72.1 us
    psum x1, blocking collectives, on_device(): kernel_total, gain_total = lax.psum((kernel_grad, gain_gradient), 'seq')  50.4 us
  transfers between devices with their start and end apart: 7, of which 4 were waited for; matrix products, arithmetic and copies ran while one was open for 6% of the time, Pallas kernels for 0%

commit v1 on v0

v1 whole, which is shorter than its diff:
```python
import jax
import jax.numpy as jnp
from jax import lax
from jax.sharding import PartitionSpec as P

KW = 32
HALF = KW // 2
SEQ = [(y, z, c) for y in range(4) for z in range(2) for c in range(2)]
DP = [(x, z) for x in range(4) for z in range(4)]


def seq_at(y, z, c):
    return ((y % 4) * 2 + z % 2) * 2 + c % 2


def move_y(value, step):
    return lax.ppermute(value, "seq", [(seq_at(*p), seq_at(p[0] + step, p[1], p[2])) for p in SEQ])


def move_z_hi(value):
    return lax.ppermute(value, "seq", [(seq_at(*p), seq_at(p[0], p[1] + 1, p[2])) for p in SEQ])


def move_core(value):
    return lax.ppermute(value, "seq", [(seq_at(*p), seq_at(p[0], p[1], p[2] + 1)) for p in SEQ])


def move_x(value, step):
    return lax.ppermute(
        value, "dp", [(x * 4 + z, ((x + step) % 4) * 4 + z) for x, z in DP]
    )


def move_z_lo(value, step):
    return lax.ppermute(value, "dp", [(x * 4 + z, x * 4 + (z + step) % 4) for x, z in DP])


def halo(block):
    forward = [(i, i + 1) for i in range(15)]
    backward = [(i + 1, i) for i in range(15)]
    low = lax.ppermute(block[-HALF:], "seq", forward)
    high = lax.ppermute(block[:HALF], "seq", backward)
    return jnp.concatenate([low, block, high], axis=0)


def part(value, index, size, axis):
    return lax.dynamic_slice_in_dim(value, index * size, size, axis)


def reduce_out(hidden, cot_pair):
    bf16, f32 = jnp.bfloat16, jnp.float32
    seq = lax.axis_index("seq")
    y, z_hi, core = seq // 4, (seq // 2) % 2, seq % 2
    hidden_pair = jnp.concatenate([hidden, move_core(hidden)], axis=0)

    def chunk(step):
        rows = part(hidden_pair, (y + step) % 4, 384, 1)
        return lax.dot_general(
            rows, cot_pair, (((0,), (0,)), ((), ())), preferred_element_type=f32
        )

    far = chunk(2).astype(bf16)
    up_a = move_y(far[:, :384], 1)
    down_b = move_y(far[:, 384:], -1)
    above = chunk(1)
    below = chunk(3)
    up_b = move_y(above[:, 384:].astype(bf16), 1)
    down_a = move_y(below[:, :384].astype(bf16), -1)
    own = chunk(0)
    up_a = move_y((above[:, :384] + up_a.astype(f32)).astype(bf16), 1)
    down_b = move_y((below[:, 384:] + down_b.astype(f32)).astype(bf16), -1)
    low = own[:, :384] + down_a.astype(f32) + up_a.astype(f32)
    high = own[:, 384:] + up_b.astype(f32) + down_b.astype(f32)
    total = jnp.concatenate([low, high], axis=1)
    other = move_z_hi(part(total, 1 - z_hi, 192, 0).astype(bf16))
    total = part(total, z_hi, 192, 0) + other.astype(f32)
    square = total * total
    mine = part(square, core, 96, 0)
    other = move_core(part(square, 1 - core, 96, 0).astype(bf16)).astype(f32)
    square = jnp.concatenate(
        [jnp.where(core == 0, mine, other), jnp.where(core == 0, other, mine)], axis=1
    )
    dp = lax.axis_index("dp")
    x, z_lo = dp // 4, dp % 4
    received = [move_x(part(square, (x + k) % 4, 384, 1).astype(bf16), k) for k in (1, 2, 3)]
    square = part(square, x, 384, 1)
    for value in received:
        square = square + value.astype(f32)
    received = [move_z_lo(part(square, (z_lo + k) % 4, 96, 1).astype(bf16), k) for k in (1, 2, 3)]
    square = part(square, z_lo, 96, 1)
    for value in received:
        square = square + value.astype(f32)
    return square


def reduce_rows(kernel_grad, gain_gradient):
    rows = jnp.concatenate([kernel_grad, gain_gradient[None]], axis=0)
    rows = rows.reshape(KW + 1, 16, 96).transpose(1, 0, 2).reshape(16, (KW + 1) * 96)
    rows = lax.all_to_all(rows, "seq", 0, 0, tiled=True).sum(axis=0)
    square = (rows * rows).reshape(KW + 1, 96)
    kernel = square[:KW].reshape(16, 2 * 96)
    gain = jnp.broadcast_to(square[KW][None], (16, 96))
    rows = jnp.concatenate([kernel, gain], axis=1)
    rows = lax.all_to_all(rows, "dp", 0, 0, tiled=True).sum(axis=0)
    return rows[: 2 * 96].reshape(2, 96), rows[2 * 96 :]


def on_device(frames_in, cotangent, lengths, out_weight, conv_kernel, layer_norm_gain):
    bf16, f32 = jnp.bfloat16, jnp.float32
    frame_count = frames_in.shape[1]
    width = out_weight.shape[0]
    seq = lax.axis_index("seq")
    core = seq % 2
    position = seq * frame_count + jnp.arange(frame_count, dtype=jnp.int32)
    valid = (position < lengths[0])[:, None]
    masked = jnp.where(valid, frames_in[0], jnp.zeros((), bf16))
    padded_wide = halo(masked).astype(f32)
    grad_out = jnp.where(valid, cotangent[0], jnp.zeros((), bf16))
    cot_pair = jnp.concatenate(
        [part(grad_out, core, 768, 1), move_core(part(grad_out, 1 - core, 768, 1))], axis=0
    )
    conv_out = jnp.zeros((frame_count, width), f32)
    for offset in range(KW):
        conv_out = conv_out + conv_kernel[offset] * padded_wide[offset : offset + frame_count]
    row_mean = jnp.mean(conv_out, axis=1, keepdims=True)
    centered = conv_out - row_mean
    inverse_deviation = lax.rsqrt(jnp.mean(centered * centered, axis=1, keepdims=True) + 1e-05)
    standardized = centered * inverse_deviation
    normalized = standardized * layer_norm_gain
    sigma = jax.nn.sigmoid(normalized)
    hidden = (normalized * sigma).astype(bf16)
    fisher_out = reduce_out(hidden, cot_pair)
    hidden_grad = lax.dot_general(
        grad_out, out_weight, (((1,), (1,)), ((), ())), preferred_element_type=f32
    )
    normalized_grad = hidden_grad * (sigma + normalized * sigma * (1.0 - sigma))
    gain_gradient = jnp.sum(normalized_grad * standardized, axis=0)
    scaled = normalized_grad * layer_norm_gain
    conv_grad = inverse_deviation * (
        scaled
        - jnp.mean(scaled, axis=1, keepdims=True)
        - standardized * jnp.mean(scaled * standardized, axis=1, keepdims=True)
    )
    conv_grad = conv_grad.astype(bf16)
    conv_wide = conv_grad.astype(f32)
    kernel_grad = jnp.stack(
        [
            jnp.sum(conv_wide * padded_wide[offset : offset + frame_count], axis=0)
            for offset in range(KW)
        ]
    )
    fisher_kernel, fisher_gain = reduce_rows(kernel_grad, gain_gradient)
    grad_padded = halo(conv_grad).astype(f32)
    summed = jnp.zeros((frame_count, width), f32)
    for offset in range(KW):
        begin = KW - offset
        summed = summed + conv_kernel[offset] * grad_padded[begin : begin + frame_count]
    input_grad = jnp.where(valid, summed, 0.0).astype(bf16)[None]
    return input_grad, fisher_out / 16, fisher_kernel / 16, fisher_gain / 16


def solution(mesh):
    return jax.shard_map(
        on_device,
        mesh=mesh,
        in_specs=(P("dp", "seq", None), P("dp", "seq", None), P("dp"), P(), P(), P()),
        out_specs=(P("dp", "seq", None), P("seq", "dp"), P("dp", "seq"), P("seq")),
        check_vma=False,
    )
```

time: 532 us -> 151 us (0.28); the launches traced: 524 us -> 150 us
  waiting for transfers between devices: 325 us -> 15.7 us
  blocking collectives: 123 us -> 0 us
  starting transfers between devices: 13.2 us -> 60.3 us
  local copies, waits for them, and re-layouts: 5.37 us -> 31.3 us
  between operations: 15.4 us -> 2.84 us
  matrix products: 10.7 us -> 4.55 us
    psum x2 -> x0, waiting for transfers between devices: 243 us -> none  [the longest x1 160 us: on_device(): kernel_total, gain_total = lax.psum((kernel_grad, gain_gradient), 'seq')]
    psum x2 -> x0, blocking collectives: 123 us -> none  [the longest x1 72.1 us: on_device(): out_whole, kernel_whole = lax.psum((out_square, kernel_square), 'dp')]
    reduce_scatter x1 -> x0, waiting for transfers between devices: 73.7 us -> none  [on_device(): lax.psum_scatter(out_grad, 'seq', scatter_dimension=0, tiled=True)]
    ppermute x4 -> x20, starting transfers between devices: 12.9 us -> 49.8 us  [the longest x3 14.3 us: move_core(): lax.ppermute(value, 'seq', [(seq_at(*p), seq_at(p[0], p[1], p[2] + 1)) fo...]
    concatenate x0 -> x35, local copies, waits for them, and re-layouts: none -> 25.5 us  [the longest x34 25.4 us: reduce_rows(): rows = jnp.concatenate([kernel_grad, gain_gradient[None]], axis=0)]
    all_to_all x0 -> x2, starting transfers between devices: none -> 10.5 us  [the longest x1 6.37 us: reduce_rows(): rows = lax.all_to_all(rows, 'dp', 0, 0, tiled=True).sum(axis=0)]
    ppermute x4 -> x20, waiting for transfers between devices: 8.19 us -> 15.7 us  [the longest x3 5.56 us: move_x(): lax.ppermute(value, 'dp', [(x * 4 + z, (x + step) % 4 * 4 + z) for x, z i...]
  transfers between devices with their start and end apart: 7 -> 22, of which waited for: 4 -> 8; matrix products, arithmetic and copies ran while one was open for 6% -> 44% of each run, Pallas kernels for 0% -> 0%
where the time goes in v1:
time: 151 us; the launch traced here: 150 us
  starting transfers between devices  60.3 us (40%)
  other arithmetic  35 us (23%)
  local copies, waits for them, and re-layouts  31.3 us (21%)
  waiting for transfers between devices  15.7 us (10%)
  matrix products  4.55 us (3%)
  between operations  2.84 us (2%)
    concatenate x34, local copies, waits for them, and re-layouts, reduce_rows(): rows = jnp.concatenate([kernel_grad, gain_gradient[None]], axis=0)  25.4 us
    ppermute x3, starting transfers between devices, move_core(): lax.ppermute(value, 'seq', [(seq_at(*p), seq_at(p[0], p[1], p[2] + 1)) fo...  14.3 us
    ppermute x1, starting transfers between devices, move_z_hi(): lax.ppermute(value, 'seq', [(seq_at(*p), seq_at(p[0], p[1] + 1, p[2])) fo...  11.7 us
    ppermute x6, starting transfers between devices, move_y(): lax.ppermute(value, 'seq', [(seq_at(*p), seq_at(p[0] + step, p[1], p[2]))...  10.3 us
    reduce_sum x2, other arithmetic, on_device(): jnp.sum(conv_wide * padded_wide[offset:offset + frame_count], axis=0)  8.5 us
    broadcast_in_dim x1, other arithmetic, on_device(): input_grad = jnp.where(valid, summed, 0.0).astype(bf16)[None]  8.49 us
    reduce_sum x1, other arithmetic, on_device(): row_mean = jnp.mean(conv_out, axis=1, keepdims=True)  8.27 us
    all_to_all x1, starting transfers between devices, reduce_rows(): rows = lax.all_to_all(rows, 'dp', 0, 0, tiled=True).sum(axis=0)  6.37 us
  transfers between devices with their start and end apart: 22, of which 8 were waited for; matrix products, arithmetic and copies ran while one was open for 44% of the time, Pallas kernels for 0%

profile of v1, /device:TPU:6, one launch (start us, length us, event | category | flops | bytes accessed | tf_op | source)
XLA Modules:
  0.0 149.8 jit_solution(1114549493172087570)
XLA Ops:
  1.3 1.5 %bitcast_select_fusion = (bf16[256,1536]{1,0:T(8,128)(2,1)S(1)}, bf16[256,1536]{1,0:T(8,128)(2,1)S(1)}) fusion(bf16[1,256,1536]{2,1,0:T(8,128)(2,1)} %param.7, pred[256]{0:T(512)(128)(4,1)S(1)} %add_compare_fusion, bf16[1,256,1536]{2,1,0:T(8,128)(2,1)} %param.6), kind=kLoop, calls=%fused_computation.164 | loop fusion | flops 786432 | bytes 3145984 | tf_op jit(solution)/shard_map/jit(_where)/select_n | solution.py:118
  2.9 1.9 %collective-permute-start = (bf16[16,1536]{1,0:T(8,128)(2,1)S(1)}, bf16[16,1536]{1,0:T(8,128)(2,1)S(1)}, u32[]{:S(2)}, u32[]{:S(2)}) collective-permute-start(bf16[16,1536]{1,0:T(8,128)(2,1)S(1)} %get-tuple-element.81), channel_id=1, source_target_pairs={{0,1},{1,2},{2,3},{3,4},{4,5},{5,6},{6,7},{7,8},{8,9},{9,10},{10,1... | collective-permute-start | bytes 147464 | tf_op jit(solution)/shard_map/ppermute | solution.py:41
  4.8 1.3 collective-permute-start.1
  6.2 8.2 %collective-permute-start.5 = (bf16[256,768]{1,0:T(8,128)(2,1)S(1)}, bf16[256,768]{1,0:T(8,128)(2,1)S(1)}, u32[]{:S(2)}, u32[]{:S(2)}) collective-permute-start(bf16[256,768]{1,0:T(8,128)(2,1)S(1)} %get-tuple-element.78), channel_id=1, source_target_pairs={{0,1},{1,0},{2,3},{3,2},{4,5},{5,4},{6,7},{7,6},{8,9},{9,8},{10,11... | collective-permute-start | bytes 1179656 | tf_op jit(solution)/shard_map/ppermute | solution.py:25
  16.0 8.3 %fusion.105 = (f32[256]{0:T(256)S(1)}, f32[256,1536]{1,0:T(8,128)S(1)}) fusion(f32[288,1536]{1,0:T(8,128)S(1)} %maximum_convert_fusion, f32[1536]{0:T(1024)S(1)} %get-tuple-element.69, f32[1536]{0:T(1024)S(1)} %get-tuple-element.70, f32[1536]{0:T(1024)S(1)} %get-tuple-element.40, f32[1536]{0:T(1024)S(1)} %get-tuple-element.41, ...), kind=kLoop, calls=%fused_computation.256 | loop fusion | flops 25165568 | bytes 52102144 | tf_op jit(solution)/shard_map/reduce_sum | solution.py:125
  25.0 2.5 %multiply_reduce_fusion = (f32[1536]{0:T(1024)}, f32[256]{0:T(256)S(1)}, f32[256]{0:T(256)S(1)}, bf16[256,1536]{1,0:T(8,128)(2,1)S(1)}, f32[256,1536]{1,0:T(8,128)S(1)}) fusion(f32[256,1536]{1,0:T(8,128)S(1)} %get-tuple-element.73, f32[256]{0:T(256)S(1)} %add_rsqrt_fusion, f32[256]{0:T(256)S(1)} %broadcast_multiply_fusion.2, f32[1536]{0:T(1024)S(1)} %copy-done.62, ...), kind=kOutput, calls=%fused_computation.138 | convolution fusion | flops 1215035392 | bytes 9453568 | tf_op jit(solution)/shard_map/dot_general | solution.py:133
  27.6 6.0 %collective-permute-start.4 = (bf16[256,1536]{1,0:T(8,128)(2,1)S(1)}, bf16[256,1536]{1,0:T(8,128)(2,1)S(1)}, u32[]{:S(2)}, u32[]{:S(2)}) collective-permute-start(bf16[256,1536]{1,0:T(8,128)(2,1)S(1)} %get-tuple-element.74), channel_id=1, source_target_pairs={{0,1},{1,0},{2,3},{3,2},{4,5},{5,4},{6,7},{7,6},{8,9},{9,8},{10,11... | collective-permute-start | bytes 2359304 | tf_op jit(solution)/shard_map/ppermute | solution.py:25
  33.6 5.6 %fusion.31 = (f32[1536]{0:T(1024)}, f32[1536]{0:T(1024)}, f32[1536]{0:T(1024)}, f32[1536]{0:T(1024)}, f32[1536]{0:T(1024)}, /*index=5*/f32[1536]{0:T(1024)}, f32...) fusion(f32[288,1536]{1,0:T(8,128)S(1)} %maximum_convert_fusion,, ...), kind=kLoop, calls=%fused_computation.72 | loop fusion | flops 17667072 | bytes 32364544 | tf_op jit(solution)/shard_map/reduce_sum | solution.py:148
  39.8 2.2 %collective-permute-start.7 = (bf16[384,384]{1,0:T(8,128)(2,1)S(1)}, bf16[384,384]{1,0:T(8,128)(2,1)S(1)}, u32[]{:S(2)}, u32[]{:S(2)}) collective-permute-start(bf16[384,384]{1,0:T(8,128)(2,1)S(1)} %get-tuple-element.89), channel_id=1, source_target_pairs={{0,4},{1,5},{2,6},{3,7},{4,8},{5,9},{6,10},{7,11},{8,12},{9,13},{1... | collective-permute-start | bytes 884744 | tf_op jit(solution)/shard_map/ppermute | solution.py:17
  42.0 2.9 %fusion.30 = (f32[1536]{0:T(1024)S(1)}, f32[1536]{0:T(1024)S(1)}, f32[1536]{0:T(1024)S(1)}, f32[1536]{0:T(1024)S(1)}, f32[1536]{0:T(1024)S(1)}, /*index=5*/f32[1...) fusion(bf16[256,1536]{1,0:T(8,128)(2,1)S(1)} %get-tuple-element, ...), kind=kLoop, calls=%fused_computation.71 | loop fusion | flops 11381760 | bytes 22892544 | tf_op jit(solution)/shard_map/reduce_sum | solution.py:148
  45.4 0.7 slice.938
  46.1 1.6 %collective-permute-start.9 = (bf16[384,384]{1,0:T(8,128)(2,1)}, bf16[384,384]{1,0:T(8,128)(2,1)}, u32[]{:S(2)}, u32[]{:S(2)}) collective-permute-start(bf16[384,384]{1,0:T(8,128)(2,1)} %slice.938), channel_id=1, source_target_pairs={{0,4},{1,5},{2,6},{3,7},{4,8},{5,9},{6,10},{7,11},{8,12},{9,13},{1... | collective-permute-start | bytes 884744 | tf_op jit(solution)/shard_map/ppermute | solution.py:17
  47.7 1.7 %collective-permute-start.10 = (bf16[384,384]{1,0:T(8,128)(2,1)S(1)}, bf16[384,384]{1,0:T(8,128)(2,1)S(1)}, u32[]{:S(2)}, u32[]{:S(2)}) collective-permute-start(bf16[384,384]{1,0:T(8,128)(2,1)S(1)} %get-tuple-element.88), channel_id=1, source_target_pairs={{0,12},{1,13},{2,14},{3,15},{4,0},{5,1},{6,2},{7,3},{8,4},{9,5},{1... | collective-permute-start | bytes 884744 | tf_op jit(solution)/shard_map/ppermute | solution.py:17
  49.9 0.7 slice.939
  51.2 0.8 fusion.74
  52.0 1.7 %collective-permute-start.8 = (bf16[384,384]{1,0:T(8,128)(2,1)}, bf16[384,384]{1,0:T(8,128)(2,1)}, u32[]{:S(2)}, u32[]{:S(2)}) collective-permute-start(bf16[384,384]{1,0:T(8,128)(2,1)} %fusion.74), channel_id=1, source_target_pairs={{0,4},{1,5},{2,6},{3,7},{4,8},{5,9},{6,10},{7,11},{8,12},{9,13},{1... | collective-permute-start | bytes 884744 | tf_op jit(solution)/shard_map/ppermute | solution.py:17
  53.7 4.0 %collective-permute-done.10 = bf16[384,384]{1,0:T(8,128)(2,1)S(1)} collective-permute-done((bf16[384,384]{1,0:T(8,128)(2,1)S(1)}, bf16[384,384]{1,0:T(8,128)(2,1)S(1)}, u32[]{:S(2)}, u32[]{:S(2)}) %collective-permute-start.10) | collective-permute-done | bytes 294944 | tf_op jit(solution)/shard_map/ppermute | solution.py:17
  57.6 0.8 fusion.72
  58.4 2.9 %collective-permute-start.11 = (bf16[384,384]{1,0:T(8,128)(2,1)}, bf16[384,384]{1,0:T(8,128)(2,1)}, u32[]{:S(2)}, u32[]{:S(2)}) collective-permute-start(bf16[384,384]{1,0:T(8,128)(2,1)} %fusion.72), channel_id=1, source_target_pairs={{0,12},{1,13},{2,14},{3,15},{4,0},{5,1},{6,2},{7,3},{8,4},{9,5},{1... | collective-permute-start | bytes 884744 | tf_op jit(solution)/shard_map/ppermute | solution.py:17
  61.9 0.7 concatenate.115
  63.3 0.7 concatenate.117
  64.6 0.7 concatenate.119
  65.3 0.7 concatenate.120
  66.0 0.7 concatenate.121
  66.7 0.7 concatenate.122
  67.3 0.7 concatenate.123
  68.0 0.7 concatenate.124
  68.7 0.7 concatenate.125
  69.4 0.7 concatenate.126
  70.0 0.7 concatenate.127
  71.6 0.7 concatenate.102
  72.2 0.7 concatenate.103
  72.9 0.7 concatenate.104
  73.6 0.7 concatenate.105
  75.6 0.7 concatenate.108
  76.3 0.7 concatenate.109
  77.7 0.7 concatenate.111
  79.0 0.7 concatenate.113
  79.7 0.7 concatenate.114
  80.4 0.7 concatenate.128
  81.1 0.7 concatenate.98
  81.7 0.7 concatenate.99
  82.4 0.7 concatenate.129
  83.1 4.3 %concatenate.130 = f32[33,16,96]{2,0,1:T(8,128)S(1)} concatenate(f32[1,16,96]{2,0,1:T(1,128)S(1)} %concatenate.97, f32[1,16,96]{2,0,1:T(1,128)} %concatenate.98, f32[1,16,96]{2,0,1:T(1,128)} %concatenate.99, f32[1,16,96]{2,0,1:T(1,128)S(1)} %concatenate.100, f32[1,16,96]{2,0,1:T(1,128)} %concatenate.101, f32[1,16,96]{2,0,1:T(1,128)} %concatenate.102, f32[1,16,96]{2,0,1:T(1,128)} %concatenate.103, ...), dimensions={0} | concatenate | bytes 405504 | tf_op jit(solution)/shard_map/concatenate | solution.py:97
  87.4 1.0 all_to_all.16
  88.4 4.2 %all-to-all-start = ((f32[16,1,3168]{2,1,0:T(1,128)}), f32[16,1,3168]{2,1,0:T(1,128)}, u32[]{:S(2)}, u32[]{:S(2)}) async-start(f32[16,1,3168]{2,1,0:T(1,128)} %all_to_all.16), calls=%async_computation | async-start | bytes 409600 | tf_op jit(solution)/shard_map/all_to_all | solution.py:99
  92.6 2.1 %collective-permute-start.2 = (bf16[16,1536]{1,0:T(8,128)(2,1)}, bf16[16,1536]{1,0:T(8,128)(2,1)S(1)}, u32[]{:S(2)}, u32[]{:S(2)}) collective-permute-start(bf16[16,1536]{1,0:T(8,128)(2,1)} %get-tuple-element.79), channel_id=1, source_target_pairs={{0,1},{1,2},{2,3},{3,4},{4,5},{5,6},{6,7},{7,8},{8,9},{9,10},{10,1... | collective-permute-start | bytes 147464 | tf_op jit(solution)/shard_map/ppermute | solution.py:41
  95.2 1.3 collective-permute-start.3
  96.6 1.4 fusion.73
  98.0 0.8 fusion.68
  98.8 11.7 %collective-permute-start.12 = (bf16[192,768]{1,0:T(8,128)(2,1)}, bf16[192,768]{1,0:T(8,128)(2,1)S(1)}, u32[]{:S(2)}, u32[]{:S(2)}) collective-permute-start(bf16[192,768]{1,0:T(8,128)(2,1)} %fusion.68), channel_id=1, source_target_pairs={{0,2},{1,3},{2,0},{3,1},{4,6},{5,7},{6,4},{7,5},{8,10},{9,11},{10,... | collective-permute-start | bytes 884744 | tf_op jit(solution)/shard_map/ppermute | solution.py:21
  110.9 1.1 reduce_sum.388
  112.8 6.4 %all-to-all-start.1 = ((f32[16,1,288]{2,1,0:T(1,128)}), f32[16,1,288]{2,1,0:T(1,128)S(1)}, u32[]{:S(2)}, u32[]{:S(2)}) async-start(f32[16,1,288]{2,1,0:T(1,128)} %all_to_all.14), calls=%async_computation.1 | async-start | bytes 49152 | tf_op jit(solution)/shard_map/all_to_all | solution.py:104
  119.2 4.8 %collective-permute-done.12 = bf16[192,768]{1,0:T(8,128)(2,1)S(1)} collective-permute-done((bf16[192,768]{1,0:T(8,128)(2,1)}, bf16[192,768]{1,0:T(8,128)(2,1)S(1)}, u32[]{:S(2)}, u32[]{:S(2)}) %collective-permute-start.12) | collective-permute-done | bytes 294944 | tf_op jit(solution)/shard_map/ppermute | solution.py:21
  124.0 1.0 fusion.71
  125.3 8.5 %fusion.66 = bf16[1,256,1536]{2,1,0:T(8,128)(2,1)} fusion(f32[288,1536]{1,0:T(8,128)S(1)} %maximum_convert_fusion.1, f32[1536]{0:T(1024)} %copy-done.42, f32[1536]{0:T(1024)} %copy-done.43, f32[1536]{0:T(1024)S(1)} %get-tuple-element.40, f32[1536]{0:T(1024)S(1)} %copy-done.3, f32[1536]{0:T(1024)S(1)} %copy-done.5, f32[1536]{0:T(1024)S(1)} %copy-done.7, ...), kind=kLoop, calls=%fused_computation.166 | loop fusion | flops 25559040 | bytes 51314944 | tf_op jit(solution)/shard_map/broadcast_in_dim | solution.py:158
  134.6 2.4 %collective-permute-start.15 = (bf16[96,384]{1,0:T(8,128)(2,1)S(1)}, bf16[96,384]{1,0:T(8,128)(2,1)S(1)}, u32[]{:S(2)}, u32[]{:S(2)}) collective-permute-start(bf16[96,384]{1,0:T(8,128)(2,1)S(1)} %get-tuple-element.86), channel_id=1, source_target_pairs={{0,128},{16,144},{32,160},{48,176},{64,192},{80,208},{96,224},{112... | collective-permute-start | bytes 221192 | tf_op jit(solution)/shard_map/ppermute | solution.py:29
  137.0 2.2 %collective-permute-done.14 = bf16[96,384]{1,0:T(8,128)(2,1)S(1)} collective-permute-done((bf16[96,384]{1,0:T(8,128)(2,1)S(1)}, bf16[96,384]{1,0:T(8,128)(2,1)S(1)}, u32[]{:S(2)}, u32[]{:S(2)}) %collective-permute-start.14) | collective-permute-done | bytes 73760 | tf_op jit(solution)/shard_map/ppermute | solution.py:29
  139.2 1.4 collective-permute-done.15
  140.6 2.0 %collective-permute-done.16 = bf16[96,384]{1,0:T(8,128)(2,1)S(1)} collective-permute-done((bf16[96,384]{1,0:T(8,128)(2,1)S(1)}, bf16[96,384]{1,0:T(8,128)(2,1)S(1)}, u32[]{:S(2)}, u32[]{:S(2)}) %collective-permute-start.16) | collective-permute-done | bytes 73760 | tf_op jit(solution)/shard_map/ppermute | solution.py:29
  142.8 2.5 %collective-permute-start.18 = (bf16[96,96]{1,0:T(8,128)(2,1)S(1)}, bf16[96,96]{1,0:T(8,128)(2,1)S(1)}, u32[]{:S(2)}, u32[]{:S(2)}) collective-permute-start(bf16[96,96]{1,0:T(8,128)(2,1)S(1)} %get-tuple-element.92), channel_id=1, source_target_pairs={{0,32},{16,48},{32,0},{48,16},{64,96},{80,112},{96,64},{112,80},{1... | collective-permute-start | bytes 55304 | tf_op jit(solution)/shard_map/ppermute | solution.py:35
  145.3 1.4 collective-permute-start.19
  148.4 0.7 collective-permute-done.19
  149.1 0.7 add_multiply_fusion
  (198 shorter events, 13.7 us)
Async XLA Ops:
  1.3 1.6 %copy-start.64 = (pred[256]{0:T(512)(128)(4,1)}, pred[256]{0:T(512)(128)(4,1)S(1)}, u32[]{:S(2)}) copy-start(pred[256]{0:T(512)(128)(4,1)S(1)} %add_compare_fusion) | copy-start | bytes 772
  2.9 11.5 %copy-start.1 = (f32[32,1536]{1,0:T(8,128)S(1)}, f32[32,1536]{1,0:T(8,128)}, u32[]{:S(2)}) copy-start(f32[32,1536]{1,0:T(8,128)} %param.10) | copy-start | bytes 589828
  2.9 12.6 %collective-permute-start = (bf16[16,1536]{1,0:T(8,128)(2,1)S(1)}, bf16[16,1536]{1,0:T(8,128)(2,1)S(1)}, u32[]{:S(2)}, u32[]{:S(2)}) collective-permute-start(bf16[16,1536]{1,0:T(8,128)(2,1)S(1)} %get-tuple-element.81), channel_id=1, source_target_pairs={{0,1},{1,2},{2,3},{3,4},{4,5},{5,6},{6,7},{7,8},{8,9},{9,10},{10,1... | collective-permute-start | bytes 147464 | tf_op jit(solution)/shard_map/ppermute | solution.py:41
  4.8 10.7 %collective-permute-start.1 = (bf16[16,1536]{1,0:T(8,128)(2,1)S(1)}, bf16[16,1536]{1,0:T(8,128)(2,1)S(1)}, u32[]{:S(2)}, u32[]{:S(2)}) collective-permute-start(bf16[16,1536]{1,0:T(8,128)(2,1)S(1)} %get-tuple-element.82), channel_id=1, source_target_pairs={{1,0},{2,1},{3,2},{4,3},{5,4},{6,5},{7,6},{8,7},{9,8},{10,9},{11,1... | collective-permute-start | bytes 147464 | tf_op jit(solution)/shard_map/ppermute | solution.py:42
  6.2 33.0 %collective-permute-start.5 = (bf16[256,768]{1,0:T(8,128)(2,1)S(1)}, bf16[256,768]{1,0:T(8,128)(2,1)S(1)}, u32[]{:S(2)}, u32[]{:S(2)}) collective-permute-start(bf16[256,768]{1,0:T(8,128)(2,1)S(1)} %get-tuple-element.78), channel_id=1, source_target_pairs={{0,1},{1,0},{2,3},{3,2},{4,5},{5,4},{6,7},{7,6},{8,9},{9,8},{10,11... | collective-permute-start | bytes 1179656 | tf_op jit(solution)/shard_map/ppermute | solution.py:25
  14.7 1.1 copy-start.2
  14.7 1.1 copy-start.4
  14.7 1.1 copy-start.6
  14.7 1.1 copy-start.8
  14.8 9.5 %copy-start.26 = (f32[1536]{0:T(1024)}, f32[1536]{0:T(1024)S(1)}, u32[]{:S(2)}) copy-start(f32[1536]{0:T(1024)S(1)} %get-tuple-element.53) | copy-start | bytes 18436
  14.8 9.5 %copy-start.27 = (f32[1536]{0:T(1024)}, f32[1536]{0:T(1024)S(1)}, u32[]{:S(2)}) copy-start(f32[1536]{0:T(1024)S(1)} %get-tuple-element.54) | copy-start | bytes 18436
  15.7 8.9 %slice-start = ((s8[4718592]{0:T(1024)(128)(4,1)}), s8[4194304]{0:T(1024)(128)(4,1)S(1)}, s32[]{:S(2)}) async-start(s8[4718592]{0:T(1024)(128)(4,1)} %bitcast.12), calls=%async_computation.2 | async-start | bytes 8388608
  16.0 8.6 %slice-start.1 = ((s8[4718592]{0:T(1024)(128)(4,1)}), s8[524288]{0:T(1024)(128)(4,1)S(1)}, s32[]{:S(2)}) async-start(s8[4718592]{0:T(1024)(128)(4,1)} %bitcast.12), calls=%async_computation.3 | async-start | bytes 1048576
  27.6 11.7 %collective-permute-start.4 = (bf16[256,1536]{1,0:T(8,128)(2,1)S(1)}, bf16[256,1536]{1,0:T(8,128)(2,1)S(1)}, u32[]{:S(2)}, u32[]{:S(2)}) collective-permute-start(bf16[256,1536]{1,0:T(8,128)(2,1)S(1)} %get-tuple-element.74), channel_id=1, source_target_pairs={{0,1},{1,0},{2,3},{3,2},{4,5},{5,4},{6,7},{7,6},{8,9},{9,8},{10,11... | collective-permute-start | bytes 2359304 | tf_op jit(solution)/shard_map/ppermute | solution.py:25
  39.8 11.4 %collective-permute-start.7 = (bf16[384,384]{1,0:T(8,128)(2,1)S(1)}, bf16[384,384]{1,0:T(8,128)(2,1)S(1)}, u32[]{:S(2)}, u32[]{:S(2)}) collective-permute-start(bf16[384,384]{1,0:T(8,128)(2,1)S(1)} %get-tuple-element.89), channel_id=1, source_target_pairs={{0,4},{1,5},{2,6},{3,7},{4,8},{5,9},{6,10},{7,11},{8,12},{9,13},{1... | collective-permute-start | bytes 884744 | tf_op jit(solution)/shard_map/ppermute | solution.py:17
  46.1 49.1 %collective-permute-start.9 = (bf16[384,384]{1,0:T(8,128)(2,1)}, bf16[384,384]{1,0:T(8,128)(2,1)}, u32[]{:S(2)}, u32[]{:S(2)}) collective-permute-start(bf16[384,384]{1,0:T(8,128)(2,1)} %slice.938), channel_id=1, source_target_pairs={{0,4},{1,5},{2,6},{3,7},{4,8},{5,9},{6,10},{7,11},{8,12},{9,13},{1... | collective-permute-start | bytes 884744 | tf_op jit(solution)/shard_map/ppermute | solution.py:17
  47.7 9.9 %collective-permute-start.10 = (bf16[384,384]{1,0:T(8,128)(2,1)S(1)}, bf16[384,384]{1,0:T(8,128)(2,1)S(1)}, u32[]{:S(2)}, u32[]{:S(2)}) collective-permute-start(bf16[384,384]{1,0:T(8,128)(2,1)S(1)} %get-tuple-element.88), channel_id=1, source_target_pairs={{0,12},{1,13},{2,14},{3,15},{4,0},{5,1},{6,2},{7,3},{8,4},{9,5},{1... | collective-permute-start | bytes 884744 | tf_op jit(solution)/shard_map/ppermute | solution.py:17
  49.9 20.9 %copy-start.61 = (f32[1536]{0:T(1024)S(1)}, f32[1536]{0:T(1024)}, u32[]{:S(2)}) copy-start(f32[1536]{0:T(1024)} %get-tuple-element.9) | copy-start | bytes 18436
  49.9 21.0 %copy-start.60 = (f32[1536]{0:T(1024)S(1)}, f32[1536]{0:T(1024)}, u32[]{:S(2)}) copy-start(f32[1536]{0:T(1024)} %get-tuple-element.10) | copy-start | bytes 18436
  50.6 20.9 %copy-start.59 = (f32[1536]{0:T(1024)S(1)}, f32[1536]{0:T(1024)}, u32[]{:S(2)}) copy-start(f32[1536]{0:T(1024)} %get-tuple-element.11) | copy-start | bytes 18436
  50.6 21.6 %copy-start.58 = (f32[1536]{0:T(1024)S(1)}, f32[1536]{0:T(1024)}, u32[]{:S(2)}) copy-start(f32[1536]{0:T(1024)} %get-tuple-element.12) | copy-start | bytes 18436
  50.7 22.3 %copy-start.57 = (f32[1536]{0:T(1024)S(1)}, f32[1536]{0:T(1024)}, u32[]{:S(2)}) copy-start(f32[1536]{0:T(1024)} %get-tuple-element.13) | copy-start | bytes 18436
  50.7 22.9 %copy-start.56 = (f32[1536]{0:T(1024)S(1)}, f32[1536]{0:T(1024)}, u32[]{:S(2)}) copy-start(f32[1536]{0:T(1024)} %get-tuple-element.14) | copy-start | bytes 18436
  50.7 23.6 %copy-start.55 = (f32[1536]{0:T(1024)S(1)}, f32[1536]{0:T(1024)}, u32[]{:S(2)}) copy-start(f32[1536]{0:T(1024)} %get-tuple-element.15) | copy-start | bytes 18436
  50.7 24.3 %copy-start.54 = (f32[1536]{0:T(1024)S(1)}, f32[1536]{0:T(1024)}, u32[]{:S(2)}) copy-start(f32[1536]{0:T(1024)} %get-tuple-element.16) | copy-start | bytes 18436
  50.7 25.0 %copy-start.53 = (f32[1536]{0:T(1024)S(1)}, f32[1536]{0:T(1024)}, u32[]{:S(2)}) copy-start(f32[1536]{0:T(1024)} %get-tuple-element.17) | copy-start | bytes 18436
  50.7 25.6 %copy-start.52 = (f32[1536]{0:T(1024)S(1)}, f32[1536]{0:T(1024)}, u32[]{:S(2)}) copy-start(f32[1536]{0:T(1024)} %get-tuple-element.18) | copy-start | bytes 18436
  50.7 26.3 %copy-start.51 = (f32[1536]{0:T(1024)S(1)}, f32[1536]{0:T(1024)}, u32[]{:S(2)}) copy-start(f32[1536]{0:T(1024)} %get-tuple-element.19) | copy-start | bytes 18436
  50.7 27.0 %copy-start.50 = (f32[1536]{0:T(1024)S(1)}, f32[1536]{0:T(1024)}, u32[]{:S(2)}) copy-start(f32[1536]{0:T(1024)} %get-tuple-element.20) | copy-start | bytes 18436
  50.7 27.6 %copy-start.49 = (f32[1536]{0:T(1024)S(1)}, f32[1536]{0:T(1024)}, u32[]{:S(2)}) copy-start(f32[1536]{0:T(1024)} %get-tuple-element.21) | copy-start | bytes 18436
  50.7 28.3 %copy-start.48 = (f32[1536]{0:T(1024)S(1)}, f32[1536]{0:T(1024)}, u32[]{:S(2)}) copy-start(f32[1536]{0:T(1024)} %get-tuple-element.22) | copy-start | bytes 18436
  50.7 29.0 %copy-start.47 = (f32[1536]{0:T(1024)S(1)}, f32[1536]{0:T(1024)}, u32[]{:S(2)}) copy-start(f32[1536]{0:T(1024)} %get-tuple-element.23) | copy-start | bytes 18436
  50.7 29.6 %copy-start.46 = (f32[1536]{0:T(1024)S(1)}, f32[1536]{0:T(1024)}, u32[]{:S(2)}) copy-start(f32[1536]{0:T(1024)} %get-tuple-element.6) | copy-start | bytes 18436
  50.8 30.3 %copy-start.45 = (f32[1536]{0:T(1024)S(1)}, f32[1536]{0:T(1024)}, u32[]{:S(2)}) copy-start(f32[1536]{0:T(1024)} %get-tuple-element.7) | copy-start | bytes 18436
  50.8 31.0 %copy-start.44 = (f32[1536]{0:T(1024)S(1)}, f32[1536]{0:T(1024)}, u32[]{:S(2)}) copy-start(f32[1536]{0:T(1024)} %get-tuple-element.8) | copy-start | bytes 18436
  50.8 31.6 %copy-start.63 = (f32[1536]{0:T(1024)S(1)}, f32[1536]{0:T(1024)}, u32[]{:S(2)}) copy-start(f32[1536]{0:T(1024)} %get-tuple-element.4) | copy-start | bytes 18436
  50.8 45.7 %collective-permute-start.6 = (bf16[384,384]{1,0:T(8,128)(2,1)}, bf16[384,384]{1,0:T(8,128)(2,1)}, u32[]{:S(2)}, u32[]{:S(2)}) collective-permute-start(bf16[384,384]{1,0:T(8,128)(2,1)} %slice.939), channel_id=1, source_target_pairs={{0,12},{1,13},{2,14},{3,15},{4,0},{5,1},{6,2},{7,3},{8,4},{9,5},{1... | collective-permute-start | bytes 884744 | tf_op jit(solution)/shard_map/ppermute | solution.py:17
  52.0 44.5 %collective-permute-start.8 = (bf16[384,384]{1,0:T(8,128)(2,1)}, bf16[384,384]{1,0:T(8,128)(2,1)}, u32[]{:S(2)}, u32[]{:S(2)}) collective-permute-start(bf16[384,384]{1,0:T(8,128)(2,1)} %fusion.74), channel_id=1, source_target_pairs={{0,4},{1,5},{2,6},{3,7},{4,8},{5,9},{6,10},{7,11},{8,12},{9,13},{1... | collective-permute-start | bytes 884744 | tf_op jit(solution)/shard_map/ppermute | solution.py:17
  58.4 38.1 %collective-permute-start.11 = (bf16[384,384]{1,0:T(8,128)(2,1)}, bf16[384,384]{1,0:T(8,128)(2,1)}, u32[]{:S(2)}, u32[]{:S(2)}) collective-permute-start(bf16[384,384]{1,0:T(8,128)(2,1)} %fusion.72), channel_id=1, source_target_pairs={{0,12},{1,13},{2,14},{3,15},{4,0},{5,1},{6,2},{7,3},{8,4},{9,5},{1... | collective-permute-start | bytes 884744 | tf_op jit(solution)/shard_map/ppermute | solution.py:17
  88.4 22.5 %all-to-all-start = ((f32[16,1,3168]{2,1,0:T(1,128)}), f32[16,1,3168]{2,1,0:T(1,128)}, u32[]{:S(2)}, u32[]{:S(2)}) async-start(f32[16,1,3168]{2,1,0:T(1,128)} %all_to_all.16), calls=%async_computation | async-start | bytes 409600 | tf_op jit(solution)/shard_map/all_to_all | solution.py:99
  92.6 18.0 %collective-permute-start.2 = (bf16[16,1536]{1,0:T(8,128)(2,1)}, bf16[16,1536]{1,0:T(8,128)(2,1)S(1)}, u32[]{:S(2)}, u32[]{:S(2)}) collective-permute-start(bf16[16,1536]{1,0:T(8,128)(2,1)} %get-tuple-element.79), channel_id=1, source_target_pairs={{0,1},{1,2},{2,3},{3,4},{4,5},{5,6},{6,7},{7,8},{8,9},{9,10},{10,1... | collective-permute-start | bytes 147464 | tf_op jit(solution)/shard_map/ppermute | solution.py:41
  95.2 15.3 %collective-permute-start.3 = (bf16[16,1536]{1,0:T(8,128)(2,1)S(1)}, bf16[16,1536]{1,0:T(8,128)(2,1)S(1)}, u32[]{:S(2)}, u32[]{:S(2)}) collective-permute-start(bf16[16,1536]{1,0:T(8,128)(2,1)S(1)} %get-tuple-element.80), channel_id=1, source_target_pairs={{1,0},{2,1},{3,2},{4,3},{5,4},{6,5},{7,6},{8,7},{9,8},{10,9},{11,1... | collective-permute-start | bytes 147464 | tf_op jit(solution)/shard_map/ppermute | solution.py:42
  98.0 12.5 %copy-start = (f32[384,384]{1,0:T(8,128)}, f32[384,384]{1,0:T(8,128)S(1)}, u32[]{:S(2)}) copy-start(f32[384,384]{1,0:T(8,128)S(1)} %get-tuple-element.76) | copy-start | bytes 1769476
  98.8 25.2 %collective-permute-start.12 = (bf16[192,768]{1,0:T(8,128)(2,1)}, bf16[192,768]{1,0:T(8,128)(2,1)S(1)}, u32[]{:S(2)}, u32[]{:S(2)}) collective-permute-start(bf16[192,768]{1,0:T(8,128)(2,1)} %fusion.68), channel_id=1, source_target_pairs={{0,2},{1,3},{2,0},{3,1},{4,6},{5,7},{6,4},{7,5},{8,10},{9,11},{10,... | collective-permute-start | bytes 884744 | tf_op jit(solution)/shard_map/ppermute | solution.py:21
  110.8 14.4 %copy-start.3 = (f32[1536]{0:T(1024)S(1)}, f32[1536]{0:T(1024)}, u32[]{:S(2)}) copy-start(f32[1536]{0:T(1024)} %copy-done.2) | copy-start | bytes 18436
  110.8 14.4 %copy-start.5 = (f32[1536]{0:T(1024)S(1)}, f32[1536]{0:T(1024)}, u32[]{:S(2)}) copy-start(f32[1536]{0:T(1024)} %copy-done.4) | copy-start | bytes 18436
  110.8 14.4 %copy-start.7 = (f32[1536]{0:T(1024)S(1)}, f32[1536]{0:T(1024)}, u32[]{:S(2)}) copy-start(f32[1536]{0:T(1024)} %copy-done.6) | copy-start | bytes 18436
  110.8 14.4 %copy-start.9 = (f32[1536]{0:T(1024)S(1)}, f32[1536]{0:T(1024)}, u32[]{:S(2)}) copy-start(f32[1536]{0:T(1024)} %copy-done.8) | copy-start | bytes 18436
  110.8 14.4 %copy-start.11 = (f32[1536]{0:T(1024)S(1)}, f32[1536]{0:T(1024)}, u32[]{:S(2)}) copy-start(f32[1536]{0:T(1024)} %copy-done.10) | copy-start | bytes 18436
  110.8 14.4 %copy-start.13 = (f32[1536]{0:T(1024)S(1)}, f32[1536]{0:T(1024)}, u32[]{:S(2)}) copy-start(f32[1536]{0:T(1024)} %copy-done.12) | copy-start | bytes 18436
  110.8 14.4 %copy-start.15 = (f32[1536]{0:T(1024)S(1)}, f32[1536]{0:T(1024)}, u32[]{:S(2)}) copy-start(f32[1536]{0:T(1024)} %copy-done.14) | copy-start | bytes 18436
  110.8 14.4 %copy-start.17 = (f32[1536]{0:T(1024)S(1)}, f32[1536]{0:T(1024)}, u32[]{:S(2)}) copy-start(f32[1536]{0:T(1024)} %copy-done.16) | copy-start | bytes 18436
  110.8 14.4 %copy-start.19 = (f32[1536]{0:T(1024)S(1)}, f32[1536]{0:T(1024)}, u32[]{:S(2)}) copy-start(f32[1536]{0:T(1024)} %copy-done.18) | copy-start | bytes 18436
  110.8 14.4 %copy-start.21 = (f32[1536]{0:T(1024)S(1)}, f32[1536]{0:T(1024)}, u32[]{:S(2)}) copy-start(f32[1536]{0:T(1024)} %copy-done.20) | copy-start | bytes 18436
  110.9 14.4 %copy-start.23 = (f32[1536]{0:T(1024)S(1)}, f32[1536]{0:T(1024)}, u32[]{:S(2)}) copy-start(f32[1536]{0:T(1024)} %copy-done.22) | copy-start | bytes 18436
  110.9 14.4 %copy-start.25 = (f32[1536]{0:T(1024)S(1)}, f32[1536]{0:T(1024)}, u32[]{:S(2)}) copy-start(f32[1536]{0:T(1024)} %copy-done.24) | copy-start | bytes 18436
  112.8 21.0 %all-to-all-start.1 = ((f32[16,1,288]{2,1,0:T(1,128)}), f32[16,1,288]{2,1,0:T(1,128)S(1)}, u32[]{:S(2)}, u32[]{:S(2)}) async-start(f32[16,1,288]{2,1,0:T(1,128)} %all_to_all.14), calls=%async_computation.1 | async-start | bytes 49152 | tf_op jit(solution)/shard_map/all_to_all | solution.py:104
  125.1 8.8 %collective-permute-start.13 = (bf16[96,768]{1,0:T(8,128)(2,1)S(1)}, bf16[96,768]{1,0:T(8,128)(2,1)S(1)}, u32[]{:S(2)}, u32[]{:S(2)}) collective-permute-start(bf16[96,768]{1,0:T(8,128)(2,1)S(1)} %dynamic-slice_convert_fusion), channel_id=1, source_target_pairs={{0,1},{1,0},{2,3},{3,2},{4,5},{5,4},{6,7},{7,6},{8,9},{9,8},{10,11... | collective-permute-start | bytes 442376 | tf_op jit(solution)/shard_map/ppermute | solution.py:25
  134.0 5.1 %collective-permute-start.14 = (bf16[96,384]{1,0:T(8,128)(2,1)S(1)}, bf16[96,384]{1,0:T(8,128)(2,1)S(1)}, u32[]{:S(2)}, u32[]{:S(2)}) collective-permute-start(bf16[96,384]{1,0:T(8,128)(2,1)S(1)} %get-tuple-element.85), channel_id=1, source_target_pairs={{0,64},{16,80},{32,96},{48,112},{64,128},{80,144},{96,160},{112,17... | collective-permute-start | bytes 221192 | tf_op jit(solution)/shard_map/ppermute | solution.py:29
  134.6 6.0 %collective-permute-start.15 = (bf16[96,384]{1,0:T(8,128)(2,1)S(1)}, bf16[96,384]{1,0:T(8,128)(2,1)S(1)}, u32[]{:S(2)}, u32[]{:S(2)}) collective-permute-start(bf16[96,384]{1,0:T(8,128)(2,1)S(1)} %get-tuple-element.86), channel_id=1, source_target_pairs={{0,128},{16,144},{32,160},{48,176},{64,192},{80,208},{96,224},{112... | collective-permute-start | bytes 221192 | tf_op jit(solution)/shard_map/ppermute | solution.py:29
  137.0 5.6 %collective-permute-start.16 = (bf16[96,384]{1,0:T(8,128)(2,1)S(1)}, bf16[96,384]{1,0:T(8,128)(2,1)S(1)}, u32[]{:S(2)}, u32[]{:S(2)}) collective-permute-start(bf16[96,384]{1,0:T(8,128)(2,1)S(1)} %get-tuple-element.87), channel_id=1, source_target_pairs={{0,192},{16,208},{32,224},{48,240},{64,0},{80,16},{96,32},{112,48}... | collective-permute-start | bytes 221192 | tf_op jit(solution)/shard_map/ppermute | solution.py:29
  142.7 5.7 %collective-permute-start.17 = (bf16[96,96]{1,0:T(8,128)(2,1)S(1)}, bf16[96,96]{1,0:T(8,128)(2,1)S(1)}, u32[]{:S(2)}, u32[]{:S(2)}) collective-permute-start(bf16[96,96]{1,0:T(8,128)(2,1)S(1)} %get-tuple-element.90), channel_id=1, source_target_pairs={{0,16},{16,32},{32,48},{48,0},{64,80},{80,96},{96,112},{112,64},{1... | collective-permute-start | bytes 55304 | tf_op jit(solution)/shard_map/ppermute | solution.py:35
  142.8 5.6 %collective-permute-start.18 = (bf16[96,96]{1,0:T(8,128)(2,1)S(1)}, bf16[96,96]{1,0:T(8,128)(2,1)S(1)}, u32[]{:S(2)}, u32[]{:S(2)}) collective-permute-start(bf16[96,96]{1,0:T(8,128)(2,1)S(1)} %get-tuple-element.92), channel_id=1, source_target_pairs={{0,32},{16,48},{32,0},{48,16},{64,96},{80,112},{96,64},{112,80},{1... | collective-permute-start | bytes 55304 | tf_op jit(solution)/shard_map/ppermute | solution.py:35
  145.3 3.8 %collective-permute-start.19 = (bf16[96,96]{1,0:T(8,128)(2,1)S(1)}, bf16[96,96]{1,0:T(8,128)(2,1)S(1)}, u32[]{:S(2)}, u32[]{:S(2)}) collective-permute-start(bf16[96,96]{1,0:T(8,128)(2,1)S(1)} %get-tuple-element.91), channel_id=1, source_target_pairs={{0,48},{16,0},{32,16},{48,32},{64,112},{80,64},{96,80},{112,96},{1... | collective-permute-start | bytes 55304 | tf_op jit(solution)/shard_map/ppermute | solution.py:35
  (25 other events, 23.5 us)

commit v2 on v1

v2 whole, which is shorter than its diff:
```python
import jax
import jax.numpy as jnp
from jax import lax
from jax.experimental import pallas as pl
from jax.experimental.pallas import tpu as pltpu
from jax.sharding import PartitionSpec as P

KW = 32
HALF = KW // 2
WIDTH = 1536
ROWS = 256
INNER = ROWS - 2 * HALF
LANES = 128
BF16, F32 = jnp.bfloat16, jnp.float32
SEQ = [(y, z, c) for y in range(4) for z in range(2) for c in range(2)]
DP = [(x, z) for x in range(4) for z in range(4)]
VMEM = pl.BlockSpec(memory_space=pltpu.VMEM)
SMEM = pl.BlockSpec(memory_space=pltpu.SMEM)


def seq_at(y, z, c):
    return ((y % 4) * 2 + z % 2) * 2 + c % 2


def move_y(value, step):
    return lax.ppermute(value, "seq", [(seq_at(*p), seq_at(p[0] + step, p[1], p[2])) for p in SEQ])


def move_z_hi(value):
    return lax.ppermute(value, "seq", [(seq_at(*p), seq_at(p[0], p[1] + 1, p[2])) for p in SEQ])


def move_core(value):
    return lax.ppermute(value, "seq", [(seq_at(*p), seq_at(p[0], p[1], p[2] + 1)) for p in SEQ])


def move_x(value, step):
    return lax.ppermute(value, "dp", [(x * 4 + z, ((x + step) % 4) * 4 + z) for x, z in DP])


def move_z_lo(value, step):
    return lax.ppermute(value, "dp", [(x * 4 + z, x * 4 + (z + step) % 4) for x, z in DP])


def halo(block):
    low = lax.ppermute(block[-HALF:], "seq", [(i, i + 1) for i in range(15)])
    high = lax.ppermute(block[:HALF], "seq", [(i + 1, i) for i in range(15)])
    return jnp.concatenate([low, high], axis=0)


def part(value, index, size, axis):
    return lax.dynamic_slice_in_dim(value, index * size, size, axis)


def masked_rows(rows, first, length):
    position = first + lax.broadcasted_iota(jnp.int32, rows.shape, 0)
    return jnp.where(position < length, rows.astype(F32), 0.0)


def depthwise(x_ref, taps_ref, out_ref, rows, chunk, finish=None, taps=None):
    taps = {j: j for j in range(KW)} if taps is None else taps

    def lane_block(i, carry):
        lanes = pl.ds(pl.multiple_of(i * LANES, LANES), LANES)
        for begin in range(0, rows, chunk):
            x = x_ref[pl.ds(begin, chunk + KW), lanes]
            total = None
            for shift in range(8):
                span = chunk if shift == 0 else chunk + 8
                sum_ = None
                for j in range(shift, KW + 1, 8):
                    if j in taps:
                        term = taps_ref[pl.ds(taps[j], 1), lanes] * x[j - shift : j - shift + span]
                        sum_ = term if sum_ is None else sum_ + term
                if shift:
                    sum_ = pltpu.roll(sum_, span - shift, 0)[:chunk]
                total = sum_ if total is None else total + sum_
            if finish is not None:
                total = finish(total, begin)
            out_ref[pl.ds(begin, chunk), lanes] = total
        return carry

    lax.fori_loop(0, WIDTH // LANES, lane_block, 0)


def normalise_rows(conv, upstream, gain, valid):
    mean = jnp.sum(conv, axis=1, keepdims=True) * (1.0 / WIDTH)
    centered = conv - mean
    variance = jnp.sum(centered * centered, axis=1, keepdims=True) * (1.0 / WIDTH)
    inverse = lax.rsqrt(variance + 1e-05)
    standardized = centered * inverse
    normalized = standardized * gain
    sigma = 1.0 / (1.0 + jnp.exp(-normalized))
    hidden = normalized * sigma
    grad = jnp.where(valid, upstream * (sigma + hidden * (1.0 - sigma)), 0.0)
    gain_term = grad * standardized
    scaled = grad * gain
    first = jnp.sum(scaled, axis=1, keepdims=True) * (1.0 / WIDTH)
    second = jnp.sum(scaled * standardized, axis=1, keepdims=True) * (1.0 / WIDTH)
    conv_grad = inverse * (scaled - first - standardized * second)
    return jnp.where(valid, hidden, 0.0), conv_grad, gain_term


def row_blocks(conv_ref, grad_ref, gain_ref, hidden_ref, conv_grad_ref, gain_sum, rows, offset, first, length):
    def block(i, total):
        local = pl.ds(pl.multiple_of(i * 16, 16), 16)
        whole = pl.ds(pl.multiple_of(i * 16 + offset, 16), 16)
        position = first + offset + i * 16 + lax.broadcasted_iota(jnp.int32, (16, 1), 0)
        hidden, conv_grad, gain_term = normalise_rows(
            conv_ref[local, :], grad_ref[whole, :], gain_ref[...], position < length
        )
        hidden_ref[whole, :] = hidden.astype(BF16)
        conv_grad_ref[whole, :] = conv_grad.astype(BF16)
        return total + gain_term[:8] + gain_term[8:]

    gain_sum[...] = lax.fori_loop(0, rows // 16, block, jnp.zeros((8, WIDTH), F32))


def inner_kernel(where, frames, upstream, taps, gain, hidden, conv_grad, gain_sum, x, conv):
    x[...] = masked_rows(frames[...], where[0], where[1])
    depthwise(x, taps, conv, INNER, 112)
    row_blocks(conv, upstream, gain, hidden, conv_grad, gain_sum, INNER, HALF, where[0], where[1])


def edge_kernel(where, frames, sides, upstream, taps, gain, _, __, hidden, conv_grad, gain_sum, x, conv):
    bottom = pl.program_id(0)
    first, length = where[0] + bottom * (ROWS - HALF), where[1]
    block = frames[...].astype(F32)
    side = sides[...].astype(F32)

    @pl.when(bottom == 0)
    def _top():
        x[pl.ds(0, HALF), :] = side
        x[pl.ds(HALF, 2 * HALF), :] = block

    @pl.when(bottom == 1)
    def _bottom():
        x[pl.ds(0, 2 * HALF), :] = block
        x[pl.ds(2 * HALF, HALF), :] = side

    x[...] = masked_rows(x[...], first - HALF, length)
    depthwise(x, taps, conv, HALF, HALF)
    row_blocks(conv, upstream, gain, hidden, conv_grad, gain_sum, HALF, 0, first, length)


def rows_of(shape, dtype):
    return jax.ShapeDtypeStruct(shape, dtype)


def forward_inner(where, frames, upstream, taps, gain):
    return pl.pallas_call(
        inner_kernel,
        out_shape=(rows_of((ROWS, WIDTH), BF16), rows_of((ROWS, WIDTH), BF16), rows_of((8, WIDTH), F32)),
        in_specs=[SMEM, VMEM, VMEM, VMEM, VMEM],
        out_specs=(VMEM, VMEM, VMEM),
        scratch_shapes=[pltpu.VMEM((ROWS, WIDTH), F32), pltpu.VMEM((INNER, WIDTH), F32)],
        compiler_params=pltpu.CompilerParams(vmem_limit_bytes=32 << 20),
        cost_estimate=pl.CostEstimate(flops=60_000_000, bytes_accessed=4_000_000, transcendentals=800_000),
        name="forward_inner",
    )(where, frames, upstream, taps, gain)


def forward_edge(where, frames, sides, upstream, taps, gain, hidden, conv_grad):
    return pl.pallas_call(
        edge_kernel,
        grid=(2,),
        out_shape=(rows_of((ROWS, WIDTH), BF16), rows_of((ROWS, WIDTH), BF16), rows_of((16, WIDTH), F32)),
        in_specs=[
            SMEM,
            pl.BlockSpec((2 * HALF, WIDTH), lambda i: (7 * i, 0)),
            pl.BlockSpec((HALF, WIDTH), lambda i: (i, 0)),
            pl.BlockSpec((HALF, WIDTH), lambda i: (15 * i, 0)),
            pl.BlockSpec((KW, WIDTH), lambda i: (0, 0)),
            pl.BlockSpec((1, WIDTH), lambda i: (0, 0)),
            pl.BlockSpec(memory_space=pl.ANY),
            pl.BlockSpec(memory_space=pl.ANY),
        ],
        out_specs=(
            pl.BlockSpec((HALF, WIDTH), lambda i: (15 * i, 0)),
            pl.BlockSpec((HALF, WIDTH), lambda i: (15 * i, 0)),
            pl.BlockSpec((8, WIDTH), lambda i: (i, 0)),
        ),
        scratch_shapes=[pltpu.VMEM((3 * HALF, WIDTH), F32), pltpu.VMEM((HALF, WIDTH), F32)],
        input_output_aliases={6: 0, 7: 1},
        compiler_params=pltpu.CompilerParams(vmem_limit_bytes=32 << 20),
        cost_estimate=pl.CostEstimate(flops=8_000_000, bytes_accessed=1_000_000, transcendentals=100_000),
        name="forward_edge",
    )(where, frames, sides, upstream, taps, gain, hidden, conv_grad)


def kernel_grad_kernel(where, frames, sides, conv_grad, gain_inner, gain_edge, out, x, g):
    first, length = where[0], where[1]
    x[pl.ds(0, HALF), :] = masked_rows(sides[pl.ds(0, HALF), :], first - HALF, length)
    x[pl.ds(HALF, ROWS), :] = masked_rows(frames[...], first, length)
    x[pl.ds(HALF + ROWS, HALF), :] = masked_rows(sides[pl.ds(HALF, HALF), :], first + ROWS, length)
    g[pl.ds(0, 8), :] = jnp.zeros((8, WIDTH), F32)
    g[pl.ds(8, ROWS), :] = conv_grad[...].astype(F32)
    g[pl.ds(8 + ROWS, 8), :] = jnp.zeros((8, WIDTH), F32)
    chunk = 88

    def lane_block(i, carry):
        lanes = pl.ds(pl.multiple_of(i * LANES, LANES), LANES)
        sums = [None] * KW
        for begin in range(0, ROWS + 8, chunk):
            rows = x_rows = x[pl.ds(begin, chunk + KW - 8), lanes]
            grad = g[pl.ds(begin, chunk + 8), lanes]
            for shift in range(8):
                moved = grad[8:] if shift == 0 else pltpu.roll(grad, shift, 0)[8:]
                for a in range(KW // 8):
                    j = 8 * a + shift
                    product = (moved * x_rows[8 * a : 8 * a + chunk]).reshape(chunk // 8, 8, LANES)
                    product = jnp.sum(product, axis=0)
                    sums[j] = product if sums[j] is None else sums[j] + product
        out[pl.ds(0, KW), lanes] = jnp.concatenate(
            [jnp.sum(value, axis=0, keepdims=True) for value in sums], axis=0
        )
        gain = gain_inner[:, lanes] + gain_edge[pl.ds(0, 8), lanes] + gain_edge[pl.ds(8, 8), lanes]
        out[pl.ds(KW, 8), lanes] = jnp.broadcast_to(jnp.sum(gain, axis=0, keepdims=True), (8, LANES))
        return carry

    lax.fori_loop(0, WIDTH // LANES, lane_block, 0)


def kernel_grads(where, frames, sides, conv_grad, gain_inner, gain_edge):
    return pl.pallas_call(
        kernel_grad_kernel,
        out_shape=rows_of((KW + 8, WIDTH), F32),
        in_specs=[SMEM, VMEM, VMEM, VMEM, VMEM, VMEM],
        out_specs=VMEM,
        scratch_shapes=[pltpu.VMEM((ROWS + KW, WIDTH), F32), pltpu.VMEM((ROWS + 16, WIDTH), F32)],
        compiler_params=pltpu.CompilerParams(vmem_limit_bytes=32 << 20),
        cost_estimate=pl.CostEstimate(flops=50_000_000, bytes_accessed=2_000_000, transcendentals=0),
        name="kernel_grads",
    )(where, frames, sides, conv_grad, gain_inner, gain_edge)


def input_grad_kernel(where, conv_grad, sides, taps, out, g):
    first, length = where[0], where[1]
    g[pl.ds(0, HALF), :] = sides[pl.ds(0, HALF), :].astype(F32)
    g[pl.ds(HALF, ROWS), :] = conv_grad[...].astype(F32)
    g[pl.ds(HALF + ROWS, HALF), :] = sides[pl.ds(HALF, HALF), :].astype(F32)

    def finish(total, begin):
        return masked_rows(total, first + begin, length).astype(BF16)

    depthwise(g, taps, out, ROWS, 64, finish, {j: KW - j for j in range(1, KW + 1)})


def input_grads(where, conv_grad, sides, taps):
    return pl.pallas_call(
        input_grad_kernel,
        out_shape=rows_of((ROWS, WIDTH), BF16),
        in_specs=[SMEM, VMEM, VMEM, VMEM],
        out_specs=VMEM,
        scratch_shapes=[pltpu.VMEM((ROWS + KW, WIDTH), F32)],
        compiler_params=pltpu.CompilerParams(vmem_limit_bytes=32 << 20),
        cost_estimate=pl.CostEstimate(flops=50_000_000, bytes_accessed=2_000_000, transcendentals=0),
        name="input_grads",
    )(where, conv_grad, sides, taps)


def reduce_out(hidden, cot_pair):
    seq = lax.axis_index("seq")
    y, z_hi, core = seq // 4, (seq // 2) % 2, seq % 2
    hidden_pair = jnp.concatenate([hidden, move_core(hidden)], axis=0)

    def chunk(step):
        rows = part(hidden_pair, (y + step) % 4, 384, 1)
        return lax.dot_general(
            rows, cot_pair, (((0,), (0,)), ((), ())), preferred_element_type=F32
        )

    far = chunk(2).astype(BF16)
    up_a = move_y(far[:, :384], 1)
    down_b = move_y(far[:, 384:], -1)
    above = chunk(1)
    below = chunk(3)
    up_b = move_y(above[:, 384:].astype(BF16), 1)
    down_a = move_y(below[:, :384].astype(BF16), -1)
    own = chunk(0)
    up_a = move_y((above[:, :384] + up_a.astype(F32)).astype(BF16), 1)
    down_b = move_y((below[:, 384:] + down_b.astype(F32)).astype(BF16), -1)
    low = own[:, :384] + down_a.astype(F32) + up_a.astype(F32)
    high = own[:, 384:] + up_b.astype(F32) + down_b.astype(F32)
    total = jnp.concatenate([low, high], axis=1)
    sent = total.astype(BF16)

    def rows_for(z, c):
        return part(sent, 2 * z + c, 96, 0)

    across = move_z_hi(rows_for(1 - z_hi, core))
    diagonal = lax.ppermute(
        rows_for(1 - z_hi, 1 - core), "seq", [(seq_at(*p), seq_at(p[0], p[1] + 1, p[2] + 1)) for p in SEQ]
    )
    beside = move_core(rows_for(z_hi, 1 - core))
    mine = part(total, 2 * z_hi + core, 96, 0) + across.astype(F32)
    other = beside.astype(F32) + diagonal.astype(F32)
    square = jnp.concatenate(
        [jnp.where(core == 0, mine, other), jnp.where(core == 0, other, mine)], axis=1
    )
    square = square * square
    dp = lax.axis_index("dp")
    x, z_lo = dp // 4, dp % 4
    received = [move_x(part(square, (x + k) % 4, 384, 1).astype(BF16), k) for k in (1, 2, 3)]
    square = part(square, x, 384, 1)
    for value in received:
        square = square + value.astype(F32)
    received = [move_z_lo(part(square, (z_lo + k) % 4, 96, 1).astype(BF16), k) for k in (1, 2, 3)]
    square = part(square, z_lo, 96, 1)
    for value in received:
        square = square + value.astype(F32)
    return square


def reduce_rows(rows):
    rows = rows[: KW + 1].reshape(KW + 1, 16, 96).transpose(1, 0, 2).reshape(16, (KW + 1) * 96)
    rows = lax.all_to_all(rows, "seq", 0, 0, tiled=True).sum(axis=0)
    square = (rows * rows).reshape(KW + 1, 96)
    kernel = square[:KW].reshape(16, 2 * 96)
    gain = jnp.broadcast_to(square[KW][None], (16, 96))
    rows = jnp.concatenate([kernel, gain], axis=1)
    rows = lax.all_to_all(rows, "dp", 0, 0, tiled=True).sum(axis=0)
    return rows[: 2 * 96].reshape(2, 96), rows[2 * 96 :]


def on_device(frames_in, cotangent, lengths, out_weight, conv_kernel, layer_norm_gain):
    seq = lax.axis_index("seq")
    core = seq % 2
    where = jnp.stack([seq * ROWS, lengths[0]]).astype(jnp.int32)
    frames, cot = frames_in[0], cotangent[0]
    gain = layer_norm_gain[None]
    sides = halo(frames)
    cot_pair = jnp.concatenate([part(cot, core, 768, 1), move_core(part(cot, 1 - core, 768, 1))], axis=0)
    upstream = lax.dot_general(cot, out_weight, (((1,), (1,)), ((), ())), preferred_element_type=F32)
    hidden, conv_grad, gain_inner = forward_inner(where, frames, upstream, conv_kernel, gain)
    hidden, conv_grad, gain_edge = forward_edge(
        where, frames, sides, upstream, conv_kernel, gain, hidden, conv_grad
    )
    fisher_out = reduce_out(hidden, cot_pair)
    grad_sides = halo(conv_grad)
    rows = kernel_grads(where, frames, sides, conv_grad, gain_inner, gain_edge)
    fisher_kernel, fisher_gain = reduce_rows(rows)
    input_grad = input_grads(where, conv_grad, grad_sides, conv_kernel)
    return input_grad[None], fisher_out / 16, fisher_kernel / 16, fisher_gain / 16


def solution(mesh):
    return jax.shard_map(
        on_device,
        mesh=mesh,
        in_specs=(P("dp", "seq", None), P("dp", "seq", None), P("dp"), P(), P(), P()),
        out_specs=(P("dp", "seq", None), P("seq", "dp"), P("dp", "seq"), P("seq")),
        check_vma=False,
    )
```

time: 151 us -> 126 us (0.83)
  other arithmetic: 35 us -> 4.79 us
  Pallas kernels: 0 us -> 24.1 us
  local copies, waits for them, and re-layouts: 31.3 us -> 9.74 us
  matrix products: 4.55 us -> 10.7 us
  waiting for transfers between devices: 15.7 us -> 14.1 us
    concatenate x34 -> x2, local copies, waits for them, and re-layouts: 25.4 us -> 1.19 us  [the longest x1 1.19 us: reduce_out(): hidden_pair = jnp.concatenate([hidden, move_core(hidden)], axis=0)]
    pallas_call x0 -> x4, Pallas kernels: none -> 24.1 us  [the longest x1 9.44 us: forward_inner(): pl.pallas_call(inner_kernel, out_shape=(rows_of((ROWS, WIDTH), BF16), row...]
    reduce_sum x4 -> x0, other arithmetic: 17.1 us -> none  [the longest x2 8.5 us: on_device(): jnp.sum(conv_wide * padded_wide[offset:offset + frame_count], axis=0)]
    broadcast_in_dim x1 -> x0, other arithmetic: 8.49 us -> none  [on_device(): input_grad = jnp.where(valid, summed, 0.0).astype(bf16)[None]]
    ppermute x3, starting transfers between devices: 14.3 us -> 8.23 us  [move_core(): lax.ppermute(value, 'seq', [(seq_at(*p), seq_at(p[0], p[1], p[2] + 1)) fo...]
    all_to_all x1, starting transfers between devices: 4.17 us -> 10 us  [reduce_rows(): rows = lax.all_to_all(rows, 'seq', 0, 0, tiled=True).sum(axis=0)]
    ppermute x4 -> x5, waiting for transfers between devices: 0.01 us -> 5.3 us  [the longest x1 5.29 us: reduce_out(): lax.ppermute(rows_for(1 - z_hi, 1 - core), 'seq', [(seq_at(*p), seq_at(p[...]
    ppermute x1, starting transfers between devices: 11.7 us -> 6.84 us  [move_z_hi(): lax.ppermute(value, 'seq', [(seq_at(*p), seq_at(p[0], p[1] + 1, p[2])) fo...]
  transfers between devices with their start and end apart: 22 -> 23, of which waited for: 8 -> 9; matrix products, arithmetic and copies ran while one was open for 44% -> 17% of each run, Pallas kernels for 0% -> 17%
where the time goes in v2:
time: 126 us; the launch traced here: 125 us
  starting transfers between devices  59.9 us (48%)
  Pallas kernels  24.1 us (19%)
  waiting for transfers between devices  14.1 us (11%)
  matrix products  10.7 us (8%)
  local copies, waits for them, and re-layouts  9.74 us (8%)
  other arithmetic  4.79 us (4%)
  between operations  1.64 us (1%)
    all_to_all x1, starting transfers between devices, reduce_rows(): rows = lax.all_to_all(rows, 'seq', 0, 0, tiled=True).sum(axis=0)  10 us
    all_to_all x1, starting transfers between devices, reduce_rows(): rows = lax.all_to_all(rows, 'dp', 0, 0, tiled=True).sum(axis=0)  9.95 us
    pallas_call x1, Pallas kernels, forward_inner(): pl.pallas_call(inner_kernel, out_shape=(rows_of((ROWS, WIDTH), BF16), row...  9.44 us
    ppermute x6, starting transfers between devices, move_y(): lax.ppermute(value, 'seq', [(seq_at(*p), seq_at(p[0] + step, p[1], p[2]))...  8.5 us
    ppermute x3, starting transfers between devices, move_core(): lax.ppermute(value, 'seq', [(seq_at(*p), seq_at(p[0], p[1], p[2] + 1)) fo...  8.23 us
    ppermute x3, starting transfers between devices, move_z_lo(): lax.ppermute(value, 'dp', [(x * 4 + z, x * 4 + (z + step) % 4) for x, z i...  7.11 us
    ppermute x1, starting transfers between devices, move_z_hi(): lax.ppermute(value, 'seq', [(seq_at(*p), seq_at(p[0], p[1] + 1, p[2])) fo...  6.84 us
    dot_general x4, matrix products, chunk(): lax.dot_general(rows, cot_pair, (((0,), (0,)), ((), ())), preferred_eleme...  6.67 us
  transfers between devices with their start and end apart: 23, of which 9 were waited for; matrix products, arithmetic and copies ran while one was open for 17% of the time, Pallas kernels for 17%

profile of v2, /device:TPU:6, one launch (start us, length us, event | category | flops | bytes accessed | tf_op | source)
XLA Modules:
  0.0 125.1 jit_solution(9194855993535406789)
XLA Ops:
  0.6 0.8 slice_bitcast_fusion
  1.5 1.7 %collective-permute-start = (bf16[16,1536]{1,0:T(8,128)(2,1)S(1)}, bf16[16,1536]{1,0:T(8,128)(2,1)S(1)}, u32[]{:S(2)}, u32[]{:S(2)}) collective-permute-start(bf16[16,1536]{1,0:T(8,128)(2,1)S(1)} %get-tuple-element.25), channel_id=1, source_target_pairs={{0,1},{1,2},{2,3},{3,4},{4,5},{5,6},{6,7},{7,8},{8,9},{9,10},{10,1... | collective-permute-start | bytes 147464 | tf_op jit(solution)/shard_map/ppermute | solution.py:46
  3.2 1.3 %collective-permute-start.1 = (bf16[16,1536]{1,0:T(8,128)(2,1)S(1)}, bf16[16,1536]{1,0:T(8,128)(2,1)S(1)}, u32[]{:S(2)}, u32[]{:S(2)}) collective-permute-start(bf16[16,1536]{1,0:T(8,128)(2,1)S(1)} %get-tuple-element.24), channel_id=1, source_target_pairs={{1,0},{2,1},{3,2},{4,3},{5,4},{6,5},{7,6},{8,7},{9,8},{10,9},{11,1... | collective-permute-start | bytes 147464 | tf_op jit(solution)/shard_map/ppermute | solution.py:47
  5.2 0.0 copy-start.3
  5.2 4.1 %fusion.1.upstream = f32[256,1536]{1,0:T(8,128)S(1)} fusion(bf16[1536,1536]{1,0:T(8,128)(2,1)} %param.9, bf16[1,256,1536]{2,1,0:T(8,128)(2,1)} %param.7), kind=kOutput, calls=%fused_computation.6 | convolution fusion | flops 1207959552 | bytes 7077888 | tf_op jit(solution)/shard_map/dot_general | solution.py:334
  9.3 0.1 pad_add_fusion.where
  9.4 9.4 %forward_inner.1 = (bf16[256,1536]{1,0:T(8,128)(2,1)S(1)}, bf16[256,1536]{1,0:T(8,128)(2,1)S(1)}, f32[8,1536]{1,0:T(8,128)S(1)}) custom-call(s32[2]{0:T(128)S(1)} %pad_add_fusion.where, bf16[256,1536]{1,0:T(8,128)(2,1)S(1)} %bitcast.19, f32[256,1536]{1,0:T(8,128)S(1)} %fusion.1.upstream, f32[32,1536]{1,0:T(8,128)S(1)} %copy-done.1, ...), custom_call_target="tpu_custom_call" | custom-call | flops 60000000 | bytes 4000000 | tf_op jit(solution)/shard_map/forward_inner/pallas_call | solution.py:151
  18.9 2.3 %forward_edge.1 = (bf16[256,1536]{1,0:T(8,128)(2,1)S(1)}, bf16[256,1536]{1,0:T(8,128)(2,1)S(1)}, f32[16,1536]{1,0:T(8,128)S(1)}) custom-call(s32[2]{0:T(128)S(1)} %pad_add_fusion.where, bf16[256,1536]{1,0:T(8,128)(2,1)S(1)} %bitcast.20, bf16[32,1536]{1,0:T(8,128)(2,1)S(1)} %constant_dynamic-update-slice_fusion.sides, ...), custom_call_target="tpu_custom_call", output_to_operand_aliasing={{0}: (6, {}), {1}: (7, {})} | custom-call | flops 8000000 | bytes 1000000 | tf_op jit(solution)/shard_map/forward_edge/pallas_call | solution.py:164
  21.1 8.2 %collective-permute-start.4 = (bf16[256,1536]{1,0:T(8,128)(2,1)S(1)}, bf16[256,1536]{1,0:T(8,128)(2,1)}, u32[]{:S(2)}, u32[]{:S(2)}) collective-permute-start(bf16[256,1536]{1,0:T(8,128)(2,1)S(1)} %get-tuple-element.13), channel_id=1, source_target_pairs={{0,1},{1,0},{2,3},{3,2},{4,5},{5,4},{6,7},{7,6},{8,9},{9,8},{10,11... | collective-permute-start | bytes 2359304 | tf_op jit(solution)/shard_map/ppermute | solution.py:34
  29.3 1.9 %dynamic-slice_bitcast_fusion.1 = (bf16[256,768]{1,0:T(8,128)(2,1)S(1)}, bf16[256,768]{1,0:T(8,128)(2,1)}) fusion(bf16[1,256,1536]{2,1,0:T(8,128)(2,1)} %param.7, s32[]{:T(128)S(6)} %select_n.138, s32[]{:T(128)S(6)} %select_n.139), kind=kLoop, calls=%fused_computation.25 | loop fusion | bytes 1572872 | tf_op jit(solution)/shard_map/dynamic_slice | solution.py:52
  31.2 0.0 collective-permute-start.5
  31.3 6.1 %kernel_grads.1 = f32[40,1536]{1,0:T(8,128)S(1)} custom-call(s32[2]{0:T(128)S(1)} %pad_add_fusion.where, bf16[256,1536]{1,0:T(8,128)(2,1)S(1)} %bitcast.21, bf16[32,1536]{1,0:T(8,128)(2,1)S(1)} %constant_dynamic-update-slice_fusion.sides, bf16[256,1536]{1,0:T(8,128)(2,1)S(1)} %get-tuple-element.12.conv_grad, f32[8,1536]{1,0:T(8,128)S(1)} %get-tuple-element.14.gain_inner, ...), custom_call_target="tpu_custom_call" | custom-call | flops 50000000 | bytes 2000000 | tf_op jit(solution)/shard_map/kernel_grads/pallas_call | solution.py:225
  37.3 0.1 reshape.40
  37.5 0.1 copy.16
  37.6 1.0 all_to_all.16
  38.5 10.0 %all-to-all-start = ((f32[16,1,3168]{2,1,0:T(1,128)}), f32[16,1,3168]{2,1,0:T(1,128)S(1)}, u32[]{:S(2)}, u32[]{:S(2)}) async-start(f32[16,1,3168]{2,1,0:T(1,128)} %all_to_all.16), calls=%async_computation | async-start | bytes 409600 | tf_op jit(solution)/shard_map/all_to_all | solution.py:317
  48.5 0.1 constant_dynamic-update-slice_fusion.3
  48.6 1.2 constant_dynamic-update-slice_fusion.2
  49.8 1.8 %convolution_convert_fusion = bf16[384,768]{1,0:T(8,128)(2,1)S(1)} fusion(bf16[512,1536]{1,0:T(8,128)(2,1)S(1)} %constant_dynamic-update-slice_fusion.2, s32[]{:T(128)S(6)} %select_n.145, bf16[256,768]{1,0:T(8,128)(2,1)} %collective-permute-done.5, bf16[256,768]{1,0:T(8,128)(2,1)S(1)} %get-tuple-element.20), kind=kOutput, calls=%fused_computation.3 | convolution fusion | flops 303857664 | bytes 1769476 | tf_op jit(solution)/shard_map/dot_general | solution.py:269
  51.6 0.8 fusion.23
  52.4 3.2 %collective-permute-start.10 = (bf16[384,384]{1,0:T(8,128)(2,1)S(1)}, bf16[384,384]{1,0:T(8,128)(2,1)}, u32[]{:S(2)}, u32[]{:S(2)}) collective-permute-start(bf16[384,384]{1,0:T(8,128)(2,1)S(1)} %get-tuple-element.33), channel_id=1, source_target_pairs={{0,12},{1,13},{2,14},{3,15},{4,0},{5,1},{6,2},{7,3},{8,4},{9,5},{1... | collective-permute-start | bytes 884744 | tf_op jit(solution)/shard_map/ppermute | solution.py:26
  55.6 0.6 fusion.22
  56.2 1.8 %collective-permute-start.2 = (bf16[16,1536]{1,0:T(8,128)(2,1)}, bf16[16,1536]{1,0:T(8,128)(2,1)S(1)}, u32[]{:S(2)}, u32[]{:S(2)}) collective-permute-start(bf16[16,1536]{1,0:T(8,128)(2,1)} %get-tuple-element.22), channel_id=1, source_target_pairs={{0,1},{1,2},{2,3},{3,4},{4,5},{5,6},{6,7},{7,8},{8,9},{9,10},{10,1... | collective-permute-start | bytes 147464 | tf_op jit(solution)/shard_map/ppermute | solution.py:46
  58.0 2.0 %all-to-all-done = f32[16,1,3168]{2,1,0:T(1,128)S(1)} async-done(((f32[16,1,3168]{2,1,0:T(1,128)}), f32[16,1,3168]{2,1,0:T(1,128)S(1)}, u32[]{:S(2)}, u32[]{:S(2)}) %all-to-all-start) | async-done | bytes 202784 | tf_op jit(solution)/shard_map/all_to_all | solution.py:317
  60.0 0.1 reduce_sum.18
  60.2 0.1 reshape.41
  60.2 0.1 pad.1.clone
  60.3 1.6 %fusion.10 = f32[384,768]{1,0:T(8,128)S(1)} fusion(bf16[512,1536]{1,0:T(8,128)(2,1)} %copy-done.2, s32[]{:T(128)S(6)} %select_n.141, bf16[256,768]{1,0:T(8,128)(2,1)} %collective-permute-done.5, bf16[256,768]{1,0:T(8,128)(2,1)S(1)} %get-tuple-element.20), kind=kOutput, calls=%fused_computation.22 | convolution fusion | flops 303562752 | bytes 2359300 | tf_op jit(solution)/shard_map/dot_general | solution.py:269
  61.9 0.7 slice.118
  62.7 0.9 collective-permute-start.6
  63.5 1.2 collective-permute-start.7
  64.7 1.6 %fusion.8 = f32[384,768]{1,0:T(8,128)S(1)} fusion(bf16[512,1536]{1,0:T(8,128)(2,1)} %copy-done.2, s32[]{:T(128)S(6)} %select_n.143, bf16[256,768]{1,0:T(8,128)(2,1)} %collective-permute-done.5, bf16[256,768]{1,0:T(8,128)(2,1)S(1)} %get-tuple-element.20), kind=kOutput, calls=%fused_computation.20 | convolution fusion | flops 303562752 | bytes 2359300 | tf_op jit(solution)/shard_map/dot_general | solution.py:269
  66.3 0.8 slice.117
  67.1 1.8 %fusion.3 = bf16[384,384]{1,0:T(8,128)(2,1)} fusion(f32[384,768]{1,0:T(8,128)S(1)} %fusion.10, bf16[384,384]{1,0:T(8,128)(2,1)} %collective-permute-done.10), kind=kLoop, calls=%fused_computation.9 | loop fusion | flops 442368 | bytes 1179648 | tf_op jit(solution)/shard_map/convert_element_type | solution.py:282
  68.9 3.2 %collective-permute-start.11 = (bf16[384,384]{1,0:T(8,128)(2,1)}, bf16[384,384]{1,0:T(8,128)(2,1)S(1)}, u32[]{:S(2)}, u32[]{:S(2)}) collective-permute-start(bf16[384,384]{1,0:T(8,128)(2,1)} %fusion.3), channel_id=1, source_target_pairs={{0,12},{1,13},{2,14},{3,15},{4,0},{5,1},{6,2},{7,3},{8,4},{9,5},{1... | collective-permute-start | bytes 884744 | tf_op jit(solution)/shard_map/ppermute | solution.py:26
  72.1 0.3 collective-permute-done.7
  72.4 0.1 fusion.5
  72.5 0.1 collective-permute-start.8
  72.6 0.6 all_to_all.14
  73.2 9.9 %all-to-all-start.1 = ((f32[16,1,288]{2,1,0:T(1,128)}), f32[16,1,288]{2,1,0:T(1,128)S(1)}, u32[]{:S(2)}, u32[]{:S(2)}) async-start(f32[16,1,288]{2,1,0:T(1,128)} %all_to_all.14), calls=%async_computation.1 | async-start | bytes 49152 | tf_op jit(solution)/shard_map/all_to_all | solution.py:322
  83.2 1.6 %fusion.12 = f32[384,768]{1,0:T(8,128)S(1)} fusion(bf16[512,1536]{1,0:T(8,128)(2,1)} %copy-done.2, s32[]{:T(128)S(6)} %select_n.137, bf16[256,768]{1,0:T(8,128)(2,1)} %collective-permute-done.5, bf16[256,768]{1,0:T(8,128)(2,1)S(1)} %get-tuple-element.20), kind=kOutput, calls=%fused_computation.26 | convolution fusion | flops 303562752 | bytes 2359300 | tf_op jit(solution)/shard_map/dot_general | solution.py:269
  84.8 1.3 %collective-permute-start.3 = (bf16[16,1536]{1,0:T(8,128)(2,1)}, bf16[16,1536]{1,0:T(8,128)(2,1)S(1)}, u32[]{:S(2)}, u32[]{:S(2)}) collective-permute-start(bf16[16,1536]{1,0:T(8,128)(2,1)} %get-tuple-element.23), channel_id=1, source_target_pairs={{1,0},{2,1},{3,2},{4,3},{5,4},{6,5},{7,6},{8,7},{9,8},{10,9},{11,1... | collective-permute-start | bytes 147464 | tf_op jit(solution)/shard_map/ppermute | solution.py:47
  86.1 1.2 fusion.6
  87.3 0.1 fusion
  87.4 6.8 %collective-permute-start.12 = (bf16[96,768]{1,0:T(8,128)(2,1)S(1)}, bf16[96,768]{1,0:T(8,128)(2,1)S(1)}, u32[]{:S(2)}, u32[]{:S(2)}) collective-permute-start(bf16[96,768]{1,0:T(8,128)(2,1)S(1)} %get-tuple-element.29), channel_id=1, source_target_pairs={{0,2},{1,3},{2,0},{3,1},{4,6},{5,7},{6,4},{7,5},{8,10},{9,11},{10,... | collective-permute-start | bytes 442376 | tf_op jit(solution)/shard_map/ppermute | solution.py:30
  94.3 0.2 collective-permute-start.14
  94.5 6.4 %input_grads.1 = bf16[256,1536]{1,0:T(8,128)(2,1)} custom-call(s32[2]{0:T(128)S(1)} %pad_add_fusion.where, bf16[256,1536]{1,0:T(8,128)(2,1)S(1)} %get-tuple-element.12.conv_grad, bf16[32,1536]{1,0:T(8,128)(2,1)S(1)} %pad_maximum_fusion.2.sides, f32[32,1536]{1,0:T(8,128)S(1)} %copy-done.1), custom_call_target="tpu_custom_call" | custom-call | flops 50000000 | bytes 2000000 | tf_op jit(solution)/shard_map/input_grads/pallas_call | solution.py:250
  100.9 0.2 collective-permute-done.12
  101.1 5.3 %collective-permute-done.14 = bf16[96,768]{1,0:T(8,128)(2,1)S(1)} collective-permute-done((bf16[96,768]{1,0:T(8,128)(2,1)S(1)}, bf16[96,768]{1,0:T(8,128)(2,1)S(1)}, u32[]{:S(2)}, u32[]{:S(2)}) %collective-permute-start.14) | collective-permute-done | bytes 147488 | tf_op jit(solution)/shard_map/ppermute | solution.py:292
  106.4 0.1 fusion.17
  106.6 0.5 collective-permute-start.15
  107.1 2.5 %collective-permute-start.16 = (bf16[96,384]{1,0:T(8,128)(2,1)S(1)}, bf16[96,384]{1,0:T(8,128)(2,1)S(1)}, u32[]{:S(2)}, u32[]{:S(2)}) collective-permute-start(bf16[96,384]{1,0:T(8,128)(2,1)S(1)} %get-tuple-element.28), channel_id=1, source_target_pairs={{0,128},{16,144},{32,160},{48,176},{64,192},{80,208},{96,224},{112... | collective-permute-start | bytes 221192 | tf_op jit(solution)/shard_map/ppermute | solution.py:38
  109.6 2.1 %collective-permute-done.15 = bf16[96,384]{1,0:T(8,128)(2,1)S(1)} collective-permute-done((bf16[96,384]{1,0:T(8,128)(2,1)S(1)}, bf16[96,384]{1,0:T(8,128)(2,1)S(1)}, u32[]{:S(2)}, u32[]{:S(2)}) %collective-permute-start.15) | collective-permute-done | bytes 73760 | tf_op jit(solution)/shard_map/ppermute | solution.py:38
  111.7 1.2 collective-permute-done.16
  113.0 2.2 %collective-permute-done.17 = bf16[96,384]{1,0:T(8,128)(2,1)S(1)} collective-permute-done((bf16[96,384]{1,0:T(8,128)(2,1)S(1)}, bf16[96,384]{1,0:T(8,128)(2,1)S(1)}, u32[]{:S(2)}, u32[]{:S(2)}) %collective-permute-start.17) | collective-permute-done | bytes 73760 | tf_op jit(solution)/shard_map/ppermute | solution.py:38
  115.2 0.1 dynamic-slice_convert_fusion.5
  115.3 3.8 %collective-permute-start.18 = (bf16[96,96]{1,0:T(8,128)(2,1)S(1)}, bf16[96,96]{1,0:T(8,128)(2,1)S(1)}, u32[]{:S(2)}, u32[]{:S(2)}) collective-permute-start(bf16[96,96]{1,0:T(8,128)(2,1)S(1)} %get-tuple-element.34), channel_id=1, source_target_pairs={{0,16},{16,32},{32,48},{48,0},{64,80},{80,96},{96,112},{112,64},{1... | collective-permute-start | bytes 55304 | tf_op jit(solution)/shard_map/ppermute | solution.py:42
  119.1 1.5 %collective-permute-start.19 = (bf16[96,96]{1,0:T(8,128)(2,1)S(1)}, bf16[96,96]{1,0:T(8,128)(2,1)S(1)}, u32[]{:S(2)}, u32[]{:S(2)}) collective-permute-start(bf16[96,96]{1,0:T(8,128)(2,1)S(1)} %get-tuple-element.36), channel_id=1, source_target_pairs={{0,32},{16,48},{32,0},{48,16},{64,96},{80,112},{96,64},{112,80},{1... | collective-permute-start | bytes 55304 | tf_op jit(solution)/shard_map/ppermute | solution.py:42
  120.6 1.9 %collective-permute-start.20 = (bf16[96,96]{1,0:T(8,128)(2,1)S(1)}, bf16[96,96]{1,0:T(8,128)(2,1)S(1)}, u32[]{:S(2)}, u32[]{:S(2)}) collective-permute-start(bf16[96,96]{1,0:T(8,128)(2,1)S(1)} %get-tuple-element.35), channel_id=1, source_target_pairs={{0,48},{16,0},{32,16},{48,32},{64,112},{80,64},{96,80},{112,96},{1... | collective-permute-start | bytes 55304 | tf_op jit(solution)/shard_map/ppermute | solution.py:42
  122.4 0.6 slice_multiply_fusion.1
  123.0 0.6 div.55
  123.7 0.1 collective-permute-done.19
  123.8 0.6 collective-permute-done.20
  124.4 0.7 add_multiply_fusion
  (38 shorter events, 0.3 us)
Async XLA Ops:
  1.5 17.4 %collective-permute-start = (bf16[16,1536]{1,0:T(8,128)(2,1)S(1)}, bf16[16,1536]{1,0:T(8,128)(2,1)S(1)}, u32[]{:S(2)}, u32[]{:S(2)}) collective-permute-start(bf16[16,1536]{1,0:T(8,128)(2,1)S(1)} %get-tuple-element.25), channel_id=1, source_target_pairs={{0,1},{1,2},{2,3},{3,4},{4,5},{5,6},{6,7},{7,8},{8,9},{9,10},{10,1... | collective-permute-start | bytes 147464 | tf_op jit(solution)/shard_map/ppermute | solution.py:46
  3.2 15.6 %collective-permute-start.1 = (bf16[16,1536]{1,0:T(8,128)(2,1)S(1)}, bf16[16,1536]{1,0:T(8,128)(2,1)S(1)}, u32[]{:S(2)}, u32[]{:S(2)}) collective-permute-start(bf16[16,1536]{1,0:T(8,128)(2,1)S(1)} %get-tuple-element.24), channel_id=1, source_target_pairs={{1,0},{2,1},{3,2},{4,3},{5,4},{6,5},{7,6},{8,7},{9,8},{10,9},{11,1... | collective-permute-start | bytes 147464 | tf_op jit(solution)/shard_map/ppermute | solution.py:47
  5.2 4.2 %copy-start.3 = (f32[1536]{0:T(1024)S(1)}, f32[1536]{0:T(1024)}, u32[]{:S(2)}) copy-start(f32[1536]{0:T(1024)} %param.11) | copy-start | bytes 18436
  5.2 4.2 %copy-start = (bf16[1,256,1536]{2,1,0:T(8,128)(2,1)S(1)}, bf16[1,256,1536]{2,1,0:T(8,128)(2,1)}, u32[]{:S(2)}) copy-start(bf16[1,256,1536]{2,1,0:T(8,128)(2,1)} %param.6) | copy-start | bytes 2359300
  5.2 4.2 %copy-start.1 = (f32[32,1536]{1,0:T(8,128)S(1)}, f32[32,1536]{1,0:T(8,128)}, u32[]{:S(2)}) copy-start(f32[32,1536]{1,0:T(8,128)} %taps.5) | copy-start | bytes 589828
  21.1 27.5 %collective-permute-start.4 = (bf16[256,1536]{1,0:T(8,128)(2,1)S(1)}, bf16[256,1536]{1,0:T(8,128)(2,1)}, u32[]{:S(2)}, u32[]{:S(2)}) collective-permute-start(bf16[256,1536]{1,0:T(8,128)(2,1)S(1)} %get-tuple-element.13), channel_id=1, source_target_pairs={{0,1},{1,0},{2,3},{3,2},{4,5},{5,4},{6,7},{7,6},{8,9},{9,8},{10,11... | collective-permute-start | bytes 2359304 | tf_op jit(solution)/shard_map/ppermute | solution.py:34
  31.2 18.6 %collective-permute-start.5 = (bf16[256,768]{1,0:T(8,128)(2,1)}, bf16[256,768]{1,0:T(8,128)(2,1)}, u32[]{:S(2)}, u32[]{:S(2)}) collective-permute-start(bf16[256,768]{1,0:T(8,128)(2,1)} %get-tuple-element.21), channel_id=1, source_target_pairs={{0,1},{1,0},{2,3},{3,2},{4,5},{5,4},{6,7},{7,6},{8,9},{9,8},{10,11... | collective-permute-start | bytes 1179656 | tf_op jit(solution)/shard_map/ppermute | solution.py:34
  38.5 21.5 %all-to-all-start = ((f32[16,1,3168]{2,1,0:T(1,128)}), f32[16,1,3168]{2,1,0:T(1,128)S(1)}, u32[]{:S(2)}, u32[]{:S(2)}) async-start(f32[16,1,3168]{2,1,0:T(1,128)} %all_to_all.16), calls=%async_computation | async-start | bytes 409600 | tf_op jit(solution)/shard_map/all_to_all | solution.py:317
  49.8 2.6 %copy-start.2 = (bf16[512,1536]{1,0:T(8,128)(2,1)}, bf16[512,1536]{1,0:T(8,128)(2,1)S(1)}, u32[]{:S(2)}) copy-start(bf16[512,1536]{1,0:T(8,128)(2,1)S(1)} %constant_dynamic-update-slice_fusion.2) | copy-start | bytes 4718596
  52.4 14.7 %collective-permute-start.10 = (bf16[384,384]{1,0:T(8,128)(2,1)S(1)}, bf16[384,384]{1,0:T(8,128)(2,1)}, u32[]{:S(2)}, u32[]{:S(2)}) collective-permute-start(bf16[384,384]{1,0:T(8,128)(2,1)S(1)} %get-tuple-element.33), channel_id=1, source_target_pairs={{0,12},{1,13},{2,14},{3,15},{4,0},{5,1},{6,2},{7,3},{8,4},{9,5},{1... | collective-permute-start | bytes 884744 | tf_op jit(solution)/shard_map/ppermute | solution.py:26
  56.2 38.3 %collective-permute-start.2 = (bf16[16,1536]{1,0:T(8,128)(2,1)}, bf16[16,1536]{1,0:T(8,128)(2,1)S(1)}, u32[]{:S(2)}, u32[]{:S(2)}) collective-permute-start(bf16[16,1536]{1,0:T(8,128)(2,1)} %get-tuple-element.22), channel_id=1, source_target_pairs={{0,1},{1,2},{2,3},{3,4},{4,5},{5,6},{6,7},{7,8},{8,9},{9,10},{10,1... | collective-permute-start | bytes 147464 | tf_op jit(solution)/shard_map/ppermute | solution.py:46
  62.7 22.1 %collective-permute-start.6 = (bf16[384,384]{1,0:T(8,128)(2,1)}, bf16[384,384]{1,0:T(8,128)(2,1)S(1)}, u32[]{:S(2)}, u32[]{:S(2)}) collective-permute-start(bf16[384,384]{1,0:T(8,128)(2,1)} %slice.118), channel_id=1, source_target_pairs={{0,12},{1,13},{2,14},{3,15},{4,0},{5,1},{6,2},{7,3},{8,4},{9,5},{1... | collective-permute-start | bytes 884744 | tf_op jit(solution)/shard_map/ppermute | solution.py:26
  63.5 8.9 %collective-permute-start.7 = (bf16[384,384]{1,0:T(8,128)(2,1)}, bf16[384,384]{1,0:T(8,128)(2,1)S(1)}, u32[]{:S(2)}, u32[]{:S(2)}) collective-permute-start(bf16[384,384]{1,0:T(8,128)(2,1)} %get-tuple-element.32), channel_id=1, source_target_pairs={{0,4},{1,5},{2,6},{3,7},{4,8},{5,9},{6,10},{7,11},{8,12},{9,13},{1... | collective-permute-start | bytes 884744 | tf_op jit(solution)/shard_map/ppermute | solution.py:26
  67.1 19.0 %collective-permute-start.9 = (bf16[384,384]{1,0:T(8,128)(2,1)}, bf16[384,384]{1,0:T(8,128)(2,1)S(1)}, u32[]{:S(2)}, u32[]{:S(2)}) collective-permute-start(bf16[384,384]{1,0:T(8,128)(2,1)} %slice.117), channel_id=1, source_target_pairs={{0,4},{1,5},{2,6},{3,7},{4,8},{5,9},{6,10},{7,11},{8,12},{9,13},{1... | collective-permute-start | bytes 884744 | tf_op jit(solution)/shard_map/ppermute | solution.py:26
  68.9 17.2 %collective-permute-start.11 = (bf16[384,384]{1,0:T(8,128)(2,1)}, bf16[384,384]{1,0:T(8,128)(2,1)S(1)}, u32[]{:S(2)}, u32[]{:S(2)}) collective-permute-start(bf16[384,384]{1,0:T(8,128)(2,1)} %fusion.3), channel_id=1, source_target_pairs={{0,12},{1,13},{2,14},{3,15},{4,0},{5,1},{6,2},{7,3},{8,4},{9,5},{1... | collective-permute-start | bytes 884744 | tf_op jit(solution)/shard_map/ppermute | solution.py:26
  72.5 13.6 %collective-permute-start.8 = (bf16[384,384]{1,0:T(8,128)(2,1)S(1)}, bf16[384,384]{1,0:T(8,128)(2,1)}, u32[]{:S(2)}, u32[]{:S(2)}) collective-permute-start(bf16[384,384]{1,0:T(8,128)(2,1)S(1)} %fusion.5), channel_id=1, source_target_pairs={{0,4},{1,5},{2,6},{3,7},{4,8},{5,9},{6,10},{7,11},{8,12},{9,13},{1... | collective-permute-start | bytes 884744 | tf_op jit(solution)/shard_map/ppermute | solution.py:26
  73.2 27.7 %all-to-all-start.1 = ((f32[16,1,288]{2,1,0:T(1,128)}), f32[16,1,288]{2,1,0:T(1,128)S(1)}, u32[]{:S(2)}, u32[]{:S(2)}) async-start(f32[16,1,288]{2,1,0:T(1,128)} %all_to_all.14), calls=%async_computation.1 | async-start | bytes 49152 | tf_op jit(solution)/shard_map/all_to_all | solution.py:322
  84.8 9.7 %collective-permute-start.3 = (bf16[16,1536]{1,0:T(8,128)(2,1)}, bf16[16,1536]{1,0:T(8,128)(2,1)S(1)}, u32[]{:S(2)}, u32[]{:S(2)}) collective-permute-start(bf16[16,1536]{1,0:T(8,128)(2,1)} %get-tuple-element.23), channel_id=1, source_target_pairs={{1,0},{2,1},{3,2},{4,3},{5,4},{6,5},{7,6},{8,7},{9,8},{10,9},{11,1... | collective-permute-start | bytes 147464 | tf_op jit(solution)/shard_map/ppermute | solution.py:47
  87.4 13.7 %collective-permute-start.12 = (bf16[96,768]{1,0:T(8,128)(2,1)S(1)}, bf16[96,768]{1,0:T(8,128)(2,1)S(1)}, u32[]{:S(2)}, u32[]{:S(2)}) collective-permute-start(bf16[96,768]{1,0:T(8,128)(2,1)S(1)} %get-tuple-element.29), channel_id=1, source_target_pairs={{0,2},{1,3},{2,0},{3,1},{4,6},{5,7},{6,4},{7,5},{8,10},{9,11},{10,... | collective-permute-start | bytes 442376 | tf_op jit(solution)/shard_map/ppermute | solution.py:30
  94.3 6.8 %collective-permute-start.13 = (bf16[96,768]{1,0:T(8,128)(2,1)S(1)}, bf16[96,768]{1,0:T(8,128)(2,1)S(1)}, u32[]{:S(2)}, u32[]{:S(2)}) collective-permute-start(bf16[96,768]{1,0:T(8,128)(2,1)S(1)} %get-tuple-element.31), channel_id=1, source_target_pairs={{0,1},{1,0},{2,3},{3,2},{4,5},{5,4},{6,7},{7,6},{8,9},{9,8},{10,11... | collective-permute-start | bytes 442376 | tf_op jit(solution)/shard_map/ppermute | solution.py:34
  94.3 12.1 %collective-permute-start.14 = (bf16[96,768]{1,0:T(8,128)(2,1)S(1)}, bf16[96,768]{1,0:T(8,128)(2,1)S(1)}, u32[]{:S(2)}, u32[]{:S(2)}) collective-permute-start(bf16[96,768]{1,0:T(8,128)(2,1)S(1)} %get-tuple-element.30), channel_id=1, source_target_pairs={{0,3},{1,2},{2,1},{3,0},{4,7},{5,6},{6,5},{7,4},{8,11},{9,10},{10,... | collective-permute-start | bytes 442376 | tf_op jit(solution)/shard_map/ppermute | solution.py:292
  106.6 5.2 %collective-permute-start.15 = (bf16[96,384]{1,0:T(8,128)(2,1)S(1)}, bf16[96,384]{1,0:T(8,128)(2,1)S(1)}, u32[]{:S(2)}, u32[]{:S(2)}) collective-permute-start(bf16[96,384]{1,0:T(8,128)(2,1)S(1)} %get-tuple-element.26), channel_id=1, source_target_pairs={{0,64},{16,80},{32,96},{48,112},{64,128},{80,144},{96,160},{112,17... | collective-permute-start | bytes 221192 | tf_op jit(solution)/shard_map/ppermute | solution.py:38
  107.1 5.9 %collective-permute-start.16 = (bf16[96,384]{1,0:T(8,128)(2,1)S(1)}, bf16[96,384]{1,0:T(8,128)(2,1)S(1)}, u32[]{:S(2)}, u32[]{:S(2)}) collective-permute-start(bf16[96,384]{1,0:T(8,128)(2,1)S(1)} %get-tuple-element.28), channel_id=1, source_target_pairs={{0,128},{16,144},{32,160},{48,176},{64,192},{80,208},{96,224},{112... | collective-permute-start | bytes 221192 | tf_op jit(solution)/shard_map/ppermute | solution.py:38
  109.6 5.6 %collective-permute-start.17 = (bf16[96,384]{1,0:T(8,128)(2,1)S(1)}, bf16[96,384]{1,0:T(8,128)(2,1)S(1)}, u32[]{:S(2)}, u32[]{:S(2)}) collective-permute-start(bf16[96,384]{1,0:T(8,128)(2,1)S(1)} %get-tuple-element.27), channel_id=1, source_target_pairs={{0,192},{16,208},{32,224},{48,240},{64,0},{80,16},{96,32},{112,48}... | collective-permute-start | bytes 221192 | tf_op jit(solution)/shard_map/ppermute | solution.py:38
  115.3 8.3 %collective-permute-start.18 = (bf16[96,96]{1,0:T(8,128)(2,1)S(1)}, bf16[96,96]{1,0:T(8,128)(2,1)S(1)}, u32[]{:S(2)}, u32[]{:S(2)}) collective-permute-start(bf16[96,96]{1,0:T(8,128)(2,1)S(1)} %get-tuple-element.34), channel_id=1, source_target_pairs={{0,16},{16,32},{32,48},{48,0},{64,80},{80,96},{96,112},{112,64},{1... | collective-permute-start | bytes 55304 | tf_op jit(solution)/shard_map/ppermute | solution.py:42
  119.1 4.7 %collective-permute-start.19 = (bf16[96,96]{1,0:T(8,128)(2,1)S(1)}, bf16[96,96]{1,0:T(8,128)(2,1)S(1)}, u32[]{:S(2)}, u32[]{:S(2)}) collective-permute-start(bf16[96,96]{1,0:T(8,128)(2,1)S(1)} %get-tuple-element.36), channel_id=1, source_target_pairs={{0,32},{16,48},{32,0},{48,16},{64,96},{80,112},{96,64},{112,80},{1... | collective-permute-start | bytes 55304 | tf_op jit(solution)/shard_map/ppermute | solution.py:42
  120.6 3.8 %collective-permute-start.20 = (bf16[96,96]{1,0:T(8,128)(2,1)S(1)}, bf16[96,96]{1,0:T(8,128)(2,1)S(1)}, u32[]{:S(2)}, u32[]{:S(2)}) collective-permute-start(bf16[96,96]{1,0:T(8,128)(2,1)S(1)} %get-tuple-element.35), channel_id=1, source_target_pairs={{0,48},{16,0},{32,16},{48,32},{64,112},{80,64},{96,80},{112,96},{1... | collective-permute-start | bytes 55304 | tf_op jit(solution)/shard_map/ppermute | solution.py:42

commit v3 on v2

v3 whole, which is shorter than its diff:
```python
import jax
import jax.numpy as jnp
from jax import lax
from jax.experimental import pallas as pl
from jax.experimental.pallas import tpu as pltpu
from jax.sharding import PartitionSpec as P

KW = 32
HALF = KW // 2
WIDTH = 1536
ROWS = 256
INNER = ROWS - 2 * HALF
LANES = 128
QUARTER = WIDTH // 4
BLOCK = WIDTH // 16
EXTRA = 16
BF16, F32 = jnp.bfloat16, jnp.float32
SEQ = [(y, z, c) for y in range(4) for z in range(2) for c in range(2)]
DP = [(x, z) for x in range(4) for z in range(4)]
VMEM = pl.BlockSpec(memory_space=pltpu.VMEM)
SMEM = pl.BlockSpec(memory_space=pltpu.SMEM)
ANY = pl.BlockSpec(memory_space=pl.ANY)
LIMIT = pltpu.CompilerParams(vmem_limit_bytes=32 << 20)


def seq_at(y, z, c):
    return ((y % 4) * 2 + z % 2) * 2 + c % 2


def move_y(value, step):
    return lax.ppermute(value, "seq", [(seq_at(*p), seq_at(p[0] + step, p[1], p[2])) for p in SEQ])


def move_z_hi(value):
    return lax.ppermute(value, "seq", [(seq_at(*p), seq_at(p[0], p[1] + 1, p[2])) for p in SEQ])


def move_core(value):
    return lax.ppermute(value, "seq", [(seq_at(*p), seq_at(p[0], p[1], p[2] + 1)) for p in SEQ])


def move_x(value, step):
    return lax.ppermute(value, "dp", [(x * 4 + z, ((x + step) % 4) * 4 + z) for x, z in DP])


def move_z_lo(value, step):
    return lax.ppermute(value, "dp", [(x * 4 + z, x * 4 + (z + step) % 4) for x, z in DP])


def move_neighbour(value):
    return lax.ppermute(value, "seq", [(i, (i + 1) % 16 if i % 2 else (i - 1) % 16) for i in range(16)])


def masked_rows(rows, first, length):
    position = first + lax.broadcasted_iota(jnp.int32, rows.shape, 0)
    return jnp.where((position >= 0) & (position < length), rows.astype(F32), 0.0)


def low_rows(core, chips, beside, begin, count):
    rows = pl.ds(begin, count)
    return jnp.where(core == 0, chips[rows, :].astype(F32), beside[rows, :].astype(F32))


def high_rows(core, chips, beside, begin, count):
    rows = pl.ds(begin, count)
    return jnp.where(core == 0, beside[rows, :].astype(F32), chips[rows, :].astype(F32))


def rows_of(shape, dtype):
    return jax.ShapeDtypeStruct(shape, dtype)


def rows_of(shape, dtype):
    return jax.ShapeDtypeStruct(shape, dtype)


def depthwise(x_ref, taps_ref, out_ref, rows, chunk, finish=None, taps=None, keep=None):
    taps = {j: j for j in range(KW)} if taps is None else taps

    def lane_block(i, carry):
        lanes = pl.ds(pl.multiple_of(i * LANES, LANES), LANES)
        for place, begin in enumerate(range(0, rows, chunk) if keep is None else keep):
            x = x_ref[pl.ds(begin, chunk + KW), lanes]
            total = None
            for shift in range(8):
                span = chunk if shift == 0 else chunk + 8
                sum_ = None
                for j in range(shift, KW + 1, 8):
                    if j in taps:
                        term = taps_ref[pl.ds(taps[j], 1), lanes] * x[j - shift : j - shift + span]
                        sum_ = term if sum_ is None else sum_ + term
                if shift:
                    sum_ = pltpu.roll(sum_, span - shift, 0)[:chunk]
                total = sum_ if total is None else total + sum_
            if finish is not None:
                total = finish(total, begin)
            out_ref[pl.ds(place * chunk, chunk), lanes] = total
        return carry

    lax.fori_loop(0, WIDTH // LANES, lane_block, 0)


LANE_BLOCKS = [pl.ds(i * LANES, LANES) for i in range(WIDTH // LANES)]


def row_sum(terms):
    total = None
    for term in terms:
        total = term if total is None else total + term
    return jnp.sum(total, axis=1, keepdims=True)


def standardise(conv, taps, refs, begin, size, offset, first, length):
    hidden, standard, inverse = refs
    rows, out = pl.ds(begin, size), pl.ds(offset, size)
    mean = row_sum(conv[rows, lanes] for lanes in LANE_BLOCKS) * (1.0 / WIDTH)
    variance = row_sum(jnp.square(conv[rows, lanes] - mean) for lanes in LANE_BLOCKS) * (1.0 / WIDTH)
    scale = lax.rsqrt(variance + 1e-05)
    valid = first + lax.broadcasted_iota(jnp.int32, (size, 1), 0) < length
    for lanes in LANE_BLOCKS:
        value = (conv[rows, lanes] - mean) * scale
        standard[out, lanes] = value
        if hidden is not None:
            normal = value * taps[pl.ds(KW, 1), lanes]
            value = normal * (0.5 + 0.5 * jnp.tanh(0.5 * normal))
            hidden[out, lanes] = jnp.where(valid, value, 0.0).astype(BF16)
    inverse[out, :] = jnp.broadcast_to(scale, (size, LANES))


def inner_kernel(where, frames, taps, hidden, standard, inverse, x, conv):
    first, length = where[0], where[1]
    x[...] = masked_rows(frames[...], first, length)
    depthwise(x, taps, conv, INNER, 112)
    for begin in range(0, INNER, 112):
        refs = (hidden, standard, inverse)
        standardise(conv, taps, refs, begin, 112, 2 * HALF + begin, first + HALF + begin, length)


def edge_kernel(where, top, bottom, chips, beside, taps, _, __, ___, hidden, standard, inverse, x, conv, h, s, i):
    first, length, core = where[0], where[1], where[2]
    end = first + ROWS

    @pl.when(pl.program_id(0) == 0)
    def _both():
        x[pl.ds(0, HALF), :] = masked_rows(low_rows(core, chips, beside, HALF, HALF), first - HALF, length)
        x[pl.ds(HALF, 2 * HALF), :] = masked_rows(top[...], first, length)
        x[pl.ds(3 * HALF, 2 * HALF), :] = masked_rows(bottom[...], end - 2 * HALF, length)
        x[pl.ds(5 * HALF, HALF), :] = masked_rows(high_rows(core, chips, beside, 0, HALF), end, length)
        depthwise(x, taps, conv, 4 * HALF, HALF, keep=(0, 3 * HALF))
        standardise(conv, taps, (h, s, i), 0, HALF, 0, first, length)
        standardise(conv, taps, (h, s, i), HALF, HALF, HALF, end - HALF, length)

    rows = pl.ds(pl.multiple_of(pl.program_id(0) * HALF, HALF), HALF)
    hidden[...] = h[rows, :]
    standard[...] = s[rows, :]
    inverse[...] = i[rows, :]


def outer_kernel(where, top, bottom, chips, beside, taps, _, __, standard, inverse, x, conv, s, i):
    first, length, core = where[0], where[1], where[2]
    end = first + ROWS

    @pl.when(pl.program_id(0) == 0)
    def _both():
        x[pl.ds(0, 2 * HALF), :] = masked_rows(low_rows(core, chips, beside, 0, 2 * HALF), first - 2 * HALF, length)
        x[pl.ds(2 * HALF, HALF), :] = masked_rows(top[...], first, length)
        x[pl.ds(3 * HALF, HALF), :] = masked_rows(bottom[...], end - HALF, length)
        x[pl.ds(4 * HALF, 2 * HALF), :] = masked_rows(high_rows(core, chips, beside, 0, 2 * HALF), end, length)
        depthwise(x, taps, conv, 4 * HALF, HALF, keep=(0, 3 * HALF))
        standardise(conv, taps, (None, s, i), 0, 2 * HALF, 0, first, length)

    rows = pl.ds(pl.multiple_of(pl.program_id(0) * HALF, HALF), HALF)
    standard[...] = s[rows, :]
    inverse[...] = i[rows, :]


SPAN = ROWS + 2 * HALF
FORWARD = (rows_of((SPAN, WIDTH), BF16), rows_of((SPAN, WIDTH), F32), rows_of((SPAN, LANES), F32))


def forward_inner(where, frames, taps):
    return pl.pallas_call(
        inner_kernel,
        out_shape=FORWARD,
        in_specs=[SMEM, VMEM, VMEM],
        out_specs=(VMEM, VMEM, VMEM),
        scratch_shapes=[pltpu.VMEM((ROWS, WIDTH), F32), pltpu.VMEM((INNER, WIDTH), F32)],
        compiler_params=LIMIT,
        cost_estimate=pl.CostEstimate(flops=60_000_000, bytes_accessed=4_000_000, transcendentals=800_000),
        name="forward_inner",
    )(where, frames, taps)


def fixed(shape, row=0):
    return pl.BlockSpec(shape, lambda i: (row, 0))


SIDE = fixed((3 * HALF, WIDTH))
SCRATCH = [pltpu.VMEM((6 * HALF, WIDTH), F32), pltpu.VMEM((2 * HALF, WIDTH), F32)]
KEPT = [pltpu.VMEM((2 * HALF, WIDTH), BF16), pltpu.VMEM((2 * HALF, WIDTH), F32), pltpu.VMEM((2 * HALF, LANES), F32)]


def forward_edge(where, frames, chips, beside, taps, forward):
    def ends(i):
        return (1 + 15 * i, 0)

    return pl.pallas_call(
        edge_kernel,
        grid=(2,),
        out_shape=FORWARD,
        in_specs=[
            SMEM,
            fixed((2 * HALF, WIDTH)),
            fixed((2 * HALF, WIDTH), 7),
            SIDE,
            SIDE,
            fixed((KW + 1, WIDTH)),
            ANY,
            ANY,
            ANY,
        ],
        out_specs=(
            pl.BlockSpec((HALF, WIDTH), ends),
            pl.BlockSpec((HALF, WIDTH), ends),
            pl.BlockSpec((HALF, LANES), ends),
        ),
        scratch_shapes=SCRATCH + KEPT,
        input_output_aliases={6: 0, 7: 1, 8: 2},
        compiler_params=LIMIT,
        cost_estimate=pl.CostEstimate(flops=8_000_000, bytes_accessed=1_000_000, transcendentals=100_000),
        name="forward_edge",
    )(where, frames, frames, chips, beside, taps, *forward)


def forward_outer(where, frames, chips, beside, taps, standard, inverse):
    def ends(i):
        return (17 * i, 0)

    return pl.pallas_call(
        outer_kernel,
        grid=(2,),
        out_shape=FORWARD[1:],
        in_specs=[
            SMEM,
            fixed((HALF, WIDTH)),
            fixed((HALF, WIDTH), 15),
            SIDE,
            SIDE,
            fixed((KW + 1, WIDTH)),
            ANY,
            ANY,
        ],
        out_specs=(pl.BlockSpec((HALF, WIDTH), ends), pl.BlockSpec((HALF, LANES), ends)),
        scratch_shapes=SCRATCH + KEPT[1:],
        input_output_aliases={6: 0, 7: 1},
        compiler_params=LIMIT,
        cost_estimate=pl.CostEstimate(flops=8_000_000, bytes_accessed=1_000_000, transcendentals=0),
        name="forward_outer",
    )(where, frames, frames, chips, beside, taps, standard, inverse)


def backward_rows(where, upstream, row, size, standard, inverse, taps, conv_grad, scaled):
    rows, held = pl.ds(row, size), pl.ds(0, size)
    position = where[0] - HALF + row + lax.broadcasted_iota(jnp.int32, (size, 1), 0)
    valid = (position >= 0) & (position < where[1])
    means, slopes, terms = None, None, []
    for lanes in LANE_BLOCKS:
        value = standard[rows, lanes]
        gain = taps[pl.ds(KW, 1), lanes]
        normal = value * gain
        sigma = 0.5 + 0.5 * jnp.tanh(0.5 * normal)
        grad = jnp.where(valid, upstream[rows, lanes] * (sigma + normal * sigma * (1.0 - sigma)), 0.0)
        terms.append(jnp.sum((grad * value).reshape(size // 8, 8, LANES), axis=0))
        grad = grad * gain
        scaled[held, lanes] = grad
        slope = grad * value
        means = grad if means is None else means + grad
        slopes = slope if slopes is None else slopes + slope
    mean = jnp.sum(means, axis=1, keepdims=True) * (1.0 / WIDTH)
    slope = jnp.sum(slopes, axis=1, keepdims=True) * (1.0 / WIDTH)
    scale = inverse[rows, :1]
    for lanes in LANE_BLOCKS:
        value = scaled[held, lanes] - mean - standard[rows, lanes] * slope
        conv_grad[rows, lanes] = (scale * value).astype(BF16)
    return terms


def backward_kernel(where, upstream, standard, inverse, taps, _, conv_grad, gain_sum, scaled):
    rest = (standard, inverse, taps, conv_grad, scaled)
    backward_rows(where, upstream, 0, HALF, *rest)
    backward_rows(where, upstream, HALF + ROWS, HALF, *rest)
    first = backward_rows(where, upstream, HALF, ROWS // 2, *rest)
    second = backward_rows(where, upstream, HALF + ROWS // 2, ROWS // 2, *rest)
    for lanes, one, two in zip(LANE_BLOCKS, first, second):
        gain_sum[:, lanes] = one + two


def backward(where, upstream, standard, inverse, taps, after):
    return pl.pallas_call(
        backward_kernel,
        out_shape=(rows_of((SPAN, WIDTH), BF16), rows_of((8, WIDTH), F32)),
        in_specs=[SMEM, VMEM, VMEM, VMEM, VMEM, ANY],
        out_specs=(VMEM, VMEM),
        scratch_shapes=[pltpu.VMEM((ROWS // 2, WIDTH), F32)],
        compiler_params=LIMIT,
        cost_estimate=pl.CostEstimate(flops=10_000_000, bytes_accessed=4_000_000, transcendentals=400_000),
        name="backward",
    )(where, upstream, standard, inverse, taps, after)


def kernel_grad_kernel(where, frames, chips, beside, conv_grad, gain_rows, _, keep, one, two, three, x, g, all_):
    first, length, core = where[0], where[1], where[2]
    x[pl.ds(0, HALF), :] = masked_rows(low_rows(core, chips, beside, HALF, HALF), first - HALF, length)
    x[pl.ds(HALF, ROWS), :] = masked_rows(frames[...], first, length)
    x[pl.ds(HALF + ROWS, HALF), :] = masked_rows(high_rows(core, chips, beside, 0, HALF), first + ROWS, length)
    g[pl.ds(0, 8), :] = jnp.zeros((8, WIDTH), F32)
    g[pl.ds(8, ROWS), :] = conv_grad[pl.ds(HALF, ROWS), :].astype(F32)
    g[pl.ds(8 + ROWS, 8), :] = jnp.zeros((8, WIDTH), F32)
    chunk = 88

    def lane_block(i, carry):
        lanes = pl.ds(pl.multiple_of(i * LANES, LANES), LANES)
        sums = [None] * KW
        for begin in range(0, ROWS + 8, chunk):
            x_rows = x[pl.ds(begin, chunk + KW - 8), lanes]
            grad = g[pl.ds(begin, chunk + 8), lanes]
            for shift in range(8):
                moved = grad[8:] if shift == 0 else pltpu.roll(grad, shift, 0)[8:]
                for a in range(KW // 8):
                    j = 8 * a + shift
                    product = (moved * x_rows[8 * a : 8 * a + chunk]).reshape(chunk // 8, 8, LANES)
                    product = jnp.sum(product, axis=0)
                    sums[j] = product if sums[j] is None else sums[j] + product
        all_[pl.ds(0, KW), lanes] = jnp.concatenate(
            [jnp.sum(value, axis=0, keepdims=True) for value in sums], axis=0
        )
        gain = jnp.sum(gain_rows[:, lanes], axis=0, keepdims=True)
        all_[pl.ds(KW, 8), lanes] = jnp.broadcast_to(gain, (8, LANES))
        return carry

    lax.fori_loop(0, WIDTH // LANES, lane_block, 0)
    for step, out in enumerate((keep, one, two, three)):
        out[...] = all_[:, pl.ds(pl.multiple_of(lax.rem(where[3] + step, 4) * QUARTER, QUARTER), QUARTER)]


def kernel_grads(where, frames, chips, beside, conv_grad, gain_rows, after):
    return pl.pallas_call(
        kernel_grad_kernel,
        out_shape=(rows_of((KW + 8, QUARTER), F32),) * 4,
        in_specs=[SMEM, VMEM, VMEM, VMEM, VMEM, VMEM, ANY],
        out_specs=(VMEM,) * 4,
        scratch_shapes=[
            pltpu.VMEM((ROWS + KW, WIDTH), F32),
            pltpu.VMEM((ROWS + 16, WIDTH), F32),
            pltpu.VMEM((KW + 8, WIDTH), F32),
        ],
        compiler_params=LIMIT,
        cost_estimate=pl.CostEstimate(flops=50_000_000, bytes_accessed=2_000_000, transcendentals=0),
        name="kernel_grads",
    )(where, frames, chips, beside, conv_grad, gain_rows, after)


def input_grad_kernel(where, conv_grad, taps, _, out, token, g):
    token[...] = jnp.zeros(token.shape, F32)
    first, length = where[0], where[1]
    g[...] = conv_grad[...].astype(F32)

    def finish(total, begin):
        return masked_rows(total, first + begin, length).astype(BF16)

    depthwise(g, taps, out, ROWS, 64, finish, {j: KW - j for j in range(1, KW + 1)})


def input_grads(where, conv_grad, taps, after):
    return pl.pallas_call(
        input_grad_kernel,
        out_shape=(rows_of((ROWS, WIDTH), BF16), rows_of((8, LANES), F32)),
        in_specs=[SMEM, VMEM, VMEM, ANY],
        out_specs=(VMEM, VMEM),
        scratch_shapes=[pltpu.VMEM((ROWS + KW, WIDTH), F32)],
        compiler_params=LIMIT,
        cost_estimate=pl.CostEstimate(flops=50_000_000, bytes_accessed=2_000_000, transcendentals=0),
        name="input_grads",
    )(where, conv_grad, taps, after)


def products_kernel(place, hidden, hidden_other, cot, cot_other, _, far_a, far_b, above_a, above_b, below_a, below_b, own):
    y, core = place[0], place[1]
    columns = pl.ds(pl.multiple_of(core * (WIDTH // 2), WIDTH // 2), WIDTH // 2)
    right, right_other = cot[:, columns], cot_other[:, columns]
    own_rows = pl.ds(HALF, ROWS)

    def chunk(step):
        rows = pl.ds(pl.multiple_of(lax.rem(y + step, 4) * QUARTER, QUARTER), QUARTER)
        dims = (((0,), (0,)), ((), ()))
        return lax.dot_general(
            hidden[own_rows, rows], right, dims, preferred_element_type=F32
        ) + lax.dot_general(hidden_other[own_rows, rows], right_other, dims, preferred_element_type=F32)

    for step, (a, b) in ((2, (far_a, far_b)), (1, (above_a, above_b)), (3, (below_a, below_b))):
        value = chunk(step)
        a[...] = value[:, :QUARTER].astype(a.dtype)
        b[...] = value[:, QUARTER:].astype(b.dtype)
    own[...] = chunk(0)


def products(place, hidden, hidden_other, cot, cot_other, after):
    half = (QUARTER, QUARTER)
    return pl.pallas_call(
        products_kernel,
        out_shape=(
            rows_of(half, BF16),
            rows_of(half, BF16),
            rows_of(half, F32),
            rows_of(half, BF16),
            rows_of(half, BF16),
            rows_of(half, F32),
            rows_of((QUARTER, 2 * QUARTER), F32),
        ),
        in_specs=[SMEM, VMEM, VMEM, VMEM, VMEM, ANY],
        out_specs=(VMEM,) * 7,
        compiler_params=LIMIT,
        cost_estimate=pl.CostEstimate(flops=1_200_000_000, bytes_accessed=8_000_000, transcendentals=0),
        name="products",
    )(place, hidden, hidden_other, cot, cot_other, after)


def seconds_kernel(above_a, up_a, below_b, down_b, _, second_a, second_b):
    second_a[...] = (above_a[...] + up_a[...].astype(F32)).astype(BF16)
    second_b[...] = (below_b[...] + down_b[...].astype(F32)).astype(BF16)


def seconds(above_a, up_a, below_b, down_b, after):
    return pl.pallas_call(
        seconds_kernel,
        out_shape=(rows_of((QUARTER, QUARTER), BF16),) * 2,
        in_specs=[VMEM, VMEM, VMEM, VMEM, ANY],
        out_specs=(VMEM,) * 2,
        compiler_params=LIMIT,
        cost_estimate=pl.CostEstimate(flops=300_000, bytes_accessed=2_400_000, transcendentals=0),
        name="seconds",
    )(above_a, up_a, below_b, down_b, after)


def blocks_kernel(
    place, own, down_a, up_a, up_b, down_b, k0, k1, k2, k3, mine, across, beside, diagonal, total, extra
):
    z_hi, core = place[2], place[1]
    total[:, :QUARTER] = own[:, :QUARTER] + (down_a[...].astype(F32) + up_a[...].astype(F32))
    total[:, QUARTER:] = own[:, QUARTER:] + (down_b[...].astype(F32) + up_b[...].astype(F32))
    sums = k0[...] + k1[...] + k2[...] + k3[...]
    extra[...] = jnp.zeros(extra.shape, F32)
    for block in range(4):
        for q in range(5):
            extra[block, pl.ds(0, 8), pl.ds(q * BLOCK, BLOCK)] = sums[
                8 * q : 8 * q + 8, block * BLOCK : (block + 1) * BLOCK
            ]
    for out, z, c in (
        (mine, z_hi, core),
        (across, 1 - z_hi, core),
        (beside, z_hi, 1 - core),
        (diagonal, 1 - z_hi, 1 - core),
    ):
        block = 2 * z + c
        out[pl.ds(0, BLOCK), :] = total[pl.ds(pl.multiple_of(block * BLOCK, BLOCK), BLOCK), :].astype(out.dtype)
        out[pl.ds(BLOCK, EXTRA), :] = extra[block].astype(out.dtype)


def blocks(place, own, down_a, up_a, up_b, down_b, rows):
    shape = (BLOCK + EXTRA, WIDTH // 2)
    return pl.pallas_call(
        blocks_kernel,
        out_shape=(rows_of(shape, F32),) + (rows_of(shape, BF16),) * 3,
        in_specs=[SMEM] + [VMEM] * 9,
        out_specs=(VMEM,) * 4,
        scratch_shapes=[pltpu.VMEM((QUARTER, 2 * QUARTER), F32), pltpu.VMEM((4, EXTRA, WIDTH // 2), F32)],
        compiler_params=LIMIT,
        cost_estimate=pl.CostEstimate(flops=1_000_000, bytes_accessed=4_000_000, transcendentals=0),
        name="blocks",
    )(place, own, down_a, up_a, up_b, down_b, *rows)


def squares_kernel(place, mine, across, beside, diagonal, _, keep, one, two, three, square, extra):
    core, x = place[1], place[3]
    half = WIDTH // 2
    rows, more = pl.ds(0, BLOCK), pl.ds(BLOCK, EXTRA)
    first = mine[rows, :] + across[rows, :].astype(F32)
    second = beside[rows, :].astype(F32) + diagonal[rows, :].astype(F32)
    square[rows, pl.ds(pl.multiple_of(core * half, half), half)] = first * first
    square[rows, pl.ds(pl.multiple_of((1 - core) * half, half), half)] = second * second
    sums = mine[more, :] + across[more, :].astype(F32) + beside[more, :].astype(F32) + diagonal[more, :].astype(F32)
    extra[...] = sums * sums
    square[more, :] = jnp.zeros((EXTRA, WIDTH), F32)
    for dp in range(16):
        columns = pl.ds(dp * BLOCK, BLOCK)
        square[pl.ds(BLOCK, 2), columns] = extra[pl.ds(2 * (dp % 4), 2), pl.ds(dp // 4 * BLOCK, BLOCK)]
        square[pl.ds(BLOCK + 2, 1), columns] = extra[pl.ds(0, 1), pl.ds(4 * BLOCK, BLOCK)]
    for step, out in enumerate((keep, one, two, three)):
        columns = pl.ds(pl.multiple_of(lax.rem(x + step, 4) * QUARTER, QUARTER), QUARTER)
        out[...] = square[:, columns].astype(out.dtype)


def squares(place, mine, across, beside, diagonal, after):
    shape = (BLOCK + EXTRA, QUARTER)
    return pl.pallas_call(
        squares_kernel,
        out_shape=(rows_of(shape, F32),) + (rows_of(shape, BF16),) * 3,
        in_specs=[SMEM] + [VMEM] * 4 + [ANY],
        out_specs=(VMEM,) * 4,
        scratch_shapes=[pltpu.VMEM((BLOCK + EXTRA, WIDTH), F32), pltpu.VMEM((EXTRA, WIDTH // 2), F32)],
        compiler_params=LIMIT,
        cost_estimate=pl.CostEstimate(flops=1_000_000, bytes_accessed=2_000_000, transcendentals=0),
        name="squares",
    )(place, mine, across, beside, diagonal, after)


def quarters_kernel(place, keep, one, two, three, own, out_one, out_two, out_three, parts):
    z_lo = place[4]
    total = keep[...] + one[...].astype(F32) + two[...].astype(F32) + three[...].astype(F32)
    for z in range(4):
        parts[lax.rem(z - z_lo + 4, 4)] = total[:, z * BLOCK : (z + 1) * BLOCK]
    for step, out in enumerate((own, out_one, out_two, out_three)):
        out[...] = parts[step].astype(out.dtype)


def quarters(place, keep, one, two, three):
    shape = (BLOCK + EXTRA, BLOCK)
    return pl.pallas_call(
        quarters_kernel,
        out_shape=(rows_of(shape, F32),) + (rows_of(shape, BF16),) * 3,
        in_specs=[SMEM] + [VMEM] * 4,
        out_specs=(VMEM,) * 4,
        scratch_shapes=[pltpu.VMEM((4,) + shape, F32)],
        compiler_params=LIMIT,
        cost_estimate=pl.CostEstimate(flops=1_000_000, bytes_accessed=1_000_000, transcendentals=0),
        name="quarters",
    )(place, keep, one, two, three)


def means_kernel(own, one, two, three, out, kernel, gain):
    total = own[...] + one[...].astype(F32) + two[...].astype(F32) + three[...].astype(F32)
    total = total * (1.0 / 16)
    out[...] = total[:BLOCK]
    kernel[...] = total[BLOCK : BLOCK + 2]
    gain[...] = total[BLOCK + 2 : BLOCK + 3]


def means(own, one, two, three):
    return pl.pallas_call(
        means_kernel,
        out_shape=(rows_of((BLOCK, BLOCK), F32), rows_of((2, BLOCK), F32), rows_of((1, BLOCK), F32)),
        in_specs=[VMEM] * 4,
        out_specs=(VMEM,) * 3,
        compiler_params=LIMIT,
        cost_estimate=pl.CostEstimate(flops=100_000, bytes_accessed=200_000, transcendentals=0),
        name="means",
    )(own, one, two, three)


def on_device(frames_in, cotangent, lengths, out_weight, conv_kernel, layer_norm_gain):
    seq, dp = lax.axis_index("seq"), lax.axis_index("dp")
    core = seq % 2
    where = jnp.stack([seq * ROWS, lengths[0], core, seq // 4]).astype(jnp.int32)
    place = jnp.stack([seq // 4, core, (seq // 2) % 2, dp // 4, dp % 4]).astype(jnp.int32)
    frames, cot = frames_in[0], cotangent[0]
    taps = jnp.concatenate([conv_kernel, layer_norm_gain[None]], axis=0)
    begin = jnp.concatenate([frames[: 2 * HALF], cot[:HALF]], axis=0)
    end = jnp.concatenate([frames[-2 * HALF :], cot[-HALF:]], axis=0)
    chips = move_neighbour(jnp.where(core == 0, begin, end))
    beside = move_core(jnp.where(core == 0, end, begin))
    cot_other = move_core(cot)
    forward = forward_inner(where, frames, taps)
    hidden, standard, inverse = forward_edge(where, frames, chips, beside, taps, forward)
    hidden_other = move_core(hidden)
    standard, inverse = forward_outer(where, frames, chips, beside, taps, standard, inverse)
    low = jnp.where(core == 0, chips[2 * HALF :], beside[2 * HALF :])
    high = jnp.where(core == 0, beside[2 * HALF :], chips[2 * HALF :])
    late_cot, _ = lax.optimization_barrier((jnp.concatenate([low, cot, high], axis=0), hidden))
    upstream = lax.dot_general(late_cot, out_weight, (((1,), (1,)), ((), ())), preferred_element_type=F32)
    far_a, far_b, above_a, above_b, below_a, below_b, own = products(
        place, hidden, hidden_other, cot, cot_other, upstream
    )
    up_a = move_y(far_a, 1)
    down_b = move_y(far_b, -1)
    up_b = move_y(above_b, 1)
    down_a = move_y(below_a, -1)
    conv_grad, gain_rows = backward(where, upstream, standard, inverse, taps, far_a)
    second_a, second_b = seconds(above_a, up_a, below_b, down_b, conv_grad)
    up_a = move_y(second_a, 1)
    down_b = move_y(second_b, -1)
    rows = kernel_grads(where, frames, chips, beside, conv_grad, gain_rows, second_a)
    rows = [rows[0]] + [move_y(rows[k], k) for k in (1, 2, 3)]
    mine, across, side, diagonal = blocks(place, own, down_a, up_a, up_b, down_b, rows)
    input_grad, token = input_grads(where, conv_grad, taps, across)
    across = move_z_hi(across)
    diagonal = lax.ppermute(
        diagonal, "seq", [(seq_at(*p), seq_at(p[0], p[1] + 1, p[2] + 1)) for p in SEQ]
    )
    side = move_core(side)
    keep, *sent = squares(place, mine, across, side, diagonal, token)
    keep, *sent = quarters(place, keep, *(move_x(value, k + 1) for k, value in enumerate(sent)))
    out, kernel, gain = means(keep, *(move_z_lo(value, k + 1) for k, value in enumerate(sent)))
    return input_grad[None], out, kernel, gain[0]


def solution(mesh):
    return jax.shard_map(
        on_device,
        mesh=mesh,
        in_specs=(P("dp", "seq", None), P("dp", "seq", None), P("dp"), P(), P(), P()),
        out_specs=(P("dp", "seq", None), P("seq", "dp"), P("dp", "seq"), P("seq")),
        check_vma=False,
    )
```

time: 126 us -> 94.1 us (0.75)
  starting transfers between devices: 59.9 us -> 35.7 us
  matrix products: 10.7 us -> 1.56 us
  waiting for transfers between devices: 14.1 us -> 21.9 us
  local copies, waits for them, and re-layouts: 9.74 us -> 4.36 us
  other arithmetic: 4.79 us -> 0.2 us
  Pallas kernels: 24.1 us -> 28.6 us
    all_to_all x2 -> x0, starting transfers between devices: 19.9 us -> none  [the longest x1 10 us: reduce_rows(): rows = lax.all_to_all(rows, 'seq', 0, 0, tiled=True).sum(axis=0)]
    dot_general x5 -> x1, matrix products: 10.7 us -> 1.56 us  [on_device(): lax.dot_general(late_cot, out_weight, (((1,), (1,)), ((), ())), preferred...]
    ppermute x5 -> x2, starting transfers between devices: 6.28 us -> 14 us  [the longest x1 9.17 us: move_neighbour(): lax.ppermute(value, 'seq', [(i, (i + 1) % 16 if i % 2 else (i - 1) % 16)...]
    ppermute x3 -> x4, starting transfers between devices: 8.23 us -> 0.7 us  [move_core(): lax.ppermute(value, 'seq', [(seq_at(*p), seq_at(p[0], p[1], p[2] + 1)) fo...]
    ppermute x6 -> x9, waiting for transfers between devices: 0.33 us -> 7.73 us  [move_y(): lax.ppermute(value, 'seq', [(seq_at(*p), seq_at(p[0] + step, p[1], p[2]))...]
    ppermute x1, waiting for transfers between devices: 0.16 us -> 6.75 us  [move_z_hi(): lax.ppermute(value, 'seq', [(seq_at(*p), seq_at(p[0], p[1] + 1, p[2])) fo...]
    ppermute x1, starting transfers between devices: 6.84 us -> 1.17 us  [move_z_hi(): lax.ppermute(value, 'seq', [(seq_at(*p), seq_at(p[0], p[1] + 1, p[2])) fo...]
    ppermute x5 -> x2, waiting for transfers between devices: 5.3 us -> 0.08 us  [the longest x1 0.08 us: on_device(): lax.ppermute(diagonal, 'seq', [(seq_at(*p), seq_at(p[0], p[1] + 1, p[2] +...]
  transfers between devices with their start and end apart: 23 -> 22, of which waited for: 9 -> 12; matrix products, arithmetic and copies ran while one was open for 17% -> 4% of each run, Pallas kernels for 17% -> 25%
where the time goes in v3:
time: 94.1 us; the launch traced here: 93.9 us
  starting transfers between devices  35.7 us (38%)
  Pallas kernels  28.6 us (30%)
  waiting for transfers between devices  21.9 us (23%)
  local copies, waits for them, and re-layouts  4.36 us (5%)
  between operations  1.57 us (2%)
  matrix products  1.56 us (2%)
    ppermute x9, starting transfers between devices, move_y(): lax.ppermute(value, 'seq', [(seq_at(*p), seq_at(p[0] + step, p[1], p[2]))...  9.86 us
    ppermute x1, starting transfers between devices, move_neighbour(): lax.ppermute(value, 'seq', [(i, (i + 1) % 16 if i % 2 else (i - 1) % 16)...  9.17 us
    ppermute x9, waiting for transfers between devices, move_y(): lax.ppermute(value, 'seq', [(seq_at(*p), seq_at(p[0] + step, p[1], p[2]))...  7.73 us
    ppermute x3, starting transfers between devices, move_z_lo(): lax.ppermute(value, 'dp', [(x * 4 + z, x * 4 + (z + step) % 4) for x, z i...  6.96 us
    ppermute x1, waiting for transfers between devices, move_z_hi(): lax.ppermute(value, 'seq', [(seq_at(*p), seq_at(p[0], p[1] + 1, p[2])) fo...  6.75 us
    pallas_call x1, Pallas kernels, input_grads(): pl.pallas_call(input_grad_kernel, out_shape=(rows_of((ROWS, WIDTH), BF16)...  6.5 us
    pallas_call x1, Pallas kernels, kernel_grads(): pl.pallas_call(kernel_grad_kernel, out_shape=(rows_of((KW + 8, QUARTER),...  6.08 us
    ppermute x3, waiting for transfers between devices, move_x(): lax.ppermute(value, 'dp', [(x * 4 + z, (x + step) % 4 * 4 + z) for x, z i...  5.69 us
  transfers between devices with their start and end apart: 22, of which 12 were waited for; matrix products, arithmetic and copies ran while one was open for 4% of the time, Pallas kernels for 25%

profile of v3, /device:TPU:6, one launch (start us, length us, event | category | flops | bytes accessed | tf_op | source)
XLA Modules:
  0.0 93.9 jit_solution(422977047161003696)
XLA Ops:
  0.6 0.0 copy-start
  0.7 0.9 slice_bitcast_fusion.3
  1.6 1.0 %slice_bitcast_fusion.1 = (bf16[32,1536]{1,0:T(8,128)(2,1)S(1)}, bf16[32,1536]{1,0:T(8,128)(2,1)S(1)}) fusion(bf16[1,256,1536]{2,1,0:T(8,128)(2,1)} %param.6), kind=kLoop, calls=%fused_computation.6 | loop fusion | bytes 393216 | tf_op jit(solution)/shard_map/slice | solution.py:567
  2.5 0.1 broadcast_select_fusion.1
  2.6 9.2 %collective-permute-start = (bf16[48,1536]{1,0:T(8,128)(2,1)S(1)}, bf16[48,1536]{1,0:T(8,128)(2,1)S(1)}, u32[]{:S(2)}, u32[]{:S(2)}) collective-permute-start(bf16[48,1536]{1,0:T(8,128)(2,1)S(1)} %get-tuple-element.92), channel_id=1, source_target_pairs={{0,15},{1,2},{2,1},{3,4},{4,3},{5,6},{6,5},{7,8},{8,7},{9,10},{10,... | collective-permute-start | bytes 442376 | tf_op jit(solution)/shard_map/ppermute | solution.py:51
  11.7 0.0 collective-permute-start.1
  11.7 0.5 collective-permute-start.3
  12.3 0.9 %constant_dynamic-update-slice_fusion = f32[33,1536]{1,0:T(8,128)S(1)} fusion(f32[32,1536]{1,0:T(8,128)} %param.10), kind=kLoop, calls=%fused_computation.11 | loop fusion | bytes 393216
  13.9 0.7 broadcast_in_dim.6
  14.6 0.1 dynamic-update-slice.1.taps
  14.7 0.1 stack.33.place
  14.8 0.1 pad_add_fusion.where
  14.9 5.3 %forward_inner.1 = (bf16[288,1536]{1,0:T(8,128)(2,1)S(1)}, f32[288,1536]{1,0:T(8,128)S(1)}, f32[288,128]{1,0:T(8,128)S(1)}) custom-call(s32[4]{0:T(128)S(1)} %pad_add_fusion.where, bf16[256,1536]{1,0:T(8,128)(2,1)S(1)} %bitcast.20, f32[33,1536]{1,0:T(8,128)S(1)} %dynamic-update-slice.1.taps), custom_call_target="tpu_custom_call" | custom-call | flops 60000000 | bytes 4000000 | tf_op jit(solution)/shard_map/forward_inner/pallas_call | solution.py:182
  20.2 0.0 collective-permute-done.chips
  20.3 0.0 copy-start.1
  20.3 0.0 copy-start.2
  20.3 1.7 %forward_edge.1 = (bf16[288,1536]{1,0:T(8,128)(2,1)S(1)}, f32[288,1536]{1,0:T(8,128)S(1)}, f32[288,128]{1,0:T(8,128)S(1)}) custom-call(s32[4]{0:T(128)S(1)} %pad_add_fusion.where, bf16[256,1536]{1,0:T(8,128)(2,1)S(1)} %bitcast.21, bf16[256,1536]{1,0:T(8,128)(2,1)S(1)} %bitcast.22, ...), custom_call_target="tpu_custom_call", output_to_operand_aliasing={{0}: (6, {}), {1}: (7, {}), {2}: (8, {})} | custom-call | flops 8000000 | bytes 1000000 | tf_op jit(solution)/shard_map/forward_edge/pallas_call | solution.py:207
  22.0 0.1 collective-permute-start.2
  22.1 0.1 pad_maximum_fusion
  22.2 0.6 copy-done.2
  22.8 1.6 %fusion._.upstream = f32[288,1536]{1,0:T(8,128)S(1)} fusion(bf16[288,1536]{1,0:T(8,128)(2,1)S(1)} %pad_maximum_fusion, bf16[1536,1536]{1,0:T(8,128)(2,1)S(1)} %copy-done.2), kind=kOutput, calls=%fused_computation.13 | convolution fusion | flops 1358954496 | bytes 7372800 | tf_op jit(solution)/shard_map/dot_general | solution.py:579
  24.4 0.1 collective-permute-done.2.hidden_other
  24.5 2.0 %products.1 = (bf16[384,384]{1,0:T(8,128)(2,1)S(1)}, bf16[384,384]{1,0:T(8,128)(2,1)S(1)}, f32[384,384]{1,0:T(8,128)S(1)}, bf16[384,384]{1,0:T(8,128)(2,1)S(1)},...) custom-call(s32[5]{0:T(128)S(1)} %stack.33.place, ...), custom_call_target="tpu_custom_call" | custom-call | flops 1200000000 | bytes 8000000 | tf_op jit(solution)/shard_map/products/pallas_call | solution.py:409
  26.5 1.0 %collective-permute-start.6 = (bf16[384,384]{1,0:T(8,128)(2,1)S(1)}, bf16[384,384]{1,0:T(8,128)(2,1)S(1)}, u32[]{:S(2)}, u32[]{:S(2)}) collective-permute-start(bf16[384,384]{1,0:T(8,128)(2,1)S(1)} %get-tuple-element.60), channel_id=1, source_target_pairs={{0,12},{1,13},{2,14},{3,15},{4,0},{5,1},{6,2},{7,3},{8,4},{9,5},{1... | collective-permute-start | bytes 884744 | tf_op jit(solution)/shard_map/ppermute | solution.py:31
  27.5 1.1 %collective-permute-start.5 = (bf16[384,384]{1,0:T(8,128)(2,1)S(1)}, bf16[384,384]{1,0:T(8,128)(2,1)S(1)}, u32[]{:S(2)}, u32[]{:S(2)}) collective-permute-start(bf16[384,384]{1,0:T(8,128)(2,1)S(1)} %get-tuple-element.54._), channel_id=1, source_target_pairs={{0,4},{1,5},{2,6},{3,7},{4,8},{5,9},{6,10},{7,11},{8,12},{9,13},{1... | collective-permute-start | bytes 884744 | tf_op jit(solution)/shard_map/ppermute | solution.py:31
  28.6 2.1 %collective-permute-start.4 = (bf16[384,384]{1,0:T(8,128)(2,1)S(1)}, bf16[384,384]{1,0:T(8,128)(2,1)S(1)}, u32[]{:S(2)}, u32[]{:S(2)}) collective-permute-start(bf16[384,384]{1,0:T(8,128)(2,1)S(1)} %get-tuple-element.57), channel_id=1, source_target_pairs={{0,12},{1,13},{2,14},{3,15},{4,0},{5,1},{6,2},{7,3},{8,4},{9,5},{1... | collective-permute-start | bytes 884744 | tf_op jit(solution)/shard_map/ppermute | solution.py:31
  30.7 0.0 collective-permute-start.8
  30.7 1.7 %forward_outer.1 = (f32[288,1536]{1,0:T(8,128)S(1)}, f32[288,128]{1,0:T(8,128)S(1)}) custom-call(s32[4]{0:T(128)S(1)} %pad_add_fusion.where, bf16[256,1536]{1,0:T(8,128)(2,1)S(1)} %bitcast.23, bf16[256,1536]{1,0:T(8,128)(2,1)S(1)} %bitcast.24, bf16[48,1536]{1,0:T(8,128)(2,1)S(1)} %collective-permute-done.chips, ...), custom_call_target="tpu_custom_call", output_to_operand_aliasing={{0}: (6, {}), {1}: (7, {})} | custom-call | flops 8000000 | bytes 1000000 | tf_op jit(solution)/shard_map/forward_outer/pallas_call | solution.py:239
  32.4 2.1 %backward.1 = (bf16[288,1536]{1,0:T(8,128)(2,1)S(1)}, f32[8,1536]{1,0:T(8,128)S(1)}) custom-call(s32[4]{0:T(128)S(1)} %pad_add_fusion.where, f32[288,1536]{1,0:T(8,128)S(1)} %fusion._.upstream, f32[288,1536]{1,0:T(8,128)S(1)} %get-tuple-element.52.standard, f32[288,128]{1,0:T(8,128)S(1)} %get-tuple-element.53.inverse, ...), custom_call_target="tpu_custom_call" | custom-call | flops 10000000 | bytes 4000000 | tf_op jit(solution)/shard_map/backward/pallas_call | solution.py:299
  34.5 2.0 %collective-permute-done.6.down_b = bf16[384,384]{1,0:T(8,128)(2,1)S(1)} collective-permute-done((bf16[384,384]{1,0:T(8,128)(2,1)S(1)}, bf16[384,384]{1,0:T(8,128)(2,1)S(1)}, u32[]{:S(2)}, u32[]{:S(2)}) %collective-permute-start.6) | collective-permute-done | bytes 294944 | tf_op jit(solution)/shard_map/ppermute | solution.py:31
  36.5 2.1 %collective-permute-done.5.up_a = bf16[384,384]{1,0:T(8,128)(2,1)S(1)} collective-permute-done((bf16[384,384]{1,0:T(8,128)(2,1)S(1)}, bf16[384,384]{1,0:T(8,128)(2,1)S(1)}, u32[]{:S(2)}, u32[]{:S(2)}) %collective-permute-start.5) | collective-permute-done | bytes 294944 | tf_op jit(solution)/shard_map/ppermute | solution.py:31
  38.6 0.1 seconds.1
  38.7 0.3 collective-permute-start.9
  38.9 2.0 %collective-permute-start.7 = (bf16[384,384]{1,0:T(8,128)(2,1)S(1)}, bf16[384,384]{1,0:T(8,128)(2,1)S(1)}, u32[]{:S(2)}, u32[]{:S(2)}) collective-permute-start(bf16[384,384]{1,0:T(8,128)(2,1)S(1)} %get-tuple-element.61._), channel_id=1, source_target_pairs={{0,4},{1,5},{2,6},{3,7},{4,8},{5,9},{6,10},{7,11},{8,12},{9,13},{1... | collective-permute-start | bytes 884744 | tf_op jit(solution)/shard_map/ppermute | solution.py:31
  41.0 6.1 %kernel_grads.1 = (f32[40,384]{1,0:T(8,128)S(1)}, f32[40,384]{1,0:T(8,128)S(1)}, f32[40,384]{1,0:T(8,128)S(1)}, f32[40,384]{1,0:T(8,128)S(1)}) custom-call(s32[4]{0:T(128)S(1)} %pad_add_fusion.where, bf16[256,1536]{1,0:T(8,128)(2,1)S(1)} %bitcast.25, bf16[48,1536]{1,0:T(8,128)(2,1)S(1)} %collective-permute-done.chips, ...), custom_call_target="tpu_custom_call" | custom-call | flops 50000000 | bytes 2000000 | tf_op jit(solution)/shard_map/kernel_grads/pallas_call | solution.py:347
  47.0 0.1 collective-permute-start.10
  47.1 2.7 %collective-permute-start.11 = (f32[40,384]{1,0:T(8,128)S(1)}, f32[40,384]{1,0:T(8,128)S(1)}, u32[]{:S(2)}, u32[]{:S(2)}) collective-permute-start(f32[40,384]{1,0:T(8,128)S(1)} %get-tuple-element.67), channel_id=1, source_target_pairs={{0,8},{1,9},{2,10},{3,11},{4,12},{5,13},{6,14},{7,15},{8,0},{9,1},... | collective-permute-start | bytes 184328 | tf_op jit(solution)/shard_map/ppermute | solution.py:31
  49.9 0.6 collective-permute-start.12
  50.5 2.8 %collective-permute-done.10.k1 = f32[40,384]{1,0:T(8,128)S(1)} collective-permute-done((f32[40,384]{1,0:T(8,128)S(1)}, f32[40,384]{1,0:T(8,128)S(1)}, u32[]{:S(2)}, u32[]{:S(2)}) %collective-permute-start.10) | collective-permute-done | bytes 61472 | tf_op jit(solution)/shard_map/ppermute | solution.py:31
  53.2 0.0 collective-permute-done.11.k2
  53.2 0.9 collective-permute-done.12.k3
  54.1 0.0 collective-permute-done.9.down_b
  54.1 0.0 collective-permute-done.7.up_a
  54.1 1.0 %blocks.1 = (f32[112,768]{1,0:T(8,128)S(1)}, bf16[112,768]{1,0:T(8,128)(2,1)S(1)}, bf16[112,768]{1,0:T(8,128)(2,1)S(1)}, bf16[112,768]{1,0:T(8,128)(2,1)S(1)}) custom-call(s32[5]{0:T(128)S(1)} %stack.33.place, f32[384,768]{1,0:T(8,128)S(1)} %get-tuple-element.56.own, bf16[384,384]{1,0:T(8,128)(2,1)S(1)} %collective-permute-done.4.down_a, ...), custom_call_target="tpu_custom_call" | custom-call | flops 1000000 | bytes 4000000 | tf_op jit(solution)/shard_map/blocks/pallas_call | solution.py:471
  55.1 0.1 collective-permute-start.14
  55.2 4.9 %collective-permute-start.15 = (bf16[112,768]{1,0:T(8,128)(2,1)S(1)}, bf16[112,768]{1,0:T(8,128)(2,1)S(1)}, u32[]{:S(2)}, u32[]{:S(2)}) collective-permute-start(bf16[112,768]{1,0:T(8,128)(2,1)S(1)} %get-tuple-element.73), channel_id=1, source_target_pairs={{0,3},{1,2},{2,1},{3,0},{4,7},{5,6},{6,5},{7,4},{8,11},{9,10},{10,... | collective-permute-start | bytes 516104 | tf_op jit(solution)/shard_map/ppermute | solution.py:596
  60.1 1.2 %collective-permute-start.13 = (bf16[112,768]{1,0:T(8,128)(2,1)S(1)}, bf16[112,768]{1,0:T(8,128)(2,1)S(1)}, u32[]{:S(2)}, u32[]{:S(2)}) collective-permute-start(bf16[112,768]{1,0:T(8,128)(2,1)S(1)} %get-tuple-element.69._), channel_id=1, source_target_pairs={{0,2},{1,3},{2,0},{3,1},{4,6},{5,7},{6,4},{7,5},{8,10},{9,11},{10,... | collective-permute-start | bytes 516104 | tf_op jit(solution)/shard_map/ppermute | solution.py:35
  61.2 6.5 %input_grads.1 = (bf16[256,1536]{1,0:T(8,128)(2,1)}, f32[8,128]{1,0:T(8,128)S(1)}) custom-call(s32[4]{0:T(128)S(1)} %pad_add_fusion.where, bf16[288,1536]{1,0:T(8,128)(2,1)S(1)} %get-tuple-element.55._.conv_grad, f32[33,1536]{1,0:T(8,128)S(1)} %dynamic-update-slice.1.taps, bf16[112,768]{1,0:T(8,128)(2,1)S(1)} %get-tuple-element.69._), custom_call_target="tpu_custom_call" | custom-call | flops 50000000 | bytes 2000000 | tf_op jit(solution)/shard_map/input_grads/pallas_call | solution.py:375
  67.7 0.1 collective-permute-done.15.diagonal
  67.8 6.7 %collective-permute-done.13.across = bf16[112,768]{1,0:T(8,128)(2,1)S(1)} collective-permute-done((bf16[112,768]{1,0:T(8,128)(2,1)S(1)}, bf16[112,768]{1,0:T(8,128)(2,1)S(1)}, u32[]{:S(2)}, u32[]{:S(2)}) %collective-permute-start.13) | collective-permute-done | bytes 172064 | tf_op jit(solution)/shard_map/ppermute | solution.py:35
  74.6 0.8 squares.1
  75.4 0.1 collective-permute-start.16
  75.4 2.9 %collective-permute-start.17 = (bf16[112,384]{1,0:T(8,128)(2,1)S(1)}, bf16[112,384]{1,0:T(8,128)(2,1)S(1)}, u32[]{:S(2)}, u32[]{:S(2)}) collective-permute-start(bf16[112,384]{1,0:T(8,128)(2,1)S(1)} %get-tuple-element.77), channel_id=1, source_target_pairs={{0,128},{16,144},{32,160},{48,176},{64,192},{80,208},{96,224},{112... | collective-permute-start | bytes 258056 | tf_op jit(solution)/shard_map/ppermute | solution.py:43
  78.3 0.0 collective-permute-start.18
  78.3 1.8 %collective-permute-done.16.one = bf16[112,384]{1,0:T(8,128)(2,1)S(1)} collective-permute-done((bf16[112,384]{1,0:T(8,128)(2,1)S(1)}, bf16[112,384]{1,0:T(8,128)(2,1)S(1)}, u32[]{:S(2)}, u32[]{:S(2)}) %collective-permute-start.16) | collective-permute-done | bytes 86048 | tf_op jit(solution)/shard_map/ppermute | solution.py:43
  80.1 2.0 %collective-permute-done.17.two = bf16[112,384]{1,0:T(8,128)(2,1)S(1)} collective-permute-done((bf16[112,384]{1,0:T(8,128)(2,1)S(1)}, bf16[112,384]{1,0:T(8,128)(2,1)S(1)}, u32[]{:S(2)}, u32[]{:S(2)}) %collective-permute-start.17) | collective-permute-done | bytes 86048 | tf_op jit(solution)/shard_map/ppermute | solution.py:43
  82.1 1.9 %collective-permute-done.18.three = bf16[112,384]{1,0:T(8,128)(2,1)S(1)} collective-permute-done((bf16[112,384]{1,0:T(8,128)(2,1)S(1)}, bf16[112,384]{1,0:T(8,128)(2,1)S(1)}, u32[]{:S(2)}, u32[]{:S(2)}) %collective-permute-start.18) | collective-permute-done | bytes 86048 | tf_op jit(solution)/shard_map/ppermute | solution.py:43
  84.0 0.7 quarters.1
  84.7 3.5 %collective-permute-start.19 = (bf16[112,96]{1,0:T(8,128)(2,1)S(1)}, bf16[112,96]{1,0:T(8,128)(2,1)S(1)}, u32[]{:S(2)}, u32[]{:S(2)}) collective-permute-start(bf16[112,96]{1,0:T(8,128)(2,1)S(1)} %get-tuple-element.80), channel_id=1, source_target_pairs={{0,16},{16,32},{32,48},{48,0},{64,80},{80,96},{96,112},{112,64},{1... | collective-permute-start | bytes 64520 | tf_op jit(solution)/shard_map/ppermute | solution.py:47
  88.2 0.7 collective-permute-start.20
  88.9 2.8 %collective-permute-start.21 = (bf16[112,96]{1,0:T(8,128)(2,1)S(1)}, bf16[112,96]{1,0:T(8,128)(2,1)S(1)}, u32[]{:S(2)}, u32[]{:S(2)}) collective-permute-start(bf16[112,96]{1,0:T(8,128)(2,1)S(1)} %get-tuple-element.82), channel_id=1, source_target_pairs={{0,48},{16,0},{32,16},{48,32},{64,112},{80,64},{96,80},{112,96},{1... | collective-permute-start | bytes 64520 | tf_op jit(solution)/shard_map/ppermute | solution.py:47
  91.7 1.3 %collective-permute-done.20.two = bf16[112,96]{1,0:T(8,128)(2,1)S(1)} collective-permute-done((bf16[112,96]{1,0:T(8,128)(2,1)S(1)}, bf16[112,96]{1,0:T(8,128)(2,1)S(1)}, u32[]{:S(2)}, u32[]{:S(2)}) %collective-permute-start.20) | collective-permute-done | bytes 21536 | tf_op jit(solution)/shard_map/ppermute | solution.py:47
  93.1 0.2 collective-permute-done.21.three
  93.3 0.6 means.1
  (9 shorter events, 0.0 us)
Async XLA Ops:
  0.6 14.3 %copy-start = (bf16[1,256,1536]{2,1,0:T(8,128)(2,1)S(1)}, bf16[1,256,1536]{2,1,0:T(8,128)(2,1)}, u32[]{:S(2)}) copy-start(bf16[1,256,1536]{2,1,0:T(8,128)(2,1)} %param.6) | copy-start | bytes 2359300
  2.6 17.7 %collective-permute-start = (bf16[48,1536]{1,0:T(8,128)(2,1)S(1)}, bf16[48,1536]{1,0:T(8,128)(2,1)S(1)}, u32[]{:S(2)}, u32[]{:S(2)}) collective-permute-start(bf16[48,1536]{1,0:T(8,128)(2,1)S(1)} %get-tuple-element.92), channel_id=1, source_target_pairs={{0,15},{1,2},{2,1},{3,4},{4,3},{5,6},{6,5},{7,8},{8,7},{9,10},{10,... | collective-permute-start | bytes 442376 | tf_op jit(solution)/shard_map/ppermute | solution.py:51
  11.7 8.5 %collective-permute-start.1 = (bf16[48,1536]{1,0:T(8,128)(2,1)S(1)}, bf16[48,1536]{1,0:T(8,128)(2,1)S(1)}, u32[]{:S(2)}, u32[]{:S(2)}) collective-permute-start(bf16[48,1536]{1,0:T(8,128)(2,1)S(1)} %get-tuple-element.93), channel_id=1, source_target_pairs={{0,1},{1,0},{2,3},{3,2},{4,5},{5,4},{6,7},{7,6},{8,9},{9,8},{10,11... | collective-permute-start | bytes 442376 | tf_op jit(solution)/shard_map/ppermute | solution.py:39
  11.7 12.7 %collective-permute-start.3 = (bf16[256,1536]{1,0:T(8,128)(2,1)}, bf16[256,1536]{1,0:T(8,128)(2,1)S(1)}, u32[]{:S(2)}, u32[]{:S(2)}) collective-permute-start(bf16[256,1536]{1,0:T(8,128)(2,1)} %bitcast.26), channel_id=1, source_target_pairs={{0,1},{1,0},{2,3},{3,2},{4,5},{5,4},{6,7},{7,6},{8,9},{9,8},{10,11... | collective-permute-start | bytes 2359304 | tf_op jit(solution)/shard_map/ppermute | solution.py:39
  20.3 1.9 %copy-start.1 = (bf16[1,256,1536]{2,1,0:T(8,128)(2,1)S(1)}, bf16[1,256,1536]{2,1,0:T(8,128)(2,1)}, u32[]{:S(2)}) copy-start(bf16[1,256,1536]{2,1,0:T(8,128)(2,1)} %param.7) | copy-start | bytes 2359300
  20.3 2.6 %copy-start.2 = (bf16[1536,1536]{1,0:T(8,128)(2,1)S(1)}, bf16[1536,1536]{1,0:T(8,128)(2,1)}, u32[]{:S(2)}) copy-start(bf16[1536,1536]{1,0:T(8,128)(2,1)} %param.9) | copy-start | bytes 14155780
  22.0 2.5 %collective-permute-start.2 = (bf16[288,1536]{1,0:T(8,128)(2,1)S(1)}, bf16[288,1536]{1,0:T(8,128)(2,1)S(1)}, u32[]{:S(2)}, u32[]{:S(2)}) collective-permute-start(bf16[288,1536]{1,0:T(8,128)(2,1)S(1)} %get-tuple-element.48.hidden), channel_id=1, source_target_pairs={{0,1},{1,0},{2,3},{3,2},{4,5},{5,4},{6,7},{7,6},{8,9},{9,8},{10,11... | collective-permute-start | bytes 2654216 | tf_op jit(solution)/shard_map/ppermute | solution.py:39
  26.5 9.9 %collective-permute-start.6 = (bf16[384,384]{1,0:T(8,128)(2,1)S(1)}, bf16[384,384]{1,0:T(8,128)(2,1)S(1)}, u32[]{:S(2)}, u32[]{:S(2)}) collective-permute-start(bf16[384,384]{1,0:T(8,128)(2,1)S(1)} %get-tuple-element.60), channel_id=1, source_target_pairs={{0,12},{1,13},{2,14},{3,15},{4,0},{5,1},{6,2},{7,3},{8,4},{9,5},{1... | collective-permute-start | bytes 884744 | tf_op jit(solution)/shard_map/ppermute | solution.py:31
  27.5 11.1 %collective-permute-start.5 = (bf16[384,384]{1,0:T(8,128)(2,1)S(1)}, bf16[384,384]{1,0:T(8,128)(2,1)S(1)}, u32[]{:S(2)}, u32[]{:S(2)}) collective-permute-start(bf16[384,384]{1,0:T(8,128)(2,1)S(1)} %get-tuple-element.54._), channel_id=1, source_target_pairs={{0,4},{1,5},{2,6},{3,7},{4,8},{5,9},{6,10},{7,11},{8,12},{9,13},{1... | collective-permute-start | bytes 884744 | tf_op jit(solution)/shard_map/ppermute | solution.py:31
  28.6 18.5 %collective-permute-start.4 = (bf16[384,384]{1,0:T(8,128)(2,1)S(1)}, bf16[384,384]{1,0:T(8,128)(2,1)S(1)}, u32[]{:S(2)}, u32[]{:S(2)}) collective-permute-start(bf16[384,384]{1,0:T(8,128)(2,1)S(1)} %get-tuple-element.57), channel_id=1, source_target_pairs={{0,12},{1,13},{2,14},{3,15},{4,0},{5,1},{6,2},{7,3},{8,4},{9,5},{1... | collective-permute-start | bytes 884744 | tf_op jit(solution)/shard_map/ppermute | solution.py:31
  30.7 19.2 %collective-permute-start.8 = (bf16[384,384]{1,0:T(8,128)(2,1)S(1)}, bf16[384,384]{1,0:T(8,128)(2,1)S(1)}, u32[]{:S(2)}, u32[]{:S(2)}) collective-permute-start(bf16[384,384]{1,0:T(8,128)(2,1)S(1)} %get-tuple-element.62), channel_id=1, source_target_pairs={{0,4},{1,5},{2,6},{3,7},{4,8},{5,9},{6,10},{7,11},{8,12},{9,13},{1... | collective-permute-start | bytes 884744 | tf_op jit(solution)/shard_map/ppermute | solution.py:31
  38.7 15.4 %collective-permute-start.9 = (bf16[384,384]{1,0:T(8,128)(2,1)S(1)}, bf16[384,384]{1,0:T(8,128)(2,1)S(1)}, u32[]{:S(2)}, u32[]{:S(2)}) collective-permute-start(bf16[384,384]{1,0:T(8,128)(2,1)S(1)} %get-tuple-element.63), channel_id=1, source_target_pairs={{0,12},{1,13},{2,14},{3,15},{4,0},{5,1},{6,2},{7,3},{8,4},{9,5},{1... | collective-permute-start | bytes 884744 | tf_op jit(solution)/shard_map/ppermute | solution.py:31
  38.9 15.2 %collective-permute-start.7 = (bf16[384,384]{1,0:T(8,128)(2,1)S(1)}, bf16[384,384]{1,0:T(8,128)(2,1)S(1)}, u32[]{:S(2)}, u32[]{:S(2)}) collective-permute-start(bf16[384,384]{1,0:T(8,128)(2,1)S(1)} %get-tuple-element.61._), channel_id=1, source_target_pairs={{0,4},{1,5},{2,6},{3,7},{4,8},{5,9},{6,10},{7,11},{8,12},{9,13},{1... | collective-permute-start | bytes 884744 | tf_op jit(solution)/shard_map/ppermute | solution.py:31
  47.0 6.2 %collective-permute-start.10 = (f32[40,384]{1,0:T(8,128)S(1)}, f32[40,384]{1,0:T(8,128)S(1)}, u32[]{:S(2)}, u32[]{:S(2)}) collective-permute-start(f32[40,384]{1,0:T(8,128)S(1)} %get-tuple-element.66), channel_id=1, source_target_pairs={{0,4},{1,5},{2,6},{3,7},{4,8},{5,9},{6,10},{7,11},{8,12},{9,13},{1... | collective-permute-start | bytes 184328 | tf_op jit(solution)/shard_map/ppermute | solution.py:31
  47.1 6.1 %collective-permute-start.11 = (f32[40,384]{1,0:T(8,128)S(1)}, f32[40,384]{1,0:T(8,128)S(1)}, u32[]{:S(2)}, u32[]{:S(2)}) collective-permute-start(f32[40,384]{1,0:T(8,128)S(1)} %get-tuple-element.67), channel_id=1, source_target_pairs={{0,8},{1,9},{2,10},{3,11},{4,12},{5,13},{6,14},{7,15},{8,0},{9,1},... | collective-permute-start | bytes 184328 | tf_op jit(solution)/shard_map/ppermute | solution.py:31
  49.9 4.2 %collective-permute-start.12 = (f32[40,384]{1,0:T(8,128)S(1)}, f32[40,384]{1,0:T(8,128)S(1)}, u32[]{:S(2)}, u32[]{:S(2)}) collective-permute-start(f32[40,384]{1,0:T(8,128)S(1)} %get-tuple-element.68), channel_id=1, source_target_pairs={{0,12},{1,13},{2,14},{3,15},{4,0},{5,1},{6,2},{7,3},{8,4},{9,5},{1... | collective-permute-start | bytes 184328 | tf_op jit(solution)/shard_map/ppermute | solution.py:31
  55.1 12.7 %collective-permute-start.14 = (bf16[112,768]{1,0:T(8,128)(2,1)S(1)}, bf16[112,768]{1,0:T(8,128)(2,1)S(1)}, u32[]{:S(2)}, u32[]{:S(2)}) collective-permute-start(bf16[112,768]{1,0:T(8,128)(2,1)S(1)} %get-tuple-element.72), channel_id=1, source_target_pairs={{0,1},{1,0},{2,3},{3,2},{4,5},{5,4},{6,7},{7,6},{8,9},{9,8},{10,11... | collective-permute-start | bytes 516104 | tf_op jit(solution)/shard_map/ppermute | solution.py:39
  55.2 12.6 %collective-permute-start.15 = (bf16[112,768]{1,0:T(8,128)(2,1)S(1)}, bf16[112,768]{1,0:T(8,128)(2,1)S(1)}, u32[]{:S(2)}, u32[]{:S(2)}) collective-permute-start(bf16[112,768]{1,0:T(8,128)(2,1)S(1)} %get-tuple-element.73), channel_id=1, source_target_pairs={{0,3},{1,2},{2,1},{3,0},{4,7},{5,6},{6,5},{7,4},{8,11},{9,10},{10,... | collective-permute-start | bytes 516104 | tf_op jit(solution)/shard_map/ppermute | solution.py:596
  60.1 14.5 %collective-permute-start.13 = (bf16[112,768]{1,0:T(8,128)(2,1)S(1)}, bf16[112,768]{1,0:T(8,128)(2,1)S(1)}, u32[]{:S(2)}, u32[]{:S(2)}) collective-permute-start(bf16[112,768]{1,0:T(8,128)(2,1)S(1)} %get-tuple-element.69._), channel_id=1, source_target_pairs={{0,2},{1,3},{2,0},{3,1},{4,6},{5,7},{6,4},{7,5},{8,10},{9,11},{10,... | collective-permute-start | bytes 516104 | tf_op jit(solution)/shard_map/ppermute | solution.py:35
  75.4 4.8 %collective-permute-start.16 = (bf16[112,384]{1,0:T(8,128)(2,1)S(1)}, bf16[112,384]{1,0:T(8,128)(2,1)S(1)}, u32[]{:S(2)}, u32[]{:S(2)}) collective-permute-start(bf16[112,384]{1,0:T(8,128)(2,1)S(1)} %get-tuple-element.76), channel_id=1, source_target_pairs={{0,64},{16,80},{32,96},{48,112},{64,128},{80,144},{96,160},{112,17... | collective-permute-start | bytes 258056 | tf_op jit(solution)/shard_map/ppermute | solution.py:43
  75.4 6.7 %collective-permute-start.17 = (bf16[112,384]{1,0:T(8,128)(2,1)S(1)}, bf16[112,384]{1,0:T(8,128)(2,1)S(1)}, u32[]{:S(2)}, u32[]{:S(2)}) collective-permute-start(bf16[112,384]{1,0:T(8,128)(2,1)S(1)} %get-tuple-element.77), channel_id=1, source_target_pairs={{0,128},{16,144},{32,160},{48,176},{64,192},{80,208},{96,224},{112... | collective-permute-start | bytes 258056 | tf_op jit(solution)/shard_map/ppermute | solution.py:43
  78.3 5.7 %collective-permute-start.18 = (bf16[112,384]{1,0:T(8,128)(2,1)S(1)}, bf16[112,384]{1,0:T(8,128)(2,1)S(1)}, u32[]{:S(2)}, u32[]{:S(2)}) collective-permute-start(bf16[112,384]{1,0:T(8,128)(2,1)S(1)} %get-tuple-element.78), channel_id=1, source_target_pairs={{0,192},{16,208},{32,224},{48,240},{64,0},{80,16},{96,32},{112,48}... | collective-permute-start | bytes 258056 | tf_op jit(solution)/shard_map/ppermute | solution.py:43
  84.7 7.0 %collective-permute-start.19 = (bf16[112,96]{1,0:T(8,128)(2,1)S(1)}, bf16[112,96]{1,0:T(8,128)(2,1)S(1)}, u32[]{:S(2)}, u32[]{:S(2)}) collective-permute-start(bf16[112,96]{1,0:T(8,128)(2,1)S(1)} %get-tuple-element.80), channel_id=1, source_target_pairs={{0,16},{16,32},{32,48},{48,0},{64,80},{80,96},{96,112},{112,64},{1... | collective-permute-start | bytes 64520 | tf_op jit(solution)/shard_map/ppermute | solution.py:47
  88.2 4.9 %collective-permute-start.20 = (bf16[112,96]{1,0:T(8,128)(2,1)S(1)}, bf16[112,96]{1,0:T(8,128)(2,1)S(1)}, u32[]{:S(2)}, u32[]{:S(2)}) collective-permute-start(bf16[112,96]{1,0:T(8,128)(2,1)S(1)} %get-tuple-element.81), channel_id=1, source_target_pairs={{0,32},{16,48},{32,0},{48,16},{64,96},{80,112},{96,64},{112,80},{1... | collective-permute-start | bytes 64520 | tf_op jit(solution)/shard_map/ppermute | solution.py:47
  88.9 4.4 %collective-permute-start.21 = (bf16[112,96]{1,0:T(8,128)(2,1)S(1)}, bf16[112,96]{1,0:T(8,128)(2,1)S(1)}, u32[]{:S(2)}, u32[]{:S(2)}) collective-permute-start(bf16[112,96]{1,0:T(8,128)(2,1)S(1)} %get-tuple-element.82), channel_id=1, source_target_pairs={{0,48},{16,0},{32,16},{48,32},{64,112},{80,64},{96,80},{112,96},{1... | collective-permute-start | bytes 64520 | tf_op jit(solution)/shard_map/ppermute | solution.py:47

commit v4 on v3

v4 whole, which is shorter than its diff:
```python
import jax
import jax.numpy as jnp
from jax import lax
from jax.experimental import pallas as pl
from jax.experimental.pallas import tpu as pltpu
from jax.sharding import PartitionSpec as P

KW = 32
HALF = KW // 2
WIDTH = 1536
ROWS = 256
INNER = ROWS - 2 * HALF
LANES = 128
QUARTER = WIDTH // 4
BLOCK = WIDTH // 16
EXTRA = 16
MORE = 48
BF16, F32 = jnp.bfloat16, jnp.float32
SEQ = [(y, z, c) for y in range(4) for z in range(2) for c in range(2)]
DP = [(x, z) for x in range(4) for z in range(4)]
VMEM = pl.BlockSpec(memory_space=pltpu.VMEM)
SMEM = pl.BlockSpec(memory_space=pltpu.SMEM)
ANY = pl.BlockSpec(memory_space=pl.ANY)
LIMIT = pltpu.CompilerParams(vmem_limit_bytes=32 << 20)


def seq_at(y, z, c):
    return ((y % 4) * 2 + z % 2) * 2 + c % 2


def move_y(value, step):
    return lax.ppermute(value, "seq", [(seq_at(*p), seq_at(p[0] + step, p[1], p[2])) for p in SEQ])


def move_z_hi(value):
    return lax.ppermute(value, "seq", [(seq_at(*p), seq_at(p[0], p[1] + 1, p[2])) for p in SEQ])


def move_core(value):
    return lax.ppermute(value, "seq", [(seq_at(*p), seq_at(p[0], p[1], p[2] + 1)) for p in SEQ])


def move_x(value, step):
    return lax.ppermute(value, "dp", [(x * 4 + z, ((x + step) % 4) * 4 + z) for x, z in DP])


def move_z_lo(value, step):
    return lax.ppermute(value, "dp", [(x * 4 + z, x * 4 + (z + step) % 4) for x, z in DP])


def move_neighbour(value):
    return lax.ppermute(value, "seq", [(i, (i + 1) % 16 if i % 2 else (i - 1) % 16) for i in range(16)])


def place_of():
    seq, dp = lax.axis_index("seq"), lax.axis_index("dp")
    return seq >> 2, seq & 1, (seq >> 1) & 1, dp >> 2, dp & 3


def where_of(lengths):
    seq = lax.axis_index("seq")
    return seq * ROWS, lengths[0], seq & 1, seq >> 2


def masked_rows(rows, first, length):
    position = first + lax.broadcasted_iota(jnp.int32, rows.shape, 0)
    return jnp.where((position >= 0) & (position < length), rows.astype(F32), 0.0)


ALL = pl.ds(0, WIDTH)


def low_rows(core, chips, beside, begin, count, lanes=ALL):
    rows = pl.ds(begin, count)
    return jnp.where(core == 0, chips[rows, lanes].astype(F32), beside[rows, lanes].astype(F32))


def high_rows(core, chips, beside, begin, count, lanes=ALL):
    rows = pl.ds(begin, count)
    return jnp.where(core == 0, beside[rows, lanes].astype(F32), chips[rows, lanes].astype(F32))


def rows_of(shape, dtype):
    return jax.ShapeDtypeStruct(shape, dtype)


def rows_of(shape, dtype):
    return jax.ShapeDtypeStruct(shape, dtype)


def depthwise(x_ref, taps_ref, out_ref, rows, chunk, finish=None, taps=None, keep=None):
    taps = {j: j for j in range(KW)} if taps is None else taps

    def lane_block(i, carry):
        lanes = pl.ds(pl.multiple_of(i * LANES, LANES), LANES)
        for place, begin in enumerate(range(0, rows, chunk) if keep is None else keep):
            x = x_ref[pl.ds(begin, chunk + KW), lanes]
            total = None
            for shift in range(8):
                span = chunk if shift == 0 else chunk + 8
                sum_ = None
                for j in range(shift, KW + 1, 8):
                    if j in taps:
                        term = taps_ref[pl.ds(taps[j], 1), lanes] * x[j - shift : j - shift + span]
                        sum_ = term if sum_ is None else sum_ + term
                if shift:
                    sum_ = pltpu.roll(sum_, span - shift, 0)[:chunk]
                total = sum_ if total is None else total + sum_
            if finish is not None:
                total = finish(total, begin)
            out_ref[pl.ds(place * chunk, chunk), lanes] = total
        return carry

    lax.fori_loop(0, WIDTH // LANES, lane_block, 0)


LANE_BLOCKS = [pl.ds(i * LANES, LANES) for i in range(WIDTH // LANES)]


def row_sum(terms):
    total = None
    for term in terms:
        total = term if total is None else total + term
    return jnp.sum(total, axis=1, keepdims=True)


def standardise(conv, taps, refs, begin, size, offset, first, length):
    hidden, standard, inverse = refs
    rows, out = pl.ds(begin, size), pl.ds(offset, size)
    mean = row_sum(conv[rows, lanes] for lanes in LANE_BLOCKS) * (1.0 / WIDTH)
    variance = row_sum(jnp.square(conv[rows, lanes] - mean) for lanes in LANE_BLOCKS) * (1.0 / WIDTH)
    scale = lax.rsqrt(variance + 1e-05)
    valid = first + lax.broadcasted_iota(jnp.int32, (size, 1), 0) < length
    for lanes in LANE_BLOCKS:
        value = (conv[rows, lanes] - mean) * scale
        standard[out, lanes] = value
        if hidden is not None:
            normal = value * taps[pl.ds(KW, 1), lanes]
            value = normal * (0.5 + 0.5 * jnp.tanh(0.5 * normal))
            hidden[out, lanes] = jnp.where(valid, value, 0.0).astype(BF16)
    inverse[out, :] = jnp.broadcast_to(scale, (size, LANES))


def inner_kernel(lengths, frames, taps, hidden, standard, inverse, x, conv):
    where = where_of(lengths)
    first, length = where[0], where[1]
    x[...] = masked_rows(frames[...], first, length)
    depthwise(x, taps, conv, INNER, 112)
    for begin in range(0, INNER, 112):
        refs = (hidden, standard, inverse)
        standardise(conv, taps, refs, begin, 112, 2 * HALF + begin, first + HALF + begin, length)


def edge_kernel(lengths, top, bottom, chips, beside, taps, _, __, ___, hidden, standard, inverse, x, conv, h, s, i):
    where = where_of(lengths)
    first, length, core = where[0], where[1], where[2]
    end = first + ROWS

    @pl.when(pl.program_id(0) == 0)
    def _both():
        x[pl.ds(0, HALF), :] = masked_rows(low_rows(core, chips, beside, HALF, HALF), first - HALF, length)
        x[pl.ds(HALF, 2 * HALF), :] = masked_rows(top[...], first, length)
        x[pl.ds(3 * HALF, 2 * HALF), :] = masked_rows(bottom[...], end - 2 * HALF, length)
        x[pl.ds(5 * HALF, HALF), :] = masked_rows(high_rows(core, chips, beside, 0, HALF), end, length)
        depthwise(x, taps, conv, 4 * HALF, HALF, keep=(0, 3 * HALF))
        standardise(conv, taps, (h, s, i), 0, HALF, 0, first, length)
        standardise(conv, taps, (h, s, i), HALF, HALF, HALF, end - HALF, length)

    rows = pl.ds(pl.multiple_of(pl.program_id(0) * HALF, HALF), HALF)
    hidden[...] = h[rows, :]
    standard[...] = s[rows, :]
    inverse[...] = i[rows, :]


SPAN = ROWS + 2 * HALF
FORWARD = (rows_of((SPAN, WIDTH), BF16), rows_of((SPAN, WIDTH), F32), rows_of((SPAN, LANES), F32))


def forward_inner(lengths, frames, taps):
    return pl.pallas_call(
        inner_kernel,
        out_shape=FORWARD,
        in_specs=[SMEM, VMEM, VMEM],
        out_specs=(VMEM, VMEM, VMEM),
        scratch_shapes=[pltpu.VMEM((ROWS, WIDTH), F32), pltpu.VMEM((INNER, WIDTH), F32)],
        compiler_params=LIMIT,
        cost_estimate=pl.CostEstimate(flops=60_000_000, bytes_accessed=4_000_000, transcendentals=800_000),
        name="forward_inner",
    )(lengths, frames, taps)


def fixed(shape, row=0):
    return pl.BlockSpec(shape, lambda i: (row, 0))


SIDE = fixed((3 * HALF, WIDTH))
SCRATCH = [pltpu.VMEM((6 * HALF, WIDTH), F32), pltpu.VMEM((2 * HALF, WIDTH), F32)]
KEPT = [pltpu.VMEM((2 * HALF, WIDTH), BF16), pltpu.VMEM((2 * HALF, WIDTH), F32), pltpu.VMEM((2 * HALF, LANES), F32)]


def forward_edge(lengths, frames, chips, beside, taps, forward):
    def ends(i):
        return (1 + 15 * i, 0)

    return pl.pallas_call(
        edge_kernel,
        grid=(2,),
        out_shape=FORWARD,
        in_specs=[
            SMEM,
            fixed((2 * HALF, WIDTH)),
            fixed((2 * HALF, WIDTH), 7),
            SIDE,
            SIDE,
            fixed((KW + 1, WIDTH)),
            ANY,
            ANY,
            ANY,
        ],
        out_specs=(
            pl.BlockSpec((HALF, WIDTH), ends),
            pl.BlockSpec((HALF, WIDTH), ends),
            pl.BlockSpec((HALF, LANES), ends),
        ),
        scratch_shapes=SCRATCH + KEPT,
        input_output_aliases={6: 0, 7: 1, 8: 2},
        compiler_params=LIMIT,
        cost_estimate=pl.CostEstimate(flops=8_000_000, bytes_accessed=1_000_000, transcendentals=100_000),
        name="forward_edge",
    )(lengths, frames, frames, chips, beside, taps, *forward)


def backward_rows(first, length, upstream, begin, standard, row, inverse, taps, conv_grad, out_row, size, scaled):
    source, rows, held, out = pl.ds(begin, size), pl.ds(row, size), pl.ds(0, size), pl.ds(out_row, size)
    position = first + lax.broadcasted_iota(jnp.int32, (size, 1), 0)
    valid = (position >= 0) & (position < length)
    means, slopes, terms = None, None, []
    for lanes in LANE_BLOCKS:
        value = standard[rows, lanes]
        gain = taps[pl.ds(KW, 1), lanes]
        normal = value * gain
        sigma = 0.5 + 0.5 * jnp.tanh(0.5 * normal)
        grad = jnp.where(valid, upstream[source, lanes] * (sigma + normal * sigma * (1.0 - sigma)), 0.0)
        terms.append(jnp.sum((grad * value).reshape(size // 8, 8, LANES), axis=0))
        grad = grad * gain
        scaled[held, lanes] = grad
        slope = grad * value
        means = grad if means is None else means + grad
        slopes = slope if slopes is None else slopes + slope
    mean = jnp.sum(means, axis=1, keepdims=True) * (1.0 / WIDTH)
    slope = jnp.sum(slopes, axis=1, keepdims=True) * (1.0 / WIDTH)
    scale = inverse[rows, :1]
    for lanes in LANE_BLOCKS:
        value = scaled[held, lanes] - mean - standard[rows, lanes] * slope
        conv_grad[out, lanes] = (scale * value).astype(BF16)
    return terms


def backward_kernel(lengths, upstream, standard, inverse, taps, _, conv_grad, gain_sum, scaled):
    where = where_of(lengths)
    terms = []
    for begin in (0, ROWS // 2):
        span = HALF + begin
        refs = (upstream, span, standard, span, inverse, taps, conv_grad, begin, ROWS // 2, scaled)
        terms.append(backward_rows(where[0] + begin, where[1], *refs))
    for lanes, one, two in zip(LANE_BLOCKS, *terms):
        gain_sum[:, lanes] = one + two


def backward(lengths, upstream, standard, inverse, taps, after):
    return pl.pallas_call(
        backward_kernel,
        out_shape=(rows_of((ROWS, WIDTH), BF16), rows_of((8, WIDTH), F32)),
        in_specs=[SMEM, VMEM, VMEM, VMEM, VMEM, ANY],
        out_specs=(VMEM, VMEM),
        scratch_shapes=[pltpu.VMEM((ROWS // 2, WIDTH), F32)],
        compiler_params=LIMIT,
        cost_estimate=pl.CostEstimate(flops=10_000_000, bytes_accessed=4_000_000, transcendentals=400_000),
        name="backward",
    )(lengths, upstream, standard, inverse, taps, after)


def outer_kernel(lengths, frames, chips, beside, taps, upstream, _, out, x, conv, standard, inverse, scaled):
    where = where_of(lengths)
    first, length, core = where[0], where[1], where[2]
    end = first + ROWS
    top, bottom = frames[pl.ds(0, HALF), :], frames[pl.ds(ROWS - HALF, HALF), :]
    x[pl.ds(0, 2 * HALF), :] = masked_rows(low_rows(core, chips, beside, 0, 2 * HALF), first - 2 * HALF, length)
    x[pl.ds(2 * HALF, HALF), :] = masked_rows(top, first, length)
    x[pl.ds(3 * HALF, HALF), :] = masked_rows(bottom, end - HALF, length)
    x[pl.ds(4 * HALF, 2 * HALF), :] = masked_rows(high_rows(core, chips, beside, 0, 2 * HALF), end, length)
    depthwise(x, taps, conv, 4 * HALF, HALF, keep=(0, 3 * HALF))
    standardise(conv, taps, (None, standard, inverse), 0, 2 * HALF, 0, first, length)
    for row, begin, position in ((0, 0, first - HALF), (HALF, HALF + ROWS, end)):
        refs = (upstream, begin, standard, row, inverse, taps, out, row, HALF, scaled)
        backward_rows(position, length, *refs)


def outer_grads(lengths, frames, chips, beside, taps, upstream, after):
    return pl.pallas_call(
        outer_kernel,
        out_shape=rows_of((2 * HALF, WIDTH), BF16),
        in_specs=[SMEM] + [VMEM] * 5 + [ANY],
        out_specs=VMEM,
        scratch_shapes=SCRATCH + KEPT[1:] + [pltpu.VMEM((HALF, WIDTH), F32)],
        compiler_params=LIMIT,
        cost_estimate=pl.CostEstimate(flops=8_000_000, bytes_accessed=1_000_000, transcendentals=0),
        name="outer_grads",
    )(lengths, frames, chips, beside, taps, upstream, after)


SIDE_LANES = WIDTH // 2


def fill_rows(where, frames, chips, beside, conv_grad, x, g, columns):
    first, length, core = where[0], where[1], where[2]
    low = low_rows(core, chips, beside, HALF, HALF, columns)
    high = high_rows(core, chips, beside, 0, HALF, columns)
    x[pl.ds(0, HALF), :] = masked_rows(low, first - HALF, length)
    x[pl.ds(HALF, ROWS), :] = masked_rows(frames[:, columns], first, length)
    x[pl.ds(HALF + ROWS, HALF), :] = masked_rows(high, first + ROWS, length)
    g[pl.ds(0, 8), :] = jnp.zeros((8, SIDE_LANES), F32)
    g[pl.ds(8, ROWS), :] = conv_grad[:, columns].astype(F32)
    g[pl.ds(8 + ROWS, 8), :] = jnp.zeros((8, SIDE_LANES), F32)


def kernel_grad_lanes(x, g, gain_rows, out, offset):
    chunk = 88

    def lane_block(i, carry):
        lanes = pl.ds(pl.multiple_of(i * LANES, LANES), LANES)
        whole = pl.ds(pl.multiple_of(i * LANES + offset, LANES), LANES)
        sums = [None] * KW
        for begin in range(0, ROWS + 8, chunk):
            x_rows = x[pl.ds(begin, chunk + KW - 8), lanes]
            grad = g[pl.ds(begin, chunk + 8), lanes]
            for shift in range(8):
                moved = grad[8:] if shift == 0 else pltpu.roll(grad, shift, 0)[8:]
                for a in range(KW // 8):
                    j = 8 * a + shift
                    product = (moved * x_rows[8 * a : 8 * a + chunk]).reshape(chunk // 8, 8, LANES)
                    product = jnp.sum(product, axis=0)
                    sums[j] = product if sums[j] is None else sums[j] + product
        out[pl.ds(0, KW), whole] = jnp.concatenate(
            [jnp.sum(value, axis=0, keepdims=True) for value in sums], axis=0
        )
        gain = jnp.sum(gain_rows[:, whole], axis=0, keepdims=True)
        out[pl.ds(KW, 8), whole] = jnp.broadcast_to(gain, (8, LANES))
        return carry

    lax.fori_loop(0, SIDE_LANES // LANES, lane_block, 0)


def first_grad_kernel(lengths, frames, chips, beside, conv_grad, gain_rows, out, x, g):
    where = where_of(lengths)
    fill_rows(where, frames, chips, beside, conv_grad, x, g, pl.ds(0, SIDE_LANES))
    kernel_grad_lanes(x, g, gain_rows, out, 0)


def other_grad_kernel(lengths, frames, chips, beside, conv_grad, gain_rows, first, _, keep, one, two, three, x, g, rows):
    where = where_of(lengths)
    fill_rows(where, frames, chips, beside, conv_grad, x, g, pl.ds(SIDE_LANES, SIDE_LANES))
    rows[pl.ds(0, KW + 8), pl.ds(0, SIDE_LANES)] = first[...]
    kernel_grad_lanes(x, g, gain_rows, rows, SIDE_LANES)
    rows[pl.ds(KW + 8, 8), :] = jnp.zeros((8, WIDTH), F32)
    for step, out in enumerate((keep, one, two, three)):
        columns = pl.ds(pl.multiple_of(lax.rem(where[3] + step, 4) * QUARTER, QUARTER), QUARTER)
        out[...] = rows[:, columns].astype(out.dtype)


GRAD_SCRATCH = [pltpu.VMEM((ROWS + KW, SIDE_LANES), F32), pltpu.VMEM((ROWS + 16, SIDE_LANES), F32)]
GRAD_COST = pl.CostEstimate(flops=25_000_000, bytes_accessed=1_000_000, transcendentals=0)


def kernel_grads_first(lengths, frames, chips, beside, conv_grad, gain_rows):
    return pl.pallas_call(
        first_grad_kernel,
        out_shape=rows_of((KW + 8, SIDE_LANES), F32),
        in_specs=[SMEM] + [VMEM] * 5,
        out_specs=VMEM,
        scratch_shapes=GRAD_SCRATCH,
        compiler_params=LIMIT,
        cost_estimate=GRAD_COST,
        name="kernel_grads_first",
    )(lengths, frames, chips, beside, conv_grad, gain_rows)


def kernel_grads_other(lengths, frames, chips, beside, conv_grad, gain_rows, first, after):
    return pl.pallas_call(
        other_grad_kernel,
        out_shape=(rows_of((MORE, QUARTER), F32),) + (rows_of((MORE, QUARTER), BF16),) * 3,
        in_specs=[SMEM] + [VMEM] * 6 + [ANY],
        out_specs=(VMEM,) * 4,
        scratch_shapes=GRAD_SCRATCH + [pltpu.VMEM((MORE, WIDTH), F32)],
        compiler_params=LIMIT,
        cost_estimate=GRAD_COST,
        name="kernel_grads_other",
    )(lengths, frames, chips, beside, conv_grad, gain_rows, first, after)


def input_grad_kernel(lengths, conv_grad, outer, taps, _, out, token, g):
    where = where_of(lengths)
    token[...] = jnp.zeros(token.shape, F32)
    first, length = where[0], where[1]
    g[pl.ds(0, HALF), :] = outer[pl.ds(0, HALF), :].astype(F32)
    g[pl.ds(HALF, ROWS), :] = conv_grad[...].astype(F32)
    g[pl.ds(HALF + ROWS, HALF), :] = outer[pl.ds(HALF, HALF), :].astype(F32)

    def finish(total, begin):
        return masked_rows(total, first + begin, length).astype(BF16)

    depthwise(g, taps, out, ROWS, 64, finish, {j: KW - j for j in range(1, KW + 1)})


def input_grads(lengths, conv_grad, outer, taps, after):
    return pl.pallas_call(
        input_grad_kernel,
        out_shape=(rows_of((ROWS, WIDTH), BF16), rows_of((8, LANES), F32)),
        in_specs=[SMEM, VMEM, VMEM, VMEM, ANY],
        out_specs=(VMEM, VMEM),
        scratch_shapes=[pltpu.VMEM((ROWS + KW, WIDTH), F32)],
        compiler_params=LIMIT,
        cost_estimate=pl.CostEstimate(flops=50_000_000, bytes_accessed=2_000_000, transcendentals=0),
        name="input_grads",
    )(lengths, conv_grad, outer, taps, after)


def small_call(kernel, name, out_shape, operands, in_specs, scratch=()):
    return pl.pallas_call(
        kernel,
        out_shape=out_shape,
        in_specs=in_specs,
        out_specs=jax.tree.map(lambda _: VMEM, out_shape),
        scratch_shapes=list(scratch),
        compiler_params=LIMIT,
        cost_estimate=pl.CostEstimate(flops=500_000, bytes_accessed=1_500_000, transcendentals=0),
        name=name,
    )(*operands)


def row_products(place, hidden, hidden_other, cot, cot_other, step):
    columns = pl.ds(pl.multiple_of(place[1] * (WIDTH // 2), WIDTH // 2), WIDTH // 2)
    rows = pl.ds(pl.multiple_of(lax.rem(place[0] + step, 4) * QUARTER, QUARTER), QUARTER)
    dims = (((0,), (0,)), ((), ()))
    own_rows = pl.ds(HALF, ROWS)
    return lax.dot_general(
        hidden[own_rows, rows], cot[:, columns], dims, preferred_element_type=F32
    ) + lax.dot_general(hidden_other[own_rows, rows], cot_other[:, columns], dims, preferred_element_type=F32)


def far_kernel(hidden, hidden_other, cot, cot_other, _, far_a, far_b):
    place = place_of()
    value = row_products(place, hidden, hidden_other, cot, cot_other, 2).astype(BF16)
    far_a[...] = value[:, :QUARTER]
    far_b[...] = value[:, QUARTER:]


def far_products(hidden, hidden_other, cot, cot_other, after):
    half = rows_of((QUARTER, QUARTER), BF16)
    operands = (hidden, hidden_other, cot, cot_other, after)
    return small_call(far_kernel, "far_products", (half, half), operands, [VMEM] * 4 + [ANY])


def near_kernel(hidden, hidden_other, cot, cot_other, _, above_a, above_b, below_a, below_b, own):
    place = place_of()
    for step, (a, b) in ((1, (above_a, above_b)), (3, (below_a, below_b))):
        value = row_products(place, hidden, hidden_other, cot, cot_other, step)
        a[...] = value[:, :QUARTER].astype(a.dtype)
        b[...] = value[:, QUARTER:].astype(b.dtype)
    own[...] = row_products(place, hidden, hidden_other, cot, cot_other, 0)


def near_products(hidden, hidden_other, cot, cot_other, after):
    half = (QUARTER, QUARTER)
    shapes = tuple(rows_of(half, dtype) for dtype in (F32, BF16, BF16, F32)) + (rows_of((QUARTER, 2 * QUARTER), F32),)
    operands = (hidden, hidden_other, cot, cot_other, after)
    return small_call(near_kernel, "near_products", shapes, operands, [VMEM] * 4 + [ANY])


def seconds_kernel(above_a, up_a, below_b, down_b, _, second_a, second_b):
    second_a[...] = (above_a[...] + up_a[...].astype(F32)).astype(BF16)
    second_b[...] = (below_b[...] + down_b[...].astype(F32)).astype(BF16)


def seconds(above_a, up_a, below_b, down_b, after):
    return pl.pallas_call(
        seconds_kernel,
        out_shape=(rows_of((QUARTER, QUARTER), BF16),) * 2,
        in_specs=[VMEM, VMEM, VMEM, VMEM, ANY],
        out_specs=(VMEM,) * 2,
        compiler_params=LIMIT,
        cost_estimate=pl.CostEstimate(flops=300_000, bytes_accessed=2_400_000, transcendentals=0),
        name="seconds",
    )(above_a, up_a, below_b, down_b, after)


HALVES = 2 * BLOCK
HELD = (HALVES + EXTRA, WIDTH // 2)


def blocks_kernel(own, down_a, up_a, up_b, down_b, k0, k1, k2, k3, keep, send, total, extra):
    place = place_of()
    core = place[1]
    total[:, :QUARTER] = own[:, :QUARTER] + (down_a[...].astype(F32) + up_a[...].astype(F32))
    total[:, QUARTER:] = own[:, QUARTER:] + (down_b[...].astype(F32) + up_b[...].astype(F32))
    sums = k0[...] + (k1[...].astype(F32) + k2[...].astype(F32) + k3[...].astype(F32))
    extra[...] = jnp.zeros(extra.shape, F32)
    for z in range(2):
        for c in range(2):
            column = (2 * z + c) * BLOCK
            for q in range(5):
                value = sums[8 * q : 8 * q + 8, column : column + BLOCK]
                extra[c, pl.ds(8 * z, 8), pl.ds(q * BLOCK, BLOCK)] = value
    for out, c in ((keep, core), (send, 1 - core)):
        for z in range(2):
            rows = pl.ds(pl.multiple_of((2 * z + c) * BLOCK, BLOCK), BLOCK)
            out[pl.ds(z * BLOCK, BLOCK), :] = total[rows, :].astype(out.dtype)
        out[pl.ds(HALVES, EXTRA), :] = extra[c].astype(out.dtype)


def blocks(own, down_a, up_a, up_b, down_b, rows):
    return small_call(
        blocks_kernel,
        "blocks",
        (rows_of(HELD, F32), rows_of(HELD, BF16)),
        (own, down_a, up_a, up_b, down_b, *rows),
        [VMEM] * 9,
        [pltpu.VMEM((QUARTER, 2 * QUARTER), F32), pltpu.VMEM((2, EXTRA, WIDTH // 2), F32)],
    )


def chips_kernel(own, other, keep, send, extra):
    place = place_of()
    z_hi, core = place[2], place[1]
    more = pl.ds(HALVES, EXTRA)
    extra[...] = own[more, :] + other[more, :].astype(F32)
    for out, z in ((keep, z_hi), (send, 1 - z_hi)):
        rows = pl.ds(pl.multiple_of(z * BLOCK, BLOCK), BLOCK)
        out[pl.ds(pl.multiple_of(core * BLOCK, BLOCK), BLOCK), :] = own[rows, :].astype(out.dtype)
        out[pl.ds(pl.multiple_of((1 - core) * BLOCK, BLOCK), BLOCK), :] = other[rows, :].astype(out.dtype)
        value = extra[pl.ds(pl.multiple_of(8 * z, 8), 8), :]
        out[more, :] = jnp.concatenate([value, jnp.zeros((8, WIDTH // 2), F32)], axis=0).astype(out.dtype)


def chip_blocks(own, other):
    return small_call(
        chips_kernel,
        "chip_blocks",
        (rows_of(HELD, F32), rows_of(HELD, BF16)),
        (own, other),
        [VMEM, VMEM],
        [pltpu.VMEM((EXTRA, WIDTH // 2), F32)],
    )


def squares_kernel(mine, other, _, keep, one, two, three, square, extra):
    place = place_of()
    x = place[3]
    for half in range(2):
        rows = pl.ds(half * BLOCK, BLOCK)
        value = mine[rows, :] + other[rows, :].astype(F32)
        square[pl.ds(0, BLOCK), pl.ds(half * (WIDTH // 2), WIDTH // 2)] = value * value
    rows, more = pl.ds(HALVES, EXTRA), pl.ds(BLOCK, EXTRA)
    sums = mine[rows, :] + other[rows, :].astype(F32)
    extra[...] = sums * sums
    square[more, :] = jnp.zeros((EXTRA, WIDTH), F32)
    for dp in range(16):
        columns = pl.ds(dp * BLOCK, BLOCK)
        square[pl.ds(BLOCK, 2), columns] = extra[pl.ds(2 * (dp % 4), 2), pl.ds(dp // 4 * BLOCK, BLOCK)]
        square[pl.ds(BLOCK + 2, 1), columns] = extra[pl.ds(0, 1), pl.ds(4 * BLOCK, BLOCK)]
    for step, out in enumerate((keep, one, two, three)):
        columns = pl.ds(pl.multiple_of(lax.rem(x + step, 4) * QUARTER, QUARTER), QUARTER)
        out[...] = square[:, columns].astype(out.dtype)


def squares(mine, other, after):
    shape = (BLOCK + EXTRA, QUARTER)
    return small_call(
        squares_kernel,
        "squares",
        (rows_of(shape, F32),) + (rows_of(shape, BF16),) * 3,
        (mine, other, after),
        [VMEM, VMEM, ANY],
        [pltpu.VMEM((BLOCK + EXTRA, WIDTH), F32), pltpu.VMEM((EXTRA, WIDTH // 2), F32)],
    )


def quarters_kernel(keep, one, two, three, own, out_one, out_two, out_three, parts):
    place = place_of()
    z_lo = place[4]
    total = keep[...] + one[...].astype(F32) + two[...].astype(F32) + three[...].astype(F32)
    for z in range(4):
        parts[lax.rem(z - z_lo + 4, 4)] = total[:, z * BLOCK : (z + 1) * BLOCK]
    for step, out in enumerate((own, out_one, out_two, out_three)):
        out[...] = parts[step].astype(out.dtype)


def quarters(keep, one, two, three):
    shape = (BLOCK + EXTRA, BLOCK)
    return pl.pallas_call(
        quarters_kernel,
        out_shape=(rows_of(shape, F32),) + (rows_of(shape, BF16),) * 3,
        in_specs=[VMEM] * 4,
        out_specs=(VMEM,) * 4,
        scratch_shapes=[pltpu.VMEM((4,) + shape, F32)],
        compiler_params=LIMIT,
        cost_estimate=pl.CostEstimate(flops=1_000_000, bytes_accessed=1_000_000, transcendentals=0),
        name="quarters",
    )(keep, one, two, three)


def means_kernel(own, one, two, three, out, kernel, gain):
    total = own[...] + one[...].astype(F32) + two[...].astype(F32) + three[...].astype(F32)
    total = total * (1.0 / 16)
    out[...] = total[:BLOCK]
    kernel[...] = total[BLOCK : BLOCK + 2]
    gain[...] = total[BLOCK + 2 : BLOCK + 3]


def means(own, one, two, three):
    return pl.pallas_call(
        means_kernel,
        out_shape=(rows_of((BLOCK, BLOCK), F32), rows_of((2, BLOCK), F32), rows_of((1, BLOCK), F32)),
        in_specs=[VMEM] * 4,
        out_specs=(VMEM,) * 3,
        compiler_params=LIMIT,
        cost_estimate=pl.CostEstimate(flops=100_000, bytes_accessed=200_000, transcendentals=0),
        name="means",
    )(own, one, two, three)


def on_device(frames_in, cotangent, lengths, out_weight, conv_kernel, layer_norm_gain):
    seq = lax.axis_index("seq")
    core = seq % 2
    frames, cot = frames_in[0], cotangent[0]
    row = lax.broadcasted_iota(jnp.int32, (KW + 1, WIDTH), 0)
    taps = jnp.where(row < KW, jnp.pad(conv_kernel, ((0, 1), (0, 0))), layer_norm_gain[None])
    begin = jnp.concatenate([frames[: 2 * HALF], cot[:HALF]], axis=0)
    end = jnp.concatenate([frames[-2 * HALF :], cot[-HALF:]], axis=0)
    chips = move_neighbour(jnp.where(core == 0, begin, end))
    beside = move_core(jnp.where(core == 0, end, begin))
    cot_other = move_core(cot)
    forward = forward_inner(lengths, frames, taps)
    hidden, standard, inverse = forward_edge(lengths, frames, chips, beside, taps, forward)
    hidden_other = move_core(hidden)
    low = jnp.where(core == 0, chips[2 * HALF :], beside[2 * HALF :])
    high = jnp.where(core == 0, beside[2 * HALF :], chips[2 * HALF :])
    late_cot, _ = lax.optimization_barrier((jnp.concatenate([low, cot, high], axis=0), hidden))
    upstream = lax.dot_general(late_cot, out_weight, (((1,), (1,)), ((), ())), preferred_element_type=F32)
    operands = (hidden, hidden_other, cot, cot_other)
    far_a, far_b = far_products(*operands, upstream)
    above_a, above_b, below_a, below_b, own = near_products(*operands, far_a)
    up_a = move_y(far_a, 1)
    down_b = move_y(far_b, -1)
    up_b = move_y(above_b, 1)
    down_a = move_y(below_a, -1)
    conv_grad, gain_rows = backward(lengths, upstream, standard, inverse, taps, own)
    operands = (lengths, frames, chips, beside, conv_grad, gain_rows)
    rows = kernel_grads_first(*operands)
    second_a, second_b = seconds(above_a, up_a, below_b, down_b, rows)
    up_a = move_y(second_a, 1)
    down_b = move_y(second_b, -1)
    rows = kernel_grads_other(*operands, rows, second_a)
    rows = [rows[0]] + [move_y(rows[k], k) for k in (1, 2, 3)]
    own, other = blocks(own, down_a, up_a, up_b, down_b, rows)
    own, other = chip_blocks(own, move_core(other))
    outer = outer_grads(lengths, frames, chips, beside, taps, upstream, other)
    input_grad, token = input_grads(lengths, conv_grad, outer, taps, other)
    keep, *sent = squares(own, move_z_hi(other), token)
    keep, *sent = quarters(keep, *(move_x(value, k + 1) for k, value in enumerate(sent)))
    out, kernel, gain = means(keep, *(move_z_lo(value, k + 1) for k, value in enumerate(sent)))
    return input_grad[None], out, kernel, gain[0]


def solution(mesh):
    return jax.shard_map(
        on_device,
        mesh=mesh,
        in_specs=(P("dp", "seq", None), P("dp", "seq", None), P("dp"), P(), P(), P()),
        out_specs=(P("dp", "seq", None), P("seq", "dp"), P("dp", "seq"), P("seq")),
        check_vma=False,
    )
```

time: 94.1 us -> 88.8 us (0.944)
  Pallas kernels: 28.6 us -> 22.9 us
    ppermute x1 -> x0, starting transfers between devices: 4.88 us -> none  [on_device(): lax.ppermute(diagonal, 'seq', [(seq_at(*p), seq_at(p[0], p[1] + 1, p[2] +...]
    ppermute x9, waiting for transfers between devices: 7.73 us -> 4.11 us  [move_y(): lax.ppermute(value, 'seq', [(seq_at(*p), seq_at(p[0] + step, p[1], p[2]))...]
    pallas_call x6 -> x9, Pallas kernels: 13.6 us -> 10 us  [the longest x1 2.58 us: kernel_grads_other(): pl.pallas_call(other_grad_kernel, out_shape=(rows_of((MORE, QUARTER), F32...]
    ppermute x1, starting transfers between devices: 1.17 us -> 4.69 us  [move_z_hi(): lax.ppermute(value, 'seq', [(seq_at(*p), seq_at(p[0], p[1] + 1, p[2])) fo...]
    ppermute x9, starting transfers between devices: 9.86 us -> 13.1 us  [move_y(): lax.ppermute(value, 'seq', [(seq_at(*p), seq_at(p[0] + step, p[1], p[2]))...]
    ppermute x3, starting transfers between devices: 6.96 us -> 3.9 us  [move_z_lo(): lax.ppermute(value, 'dp', [(x * 4 + z, x * 4 + (z + step) % 4) for x, z i...]
    ppermute x1, waiting for transfers between devices: 6.75 us -> 8.58 us  [move_z_hi(): lax.ppermute(value, 'seq', [(seq_at(*p), seq_at(p[0], p[1] + 1, p[2])) fo...]
    ppermute x4, waiting for transfers between devices: 0.11 us -> 1.61 us  [move_core(): lax.ppermute(value, 'seq', [(seq_at(*p), seq_at(p[0], p[1], p[2] + 1)) fo...]
  transfers between devices with their start and end apart: 22 -> 21, of which waited for: 12 -> 10; matrix products, arithmetic and copies ran while one was open for 4% -> 3% of each run, Pallas kernels for 25% -> 24%
where the time goes in v4:
time: 88.8 us; the launch traced here: 88.6 us
  starting transfers between devices  35.2 us (40%)
  Pallas kernels  22.9 us (26%)
  waiting for transfers between devices  22.7 us (26%)
  local copies, waits for them, and re-layouts  3.61 us (4%)
  matrix products  1.56 us (2%)
  between operations  1.54 us (2%)
  other arithmetic  1.14 us (1%)
    ppermute x9, starting transfers between devices, move_y(): lax.ppermute(value, 'seq', [(seq_at(*p), seq_at(p[0] + step, p[1], p[2]))...  13.1 us
    ppermute x1, starting transfers between devices, move_neighbour(): lax.ppermute(value, 'seq', [(i, (i + 1) % 16 if i % 2 else (i - 1) % 16)...  9.74 us
    ppermute x1, waiting for transfers between devices, move_z_hi(): lax.ppermute(value, 'seq', [(seq_at(*p), seq_at(p[0], p[1] + 1, p[2])) fo...  8.58 us
    pallas_call x1, Pallas kernels, input_grads(): pl.pallas_call(input_grad_kernel, out_shape=(rows_of((ROWS, WIDTH), BF16)...  5.96 us
    ppermute x3, waiting for transfers between devices, move_x(): lax.ppermute(value, 'dp', [(x * 4 + z, (x + step) % 4 * 4 + z) for x, z i...  5.69 us
    pallas_call x1, Pallas kernels, forward_inner(): pl.pallas_call(inner_kernel, out_shape=FORWARD, in_specs=[SMEM, VMEM, VME...  4.77 us
    ppermute x1, starting transfers between devices, move_z_hi(): lax.ppermute(value, 'seq', [(seq_at(*p), seq_at(p[0], p[1] + 1, p[2])) fo...  4.69 us
    ppermute x9, waiting for transfers between devices, move_y(): lax.ppermute(value, 'seq', [(seq_at(*p), seq_at(p[0] + step, p[1], p[2]))...  4.11 us
  transfers between devices with their start and end apart: 21, of which 10 were waited for; matrix products, arithmetic and copies ran while one was open for 3% of the time, Pallas kernels for 24%

profile of v4, /device:TPU:6, one launch (start us, length us, event | category | flops | bytes accessed | tf_op | source)
XLA Modules:
  0.0 88.6 jit_solution(12968858274455691448)
XLA Ops:
  0.6 0.8 slice_bitcast_fusion.3
  1.5 1.0 %slice_bitcast_fusion.1 = (bf16[32,1536]{1,0:T(8,128)(2,1)S(1)}, bf16[32,1536]{1,0:T(8,128)(2,1)S(1)}) fusion(bf16[1,256,1536]{2,1,0:T(8,128)(2,1)} %param.6), kind=kLoop, calls=%fused_computation.7 | loop fusion | bytes 393216 | tf_op jit(solution)/shard_map/slice | solution.py:638
  2.4 0.1 broadcast_select_fusion.1
  2.5 0.1 collective-permute-start.1
  2.6 9.7 %collective-permute-start = (bf16[48,1536]{1,0:T(8,128)(2,1)S(1)}, bf16[48,1536]{1,0:T(8,128)(2,1)S(1)}, u32[]{:S(2)}, u32[]{:S(2)}) collective-permute-start(bf16[48,1536]{1,0:T(8,128)(2,1)S(1)} %get-tuple-element.88), channel_id=1, source_target_pairs={{0,15},{1,2},{2,1},{3,4},{4,3},{5,6},{6,5},{7,8},{8,7},{9,10},{10,... | collective-permute-start | bytes 442376 | tf_op jit(solution)/shard_map/ppermute | solution.py:52
  12.3 0.0 collective-permute-start.3
  12.3 1.0 %pad_select_fusion.taps = f32[33,1536]{1,0:T(8,128)S(1)} fusion(f32[32,1536]{1,0:T(8,128)} %param.10, f32[1536]{0:T(1024)} %param.11, pred[33]{0:T(512)(128)(4,1)S(1)} %iota_compare_fusion), kind=kLoop, calls=%fused_computation.1 | loop fusion | flops 50688 | bytes 405537 | tf_op jit(solution)/shard_map/jit(_where)/select_n | solution.py:637
  14.0 0.0 copy-start
  14.0 1.1 %copy-done = bf16[1,256,1536]{2,1,0:T(8,128)(2,1)S(1)} copy-done((bf16[1,256,1536]{2,1,0:T(8,128)(2,1)S(1)}, bf16[1,256,1536]{2,1,0:T(8,128)(2,1)}, u32[]{:S(2)}) %copy-start) | copy-done | bytes 786456
  15.1 4.8 %forward_inner.1 = (bf16[288,1536]{1,0:T(8,128)(2,1)S(1)}, f32[288,1536]{1,0:T(8,128)S(1)}, f32[288,128]{1,0:T(8,128)S(1)}) custom-call(s32[1]{0:T(128)S(6)} %copy.16.lengths, bf16[256,1536]{1,0:T(8,128)(2,1)S(1)} %bitcast.14, f32[33,1536]{1,0:T(8,128)S(1)} %pad_select_fusion.taps), custom_call_target="tpu_custom_call" | custom-call | flops 60000000 | bytes 4000000 | tf_op jit(solution)/shard_map/forward_inner/pallas_call | solution.py:180
  19.9 0.0 collective-permute-done.1.beside
  19.9 0.0 collective-permute-done.chips
  19.9 0.0 copy-start.2
  20.0 0.0 copy-start.3
  20.0 1.2 %forward_edge.1 = (bf16[288,1536]{1,0:T(8,128)(2,1)S(1)}, f32[288,1536]{1,0:T(8,128)S(1)}, f32[288,128]{1,0:T(8,128)S(1)}) custom-call(s32[1]{0:T(128)S(6)} %copy.16.lengths, bf16[256,1536]{1,0:T(8,128)(2,1)S(1)} %bitcast.15, bf16[256,1536]{1,0:T(8,128)(2,1)S(1)} %bitcast.16, ...), custom_call_target="tpu_custom_call", output_to_operand_aliasing={{0}: (6, {}), {1}: (7, {}), {2}: (8, {})} | custom-call | flops 8000000 | bytes 1000000 | tf_op jit(solution)/shard_map/forward_edge/pallas_call | solution.py:205
  21.2 0.6 collective-permute-start.2
  21.8 0.1 pad_maximum_fusion
  21.8 0.7 copy-done.3
  22.5 1.6 %fusion._.upstream = f32[288,1536]{1,0:T(8,128)S(1)} fusion(bf16[288,1536]{1,0:T(8,128)(2,1)S(1)} %pad_maximum_fusion, bf16[1536,1536]{1,0:T(8,128)(2,1)S(1)} %copy-done.3), kind=kOutput, calls=%fused_computation.13 | convolution fusion | flops 1358954496 | bytes 7372800 | tf_op jit(solution)/shard_map/dot_general | solution.py:649
  24.1 0.0 collective-permute-done.3.cot_other
  24.1 0.0 collective-permute-done.2.hidden_other
  24.1 0.5 far_products.1
  24.6 0.1 collective-permute-start.5
  24.7 3.2 %collective-permute-start.6 = (bf16[384,384]{1,0:T(8,128)(2,1)S(1)}, bf16[384,384]{1,0:T(8,128)(2,1)S(1)}, u32[]{:S(2)}, u32[]{:S(2)}) collective-permute-start(bf16[384,384]{1,0:T(8,128)(2,1)S(1)} %get-tuple-element.56), channel_id=1, source_target_pairs={{0,12},{1,13},{2,14},{3,15},{4,0},{5,1},{6,2},{7,3},{8,4},{9,5},{1... | collective-permute-start | bytes 884744 | tf_op jit(solution)/shard_map/ppermute | solution.py:32
  28.0 1.1 %near_products.1 = (f32[384,384]{1,0:T(8,128)S(1)}, bf16[384,384]{1,0:T(8,128)(2,1)S(1)}, bf16[384,384]{1,0:T(8,128)(2,1)S(1)}, f32[384,384]{1,0:T(8,128)S(1)}, f32[384,768]{1,0:T(8,128)S(1)}) custom-call(bf16[288,1536]{1,0:T(8,128)(2,1)S(1)} %get-tuple-element.46.hidden, bf16[288,1536]{1,0:T(8,128)(2,1)S(1)} %collective-permute-done.2.hidden_other, ...), custom_call_target="tpu_custom_call" | custom-call | flops 500000 | bytes 1500000 | tf_op jit(solution)/shard_map/near_products/pallas_call | solution.py:429
  29.1 0.1 collective-permute-start.4
  29.2 2.0 %collective-permute-start.8 = (bf16[384,384]{1,0:T(8,128)(2,1)S(1)}, bf16[384,384]{1,0:T(8,128)(2,1)S(1)}, u32[]{:S(2)}, u32[]{:S(2)}) collective-permute-start(bf16[384,384]{1,0:T(8,128)(2,1)S(1)} %get-tuple-element.59), channel_id=1, source_target_pairs={{0,4},{1,5},{2,6},{3,7},{4,8},{5,9},{6,10},{7,11},{8,12},{9,13},{1... | collective-permute-start | bytes 884744 | tf_op jit(solution)/shard_map/ppermute | solution.py:32
  31.2 1.3 %backward.1 = (bf16[256,1536]{1,0:T(8,128)(2,1)S(1)}, f32[8,1536]{1,0:T(8,128)S(1)}) custom-call(s32[1]{0:T(128)S(6)} %copy.16.lengths, f32[288,1536]{1,0:T(8,128)S(1)} %fusion._.upstream, f32[288,1536]{1,0:T(8,128)S(1)} %get-tuple-element.48.standard, f32[288,128]{1,0:T(8,128)S(1)} %get-tuple-element.49.inverse, f32[33,1536]{1,0:T(8,128)S(1)} %pad_select_fusion.taps, ...), custom_call_target="tpu_custom_call" | custom-call | flops 10000000 | bytes 4000000 | tf_op jit(solution)/shard_map/backward/pallas_call | solution.py:271
  32.5 2.6 %kernel_grads_first.1._.first = f32[40,768]{1,0:T(8,128)S(1)} custom-call(s32[1]{0:T(128)S(6)} %copy.16.lengths, bf16[256,1536]{1,0:T(8,128)(2,1)S(1)} %bitcast.17, bf16[48,1536]{1,0:T(8,128)(2,1)S(1)} %collective-permute-done.chips, bf16[48,1536]{1,0:T(8,128)(2,1)S(1)} %collective-permute-done.1.beside, bf16[256,1536]{1,0:T(8,128)(2,1)S(1)} %get-tuple-element.52.conv_grad, ...), custom_call_target="tpu_custom_call" | custom-call | flops 25000000 | bytes 1000000 | tf_op jit(solution)/shard_map/kernel_grads_first/pallas_call | solution.py:376
  35.1 0.7 collective-permute-done.5.up_a
  35.7 0.0 collective-permute-done.6.down_b
  35.7 0.1 seconds.1
  35.9 0.3 collective-permute-start.7
  36.1 3.3 %collective-permute-start.9 = (bf16[384,384]{1,0:T(8,128)(2,1)S(1)}, bf16[384,384]{1,0:T(8,128)(2,1)S(1)}, u32[]{:S(2)}, u32[]{:S(2)}) collective-permute-start(bf16[384,384]{1,0:T(8,128)(2,1)S(1)} %get-tuple-element.60), channel_id=1, source_target_pairs={{0,12},{1,13},{2,14},{3,15},{4,0},{5,1},{6,2},{7,3},{8,4},{9,5},{1... | collective-permute-start | bytes 884744 | tf_op jit(solution)/shard_map/ppermute | solution.py:32
  39.5 2.6 %kernel_grads_other.1 = (f32[48,384]{1,0:T(8,128)S(1)}, bf16[48,384]{1,0:T(8,128)(2,1)S(1)}, bf16[48,384]{1,0:T(8,128)(2,1)S(1)}, bf16[48,384]{1,0:T(8,128)(2,1)S(1)}) custom-call(s32[1]{0:T(128)S(6)} %copy.16.lengths, bf16[256,1536]{1,0:T(8,128)(2,1)S(1)} %bitcast.18, bf16[48,1536]{1,0:T(8,128)(2,1)S(1)} %collective-permute-done.chips, ...), custom_call_target="tpu_custom_call" | custom-call | flops 25000000 | bytes 1000000 | tf_op jit(solution)/shard_map/kernel_grads_other/pallas_call | solution.py:389
  42.1 0.1 collective-permute-start.10
  42.2 3.4 %collective-permute-start.11 = (bf16[48,384]{1,0:T(8,128)(2,1)S(1)}, bf16[48,384]{1,0:T(8,128)(2,1)S(1)}, u32[]{:S(2)}, u32[]{:S(2)}) collective-permute-start(bf16[48,384]{1,0:T(8,128)(2,1)S(1)} %get-tuple-element.63), channel_id=1, source_target_pairs={{0,8},{1,9},{2,10},{3,11},{4,12},{5,13},{6,14},{7,15},{8,0},{9,1},... | collective-permute-start | bytes 110600 | tf_op jit(solution)/shard_map/ppermute | solution.py:32
  45.5 0.0 collective-permute-done.8.up_b
  45.5 0.6 collective-permute-start.12
  46.1 3.4 %collective-permute-done.10.k1 = bf16[48,384]{1,0:T(8,128)(2,1)S(1)} collective-permute-done((bf16[48,384]{1,0:T(8,128)(2,1)S(1)}, bf16[48,384]{1,0:T(8,128)(2,1)S(1)}, u32[]{:S(2)}, u32[]{:S(2)}) %collective-permute-start.10) | collective-permute-done | bytes 36896 | tf_op jit(solution)/shard_map/ppermute | solution.py:32
  49.6 0.0 collective-permute-done.11.k2
  49.6 0.4 blocks.1
  50.0 0.1 collective-permute-start.13
  50.1 1.6 %collective-permute-done.13.other = bf16[208,768]{1,0:T(8,128)(2,1)S(1)} collective-permute-done((bf16[208,768]{1,0:T(8,128)(2,1)S(1)}, bf16[208,768]{1,0:T(8,128)(2,1)S(1)}, u32[]{:S(2)}, u32[]{:S(2)}) %collective-permute-start.13) | collective-permute-done | bytes 319520 | tf_op jit(solution)/shard_map/ppermute | solution.py:40
  51.7 0.1 chip_blocks.1
  51.8 4.7 %collective-permute-start.14 = (bf16[208,768]{1,0:T(8,128)(2,1)S(1)}, bf16[208,768]{1,0:T(8,128)(2,1)S(1)}, u32[]{:S(2)}, u32[]{:S(2)}) collective-permute-start(bf16[208,768]{1,0:T(8,128)(2,1)S(1)} %get-tuple-element.67._), channel_id=1, source_target_pairs={{0,2},{1,3},{2,0},{3,1},{4,6},{5,7},{6,4},{7,5},{8,10},{9,11},{10,... | collective-permute-start | bytes 958472 | tf_op jit(solution)/shard_map/ppermute | solution.py:36
  56.5 1.3 %outer_grads.1.outer = bf16[32,1536]{1,0:T(8,128)(2,1)S(1)} custom-call(s32[1]{0:T(128)S(6)} %copy.16.lengths, bf16[256,1536]{1,0:T(8,128)(2,1)S(1)} %bitcast.19, bf16[48,1536]{1,0:T(8,128)(2,1)S(1)} %collective-permute-done.chips, bf16[48,1536]{1,0:T(8,128)(2,1)S(1)} %collective-permute-done.1.beside, f32[33,1536]{1,0:T(8,128)S(1)} %pad_select_fusion.taps, ...), custom_call_target="tpu_custom_call" | custom-call | flops 8000000 | bytes 1000000 | tf_op jit(solution)/shard_map/outer_grads/pallas_call | solution.py:300
  57.8 6.0 %input_grads.1 = (bf16[256,1536]{1,0:T(8,128)(2,1)}, f32[8,128]{1,0:T(8,128)S(1)}) custom-call(s32[1]{0:T(128)S(6)} %copy.16.lengths, bf16[256,1536]{1,0:T(8,128)(2,1)S(1)} %get-tuple-element.52.conv_grad, bf16[32,1536]{1,0:T(8,128)(2,1)S(1)} %outer_grads.1.outer, f32[33,1536]{1,0:T(8,128)S(1)} %pad_select_fusion.taps, bf16[208,768]{1,0:T(8,128)(2,1)S(1)} %get-tuple-element.67._), custom_call_target="tpu_custom_call" | custom-call | flops 50000000 | bytes 2000000 | tf_op jit(solution)/shard_map/input_grads/pallas_call | solution.py:416
  63.7 8.6 %collective-permute-done.14.other = bf16[208,768]{1,0:T(8,128)(2,1)S(1)} collective-permute-done((bf16[208,768]{1,0:T(8,128)(2,1)S(1)}, bf16[208,768]{1,0:T(8,128)(2,1)S(1)}, u32[]{:S(2)}, u32[]{:S(2)}) %collective-permute-start.14) | collective-permute-done | bytes 319520 | tf_op jit(solution)/shard_map/ppermute | solution.py:36
  72.3 0.2 squares.1
  72.5 0.6 collective-permute-start.15
  73.1 2.4 %collective-permute-start.16 = (bf16[112,384]{1,0:T(8,128)(2,1)S(1)}, bf16[112,384]{1,0:T(8,128)(2,1)S(1)}, u32[]{:S(2)}, u32[]{:S(2)}) collective-permute-start(bf16[112,384]{1,0:T(8,128)(2,1)S(1)} %get-tuple-element.73), channel_id=1, source_target_pairs={{0,128},{16,144},{32,160},{48,176},{64,192},{80,208},{96,224},{112... | collective-permute-start | bytes 258056 | tf_op jit(solution)/shard_map/ppermute | solution.py:44
  75.5 0.0 collective-permute-start.17
  75.5 1.6 %collective-permute-done.15.one = bf16[112,384]{1,0:T(8,128)(2,1)S(1)} collective-permute-done((bf16[112,384]{1,0:T(8,128)(2,1)S(1)}, bf16[112,384]{1,0:T(8,128)(2,1)S(1)}, u32[]{:S(2)}, u32[]{:S(2)}) %collective-permute-start.15) | collective-permute-done | bytes 86048 | tf_op jit(solution)/shard_map/ppermute | solution.py:44
  77.1 2.0 %collective-permute-done.16.two = bf16[112,384]{1,0:T(8,128)(2,1)S(1)} collective-permute-done((bf16[112,384]{1,0:T(8,128)(2,1)S(1)}, bf16[112,384]{1,0:T(8,128)(2,1)S(1)}, u32[]{:S(2)}, u32[]{:S(2)}) %collective-permute-start.16) | collective-permute-done | bytes 86048 | tf_op jit(solution)/shard_map/ppermute | solution.py:44
  79.1 2.1 %collective-permute-done.17.three = bf16[112,384]{1,0:T(8,128)(2,1)S(1)} collective-permute-done((bf16[112,384]{1,0:T(8,128)(2,1)S(1)}, bf16[112,384]{1,0:T(8,128)(2,1)S(1)}, u32[]{:S(2)}, u32[]{:S(2)}) %collective-permute-start.17) | collective-permute-done | bytes 86048 | tf_op jit(solution)/shard_map/ppermute | solution.py:44
  81.2 0.2 quarters.1
  81.4 1.0 %collective-permute-start.18 = (bf16[112,96]{1,0:T(8,128)(2,1)S(1)}, bf16[112,96]{1,0:T(8,128)(2,1)S(1)}, u32[]{:S(2)}, u32[]{:S(2)}) collective-permute-start(bf16[112,96]{1,0:T(8,128)(2,1)S(1)} %get-tuple-element.76), channel_id=1, source_target_pairs={{0,16},{16,32},{32,48},{48,0},{64,80},{80,96},{96,112},{112,64},{1... | collective-permute-start | bytes 64520 | tf_op jit(solution)/shard_map/ppermute | solution.py:48
  82.4 0.0 collective-permute-start.19
  82.4 2.9 %collective-permute-start.20 = (bf16[112,96]{1,0:T(8,128)(2,1)S(1)}, bf16[112,96]{1,0:T(8,128)(2,1)S(1)}, u32[]{:S(2)}, u32[]{:S(2)}) collective-permute-start(bf16[112,96]{1,0:T(8,128)(2,1)S(1)} %get-tuple-element.78), channel_id=1, source_target_pairs={{0,48},{16,0},{32,16},{48,32},{64,112},{80,64},{96,80},{112,96},{1... | collective-permute-start | bytes 64520 | tf_op jit(solution)/shard_map/ppermute | solution.py:48
  85.3 1.9 %collective-permute-done.18.one = bf16[112,96]{1,0:T(8,128)(2,1)S(1)} collective-permute-done((bf16[112,96]{1,0:T(8,128)(2,1)S(1)}, bf16[112,96]{1,0:T(8,128)(2,1)S(1)}, u32[]{:S(2)}, u32[]{:S(2)}) %collective-permute-start.18) | collective-permute-done | bytes 21536 | tf_op jit(solution)/shard_map/ppermute | solution.py:48
  87.1 0.7 collective-permute-done.19.two
  87.8 0.1 collective-permute-done.20.three
  87.9 0.6 means.1
  (9 shorter events, 0.0 us)
Async XLA Ops:
  2.5 17.4 %collective-permute-start.1 = (bf16[48,1536]{1,0:T(8,128)(2,1)S(1)}, bf16[48,1536]{1,0:T(8,128)(2,1)S(1)}, u32[]{:S(2)}, u32[]{:S(2)}) collective-permute-start(bf16[48,1536]{1,0:T(8,128)(2,1)S(1)} %get-tuple-element.89), channel_id=1, source_target_pairs={{0,1},{1,0},{2,3},{3,2},{4,5},{5,4},{6,7},{7,6},{8,9},{9,8},{10,11... | collective-permute-start | bytes 442376 | tf_op jit(solution)/shard_map/ppermute | solution.py:40
  2.6 17.3 %collective-permute-start = (bf16[48,1536]{1,0:T(8,128)(2,1)S(1)}, bf16[48,1536]{1,0:T(8,128)(2,1)S(1)}, u32[]{:S(2)}, u32[]{:S(2)}) collective-permute-start(bf16[48,1536]{1,0:T(8,128)(2,1)S(1)} %get-tuple-element.88), channel_id=1, source_target_pairs={{0,15},{1,2},{2,1},{3,4},{4,3},{5,6},{6,5},{7,8},{8,7},{9,10},{10,... | collective-permute-start | bytes 442376 | tf_op jit(solution)/shard_map/ppermute | solution.py:52
  12.3 11.8 %collective-permute-start.3 = (bf16[256,1536]{1,0:T(8,128)(2,1)}, bf16[256,1536]{1,0:T(8,128)(2,1)S(1)}, u32[]{:S(2)}, u32[]{:S(2)}) collective-permute-start(bf16[256,1536]{1,0:T(8,128)(2,1)} %bitcast.20), channel_id=1, source_target_pairs={{0,1},{1,0},{2,3},{3,2},{4,5},{5,4},{6,7},{7,6},{8,9},{9,8},{10,11... | collective-permute-start | bytes 2359304 | tf_op jit(solution)/shard_map/ppermute | solution.py:40
  14.0 1.1 %copy-start = (bf16[1,256,1536]{2,1,0:T(8,128)(2,1)S(1)}, bf16[1,256,1536]{2,1,0:T(8,128)(2,1)}, u32[]{:S(2)}) copy-start(bf16[1,256,1536]{2,1,0:T(8,128)(2,1)} %param.6) | copy-start | bytes 2359300
  19.9 1.8 %copy-start.2 = (bf16[1,256,1536]{2,1,0:T(8,128)(2,1)S(1)}, bf16[1,256,1536]{2,1,0:T(8,128)(2,1)}, u32[]{:S(2)}) copy-start(bf16[1,256,1536]{2,1,0:T(8,128)(2,1)} %param.7) | copy-start | bytes 2359300
  20.0 2.6 %copy-start.3 = (bf16[1536,1536]{1,0:T(8,128)(2,1)S(1)}, bf16[1536,1536]{1,0:T(8,128)(2,1)}, u32[]{:S(2)}) copy-start(bf16[1536,1536]{1,0:T(8,128)(2,1)} %param.9) | copy-start | bytes 14155780
  21.2 3.0 %collective-permute-start.2 = (bf16[288,1536]{1,0:T(8,128)(2,1)S(1)}, bf16[288,1536]{1,0:T(8,128)(2,1)S(1)}, u32[]{:S(2)}, u32[]{:S(2)}) collective-permute-start(bf16[288,1536]{1,0:T(8,128)(2,1)S(1)} %get-tuple-element.46.hidden), channel_id=1, source_target_pairs={{0,1},{1,0},{2,3},{3,2},{4,5},{5,4},{6,7},{7,6},{8,9},{9,8},{10,11... | collective-permute-start | bytes 2654216 | tf_op jit(solution)/shard_map/ppermute | solution.py:40
  24.6 11.1 %collective-permute-start.5 = (bf16[384,384]{1,0:T(8,128)(2,1)S(1)}, bf16[384,384]{1,0:T(8,128)(2,1)S(1)}, u32[]{:S(2)}, u32[]{:S(2)}) collective-permute-start(bf16[384,384]{1,0:T(8,128)(2,1)S(1)} %get-tuple-element.50._), channel_id=1, source_target_pairs={{0,4},{1,5},{2,6},{3,7},{4,8},{5,9},{6,10},{7,11},{8,12},{9,13},{1... | collective-permute-start | bytes 884744 | tf_op jit(solution)/shard_map/ppermute | solution.py:32
  24.7 11.0 %collective-permute-start.6 = (bf16[384,384]{1,0:T(8,128)(2,1)S(1)}, bf16[384,384]{1,0:T(8,128)(2,1)S(1)}, u32[]{:S(2)}, u32[]{:S(2)}) collective-permute-start(bf16[384,384]{1,0:T(8,128)(2,1)S(1)} %get-tuple-element.56), channel_id=1, source_target_pairs={{0,12},{1,13},{2,14},{3,15},{4,0},{5,1},{6,2},{7,3},{8,4},{9,5},{1... | collective-permute-start | bytes 884744 | tf_op jit(solution)/shard_map/ppermute | solution.py:32
  29.1 13.1 %collective-permute-start.4 = (bf16[384,384]{1,0:T(8,128)(2,1)S(1)}, bf16[384,384]{1,0:T(8,128)(2,1)S(1)}, u32[]{:S(2)}, u32[]{:S(2)}) collective-permute-start(bf16[384,384]{1,0:T(8,128)(2,1)S(1)} %get-tuple-element.53), channel_id=1, source_target_pairs={{0,12},{1,13},{2,14},{3,15},{4,0},{5,1},{6,2},{7,3},{8,4},{9,5},{1... | collective-permute-start | bytes 884744 | tf_op jit(solution)/shard_map/ppermute | solution.py:32
  29.2 16.4 %collective-permute-start.8 = (bf16[384,384]{1,0:T(8,128)(2,1)S(1)}, bf16[384,384]{1,0:T(8,128)(2,1)S(1)}, u32[]{:S(2)}, u32[]{:S(2)}) collective-permute-start(bf16[384,384]{1,0:T(8,128)(2,1)S(1)} %get-tuple-element.59), channel_id=1, source_target_pairs={{0,4},{1,5},{2,6},{3,7},{4,8},{5,9},{6,10},{7,11},{8,12},{9,13},{1... | collective-permute-start | bytes 884744 | tf_op jit(solution)/shard_map/ppermute | solution.py:32
  31.2 1.3 %copy-start.1 = (bf16[1,256,1536]{2,1,0:T(8,128)(2,1)S(1)}, bf16[1,256,1536]{2,1,0:T(8,128)(2,1)}, u32[]{:S(2)}) copy-start(bf16[1,256,1536]{2,1,0:T(8,128)(2,1)} %param.6) | copy-start | bytes 2359300
  35.9 13.7 %collective-permute-start.7 = (bf16[384,384]{1,0:T(8,128)(2,1)S(1)}, bf16[384,384]{1,0:T(8,128)(2,1)S(1)}, u32[]{:S(2)}, u32[]{:S(2)}) collective-permute-start(bf16[384,384]{1,0:T(8,128)(2,1)S(1)} %get-tuple-element.58._), channel_id=1, source_target_pairs={{0,4},{1,5},{2,6},{3,7},{4,8},{5,9},{6,10},{7,11},{8,12},{9,13},{1... | collective-permute-start | bytes 884744 | tf_op jit(solution)/shard_map/ppermute | solution.py:32
  36.1 13.5 %collective-permute-start.9 = (bf16[384,384]{1,0:T(8,128)(2,1)S(1)}, bf16[384,384]{1,0:T(8,128)(2,1)S(1)}, u32[]{:S(2)}, u32[]{:S(2)}) collective-permute-start(bf16[384,384]{1,0:T(8,128)(2,1)S(1)} %get-tuple-element.60), channel_id=1, source_target_pairs={{0,12},{1,13},{2,14},{3,15},{4,0},{5,1},{6,2},{7,3},{8,4},{9,5},{1... | collective-permute-start | bytes 884744 | tf_op jit(solution)/shard_map/ppermute | solution.py:32
  42.1 7.5 %collective-permute-start.10 = (bf16[48,384]{1,0:T(8,128)(2,1)S(1)}, bf16[48,384]{1,0:T(8,128)(2,1)S(1)}, u32[]{:S(2)}, u32[]{:S(2)}) collective-permute-start(bf16[48,384]{1,0:T(8,128)(2,1)S(1)} %get-tuple-element.62), channel_id=1, source_target_pairs={{0,4},{1,5},{2,6},{3,7},{4,8},{5,9},{6,10},{7,11},{8,12},{9,13},{1... | collective-permute-start | bytes 110600 | tf_op jit(solution)/shard_map/ppermute | solution.py:32
  42.2 7.4 %collective-permute-start.11 = (bf16[48,384]{1,0:T(8,128)(2,1)S(1)}, bf16[48,384]{1,0:T(8,128)(2,1)S(1)}, u32[]{:S(2)}, u32[]{:S(2)}) collective-permute-start(bf16[48,384]{1,0:T(8,128)(2,1)S(1)} %get-tuple-element.63), channel_id=1, source_target_pairs={{0,8},{1,9},{2,10},{3,11},{4,12},{5,13},{6,14},{7,15},{8,0},{9,1},... | collective-permute-start | bytes 110600 | tf_op jit(solution)/shard_map/ppermute | solution.py:32
  45.5 4.0 %collective-permute-start.12 = (bf16[48,384]{1,0:T(8,128)(2,1)S(1)}, bf16[48,384]{1,0:T(8,128)(2,1)S(1)}, u32[]{:S(2)}, u32[]{:S(2)}) collective-permute-start(bf16[48,384]{1,0:T(8,128)(2,1)S(1)} %get-tuple-element.64), channel_id=1, source_target_pairs={{0,12},{1,13},{2,14},{3,15},{4,0},{5,1},{6,2},{7,3},{8,4},{9,5},{1... | collective-permute-start | bytes 110600 | tf_op jit(solution)/shard_map/ppermute | solution.py:32
  50.0 1.7 %collective-permute-start.13 = (bf16[208,768]{1,0:T(8,128)(2,1)S(1)}, bf16[208,768]{1,0:T(8,128)(2,1)S(1)}, u32[]{:S(2)}, u32[]{:S(2)}) collective-permute-start(bf16[208,768]{1,0:T(8,128)(2,1)S(1)} %get-tuple-element.66), channel_id=1, source_target_pairs={{0,1},{1,0},{2,3},{3,2},{4,5},{5,4},{6,7},{7,6},{8,9},{9,8},{10,11... | collective-permute-start | bytes 958472 | tf_op jit(solution)/shard_map/ppermute | solution.py:40
  51.8 20.5 %collective-permute-start.14 = (bf16[208,768]{1,0:T(8,128)(2,1)S(1)}, bf16[208,768]{1,0:T(8,128)(2,1)S(1)}, u32[]{:S(2)}, u32[]{:S(2)}) collective-permute-start(bf16[208,768]{1,0:T(8,128)(2,1)S(1)} %get-tuple-element.67._), channel_id=1, source_target_pairs={{0,2},{1,3},{2,0},{3,1},{4,6},{5,7},{6,4},{7,5},{8,10},{9,11},{10,... | collective-permute-start | bytes 958472 | tf_op jit(solution)/shard_map/ppermute | solution.py:36
  72.5 4.6 %collective-permute-start.15 = (bf16[112,384]{1,0:T(8,128)(2,1)S(1)}, bf16[112,384]{1,0:T(8,128)(2,1)S(1)}, u32[]{:S(2)}, u32[]{:S(2)}) collective-permute-start(bf16[112,384]{1,0:T(8,128)(2,1)S(1)} %get-tuple-element.72), channel_id=1, source_target_pairs={{0,64},{16,80},{32,96},{48,112},{64,128},{80,144},{96,160},{112,17... | collective-permute-start | bytes 258056 | tf_op jit(solution)/shard_map/ppermute | solution.py:44
  73.1 6.0 %collective-permute-start.16 = (bf16[112,384]{1,0:T(8,128)(2,1)S(1)}, bf16[112,384]{1,0:T(8,128)(2,1)S(1)}, u32[]{:S(2)}, u32[]{:S(2)}) collective-permute-start(bf16[112,384]{1,0:T(8,128)(2,1)S(1)} %get-tuple-element.73), channel_id=1, source_target_pairs={{0,128},{16,144},{32,160},{48,176},{64,192},{80,208},{96,224},{112... | collective-permute-start | bytes 258056 | tf_op jit(solution)/shard_map/ppermute | solution.py:44
  75.5 5.7 %collective-permute-start.17 = (bf16[112,384]{1,0:T(8,128)(2,1)S(1)}, bf16[112,384]{1,0:T(8,128)(2,1)S(1)}, u32[]{:S(2)}, u32[]{:S(2)}) collective-permute-start(bf16[112,384]{1,0:T(8,128)(2,1)S(1)} %get-tuple-element.74), channel_id=1, source_target_pairs={{0,192},{16,208},{32,224},{48,240},{64,0},{80,16},{96,32},{112,48}... | collective-permute-start | bytes 258056 | tf_op jit(solution)/shard_map/ppermute | solution.py:44
  81.4 5.8 %collective-permute-start.18 = (bf16[112,96]{1,0:T(8,128)(2,1)S(1)}, bf16[112,96]{1,0:T(8,128)(2,1)S(1)}, u32[]{:S(2)}, u32[]{:S(2)}) collective-permute-start(bf16[112,96]{1,0:T(8,128)(2,1)S(1)} %get-tuple-element.76), channel_id=1, source_target_pairs={{0,16},{16,32},{32,48},{48,0},{64,80},{80,96},{96,112},{112,64},{1... | collective-permute-start | bytes 64520 | tf_op jit(solution)/shard_map/ppermute | solution.py:48
  82.4 5.5 %collective-permute-start.19 = (bf16[112,96]{1,0:T(8,128)(2,1)S(1)}, bf16[112,96]{1,0:T(8,128)(2,1)S(1)}, u32[]{:S(2)}, u32[]{:S(2)}) collective-permute-start(bf16[112,96]{1,0:T(8,128)(2,1)S(1)} %get-tuple-element.77), channel_id=1, source_target_pairs={{0,32},{16,48},{32,0},{48,16},{64,96},{80,112},{96,64},{112,80},{1... | collective-permute-start | bytes 64520 | tf_op jit(solution)/shard_map/ppermute | solution.py:48
  82.4 5.6 %collective-permute-start.20 = (bf16[112,96]{1,0:T(8,128)(2,1)S(1)}, bf16[112,96]{1,0:T(8,128)(2,1)S(1)}, u32[]{:S(2)}, u32[]{:S(2)}) collective-permute-start(bf16[112,96]{1,0:T(8,128)(2,1)S(1)} %get-tuple-element.78), channel_id=1, source_target_pairs={{0,48},{16,0},{32,16},{48,32},{64,112},{80,64},{96,80},{112,96},{1... | collective-permute-start | bytes 64520 | tf_op jit(solution)/shard_map/ppermute | solution.py:48

commit v5 on v4

--- a/solution.py
+++ b/solution.py
@@ -151,7 +151,7 @@
         standardise(conv, taps, refs, begin, 112, 2 * HALF + begin, first + HALF + begin, length)
 
 
-def edge_kernel(lengths, top, bottom, chips, beside, taps, _, __, ___, hidden, standard, inverse, x, conv, h, s, i):
+def edge_kernel(lengths, top, bottom, chips, beside, taps, _, __, ___, ____, hidden, standard, inverse, x, conv, h, s, i):
     where = where_of(lengths)
     first, length, core = where[0], where[1], where[2]
     end = first + ROWS
@@ -198,7 +198,7 @@
 KEPT = [pltpu.VMEM((2 * HALF, WIDTH), BF16), pltpu.VMEM((2 * HALF, WIDTH), F32), pltpu.VMEM((2 * HALF, LANES), F32)]
 
 
-def forward_edge(lengths, frames, chips, beside, taps, forward):
+def forward_edge(lengths, frames, chips, beside, taps, forward, after):
     def ends(i):
         return (1 + 15 * i, 0)
 
@@ -216,6 +216,7 @@
             ANY,
             ANY,
             ANY,
+            ANY,
         ],
         out_specs=(
             pl.BlockSpec((HALF, WIDTH), ends),
@@ -227,7 +228,7 @@
         compiler_params=LIMIT,
         cost_estimate=pl.CostEstimate(flops=8_000_000, bytes_accessed=1_000_000, transcendentals=100_000),
         name="forward_edge",
-    )(lengths, frames, frames, chips, beside, taps, *forward)
+    )(lengths, frames, frames, chips, beside, taps, *forward, after)
 
 
 def backward_rows(first, length, upstream, begin, standard, row, inverse, taps, conv_grad, out_row, size, scaled):
@@ -529,45 +530,53 @@
     )
 
 
-def chips_kernel(own, other, keep, send, extra):
+PIECE = BLOCK // 2
+PACKED = (PIECE, 4 * (WIDTH // 2) + LANES)
+TAIL = pl.ds(4 * (WIDTH // 2), LANES)
+
+
+def chips_kernel(own, other, keep, send, extra, tail):
     place = place_of()
-    z_hi, core = place[2], place[1]
+    z_hi, core, half = place[2], place[1], WIDTH // 2
     more = pl.ds(HALVES, EXTRA)
     extra[...] = own[more, :] + other[more, :].astype(F32)
     for out, z in ((keep, z_hi), (send, 1 - z_hi)):
-        rows = pl.ds(pl.multiple_of(z * BLOCK, BLOCK), BLOCK)
-        out[pl.ds(pl.multiple_of(core * BLOCK, BLOCK), BLOCK), :] = own[rows, :].astype(out.dtype)
-        out[pl.ds(pl.multiple_of((1 - core) * BLOCK, BLOCK), BLOCK), :] = other[rows, :].astype(out.dtype)
-        value = extra[pl.ds(pl.multiple_of(8 * z, 8), 8), :]
-        out[more, :] = jnp.concatenate([value, jnp.zeros((8, WIDTH // 2), F32)], axis=0).astype(out.dtype)
+        for source, c in ((own, core), (other, 1 - core)):
+            for i in range(2):
+                rows = pl.ds(pl.multiple_of(z * BLOCK + i * PIECE, PIECE), PIECE)
+                columns = pl.ds(pl.multiple_of((2 * c + i) * half, half), half)
+                out[:, columns] = source[rows, :].astype(out.dtype)
+        tail[...] = jnp.zeros(tail.shape, F32)
+        rows = pl.ds(pl.multiple_of(8 * z, 8), 8)
+        for q in range(5):
+            tail[pl.ds(8 * q, 8), pl.ds(0, BLOCK)] = extra[rows, pl.ds(q * BLOCK, BLOCK)]
+        out[:, TAIL] = tail[...].astype(out.dtype)
 
 
 def chip_blocks(own, other):
     return small_call(
         chips_kernel,
         "chip_blocks",
-        (rows_of(HELD, F32), rows_of(HELD, BF16)),
+        (rows_of(PACKED, F32), rows_of(PACKED, BF16)),
         (own, other),
         [VMEM, VMEM],
-        [pltpu.VMEM((EXTRA, WIDTH // 2), F32)],
+        [pltpu.VMEM((EXTRA, WIDTH // 2), F32), pltpu.VMEM((PIECE, LANES), F32)],
     )
 
 
 def squares_kernel(mine, other, _, keep, one, two, three, square, extra):
-    place = place_of()
-    x = place[3]
-    for half in range(2):
-        rows = pl.ds(half * BLOCK, BLOCK)
-        value = mine[rows, :] + other[rows, :].astype(F32)
-        square[pl.ds(0, BLOCK), pl.ds(half * (WIDTH // 2), WIDTH // 2)] = value * value
-    rows, more = pl.ds(HALVES, EXTRA), pl.ds(BLOCK, EXTRA)
-    sums = mine[rows, :] + other[rows, :].astype(F32)
+    x, half = lax.axis_index("dp") >> 2, WIDTH // 2
+    for block in range(4):
+        columns = pl.ds(block * half, half)
+        value = mine[:, columns] + other[:, columns].astype(F32)
+        square[pl.ds(block % 2 * PIECE, PIECE), pl.ds(block // 2 * half, half)] = value * value
+    sums = mine[:, TAIL] + other[:, TAIL].astype(F32)
     extra[...] = sums * sums
-    square[more, :] = jnp.zeros((EXTRA, WIDTH), F32)
+    square[pl.ds(BLOCK, EXTRA), :] = jnp.zeros((EXTRA, WIDTH), F32)
     for dp in range(16):
         columns = pl.ds(dp * BLOCK, BLOCK)
-        square[pl.ds(BLOCK, 2), columns] = extra[pl.ds(2 * (dp % 4), 2), pl.ds(dp // 4 * BLOCK, BLOCK)]
-        square[pl.ds(BLOCK + 2, 1), columns] = extra[pl.ds(0, 1), pl.ds(4 * BLOCK, BLOCK)]
+        square[pl.ds(BLOCK, 2), columns] = extra[pl.ds(2 * dp, 2), pl.ds(0, BLOCK)]
+        square[pl.ds(BLOCK + 2, 1), columns] = extra[pl.ds(KW, 1), pl.ds(0, BLOCK)]
     for step, out in enumerate((keep, one, two, three)):
         columns = pl.ds(pl.multiple_of(lax.rem(x + step, 4) * QUARTER, QUARTER), QUARTER)
         out[...] = square[:, columns].astype(out.dtype)
@@ -581,7 +590,7 @@
         (rows_of(shape, F32),) + (rows_of(shape, BF16),) * 3,
         (mine, other, after),
         [VMEM, VMEM, ANY],
-        [pltpu.VMEM((BLOCK + EXTRA, WIDTH), F32), pltpu.VMEM((EXTRA, WIDTH // 2), F32)],
+        [pltpu.VMEM((BLOCK + EXTRA, WIDTH), F32), pltpu.VMEM((PIECE, LANES), F32)],
     )
 
 
@@ -641,15 +650,15 @@
     beside = move_core(jnp.where(core == 0, end, begin))
     cot_other = move_core(cot)
     forward = forward_inner(lengths, frames, taps)
-    hidden, standard, inverse = forward_edge(lengths, frames, chips, beside, taps, forward)
+    hidden, standard, inverse = forward_edge(lengths, frames, chips, beside, taps, forward, cot_other)
     hidden_other = move_core(hidden)
     low = jnp.where(core == 0, chips[2 * HALF :], beside[2 * HALF :])
     high = jnp.where(core == 0, beside[2 * HALF :], chips[2 * HALF :])
-    late_cot, _ = lax.optimization_barrier((jnp.concatenate([low, cot, high], axis=0), hidden))
+    operands = (hidden, hidden_other, cot, cot_other)
+    far_a, far_b = far_products(*operands, low)
+    late_cot, far_a, far_b = lax.optimization_barrier((jnp.concatenate([low, cot, high], axis=0), far_a, far_b))
     upstream = lax.dot_general(late_cot, out_weight, (((1,), (1,)), ((), ())), preferred_element_type=F32)
-    operands = (hidden, hidden_other, cot, cot_other)
-    far_a, far_b = far_products(*operands, upstream)
-    above_a, above_b, below_a, below_b, own = near_products(*operands, far_a)
+    above_a, above_b, below_a, below_b, own = near_products(*operands, upstream)
     up_a = move_y(far_a, 1)
     down_b = move_y(far_b, -1)
     up_b = move_y(above_b, 1)

time: 88.8 us -> 88.6 us (level)
  starting transfers between devices: 35.2 us -> 36.1 us
    ppermute x4, waiting for transfers between devices: 1.61 us -> 3.56 us  [move_core(): lax.ppermute(value, 'seq', [(seq_at(*p), seq_at(p[0], p[1], p[2] + 1)) fo...]
    ppermute x3, starting transfers between devices: 3.9 us -> 5.64 us  [move_z_lo(): lax.ppermute(value, 'dp', [(x * 4 + z, x * 4 + (z + step) % 4) for x, z i...]
    ppermute x1, waiting for transfers between devices: 8.58 us -> 7.39 us  [move_z_hi(): lax.ppermute(value, 'seq', [(seq_at(*p), seq_at(p[0], p[1] + 1, p[2])) fo...]
    ppermute x3, waiting for transfers between devices: 2.66 us -> 1.56 us  [move_z_lo(): lax.ppermute(value, 'dp', [(x * 4 + z, x * 4 + (z + step) % 4) for x, z i...]
  transfers between devices with their start and end apart: 21 -> 21, of which waited for: 10 -> 11; matrix products, arithmetic and copies ran while one was open for 3% -> 5% of each run, Pallas kernels for 24% -> 22%
where the time goes in v5:
time: 88.6 us; the launch traced here: 88.4 us
  starting transfers between devices  36.1 us (41%)
  Pallas kernels  23 us (26%)
  waiting for transfers between devices  22.2 us (25%)
  local copies, waits for them, and re-layouts  2.93 us (3%)
  matrix products  1.56 us (2%)
  between operations  1.52 us (2%)
  other arithmetic  1.15 us (1%)
    ppermute x9, starting transfers between devices, move_y(): lax.ppermute(value, 'seq', [(seq_at(*p), seq_at(p[0] + step, p[1], p[2]))...  12.8 us
    ppermute x1, starting transfers between devices, move_neighbour(): lax.ppermute(value, 'seq', [(i, (i + 1) % 16 if i % 2 else (i - 1) % 16)...  9.82 us
    ppermute x1, waiting for transfers between devices, move_z_hi(): lax.ppermute(value, 'seq', [(seq_at(*p), seq_at(p[0], p[1] + 1, p[2])) fo...  7.39 us
    pallas_call x1, Pallas kernels, input_grads(): pl.pallas_call(input_grad_kernel, out_shape=(rows_of((ROWS, WIDTH), BF16)...  5.96 us
    ppermute x3, waiting for transfers between devices, move_x(): lax.ppermute(value, 'dp', [(x * 4 + z, (x + step) % 4 * 4 + z) for x, z i...  5.68 us
    ppermute x3, starting transfers between devices, move_z_lo(): lax.ppermute(value, 'dp', [(x * 4 + z, x * 4 + (z + step) % 4) for x, z i...  5.64 us
    pallas_call x1, Pallas kernels, forward_inner(): pl.pallas_call(inner_kernel, out_shape=FORWARD, in_specs=[SMEM, VMEM, VME...  4.77 us
    ppermute x1, starting transfers between devices, move_z_hi(): lax.ppermute(value, 'seq', [(seq_at(*p), seq_at(p[0], p[1] + 1, p[2])) fo...  4.08 us
  transfers between devices with their start and end apart: 21, of which 11 were waited for; matrix products, arithmetic and copies ran while one was open for 5% of the time, Pallas kernels for 22%

profile of v5, /device:TPU:6, one launch (start us, length us, event | category | flops | bytes accessed | tf_op | source)
XLA Modules:
  0.0 88.4 jit_solution(18286465648671716081)
XLA Ops:
  0.6 0.1 collective-permute-start.2
  0.7 0.8 slice_bitcast_fusion.3
  1.6 1.0 %slice_bitcast_fusion.1 = (bf16[32,1536]{1,0:T(8,128)(2,1)S(1)}, bf16[32,1536]{1,0:T(8,128)(2,1)S(1)}) fusion(bf16[1,256,1536]{2,1,0:T(8,128)(2,1)} %param.6), kind=kLoop, calls=%fused_computation.7 | loop fusion | bytes 393216 | tf_op jit(solution)/shard_map/slice | solution.py:647
  2.5 0.1 broadcast_select_fusion.1
  2.6 9.8 %collective-permute-start = (bf16[48,1536]{1,0:T(8,128)(2,1)S(1)}, bf16[48,1536]{1,0:T(8,128)(2,1)S(1)}, u32[]{:S(2)}, u32[]{:S(2)}) collective-permute-start(bf16[48,1536]{1,0:T(8,128)(2,1)S(1)} %get-tuple-element.92), channel_id=1, source_target_pairs={{0,15},{1,2},{2,1},{3,4},{4,3},{5,6},{6,5},{7,8},{8,7},{9,10},{10,... | collective-permute-start | bytes 442376 | tf_op jit(solution)/shard_map/ppermute | solution.py:52
  12.4 0.0 collective-permute-start.1
  12.4 1.0 %pad_select_fusion.taps = f32[33,1536]{1,0:T(8,128)S(1)} fusion(f32[32,1536]{1,0:T(8,128)} %param.10, f32[1536]{0:T(1024)} %param.11, pred[33]{0:T(512)(128)(4,1)S(1)} %iota_compare_fusion), kind=kLoop, calls=%fused_computation.1 | loop fusion | flops 50688 | bytes 405537 | tf_op jit(solution)/shard_map/jit(_where)/select_n | solution.py:646
  14.1 0.0 copy-start
  14.1 1.1 %copy-done = bf16[1,256,1536]{2,1,0:T(8,128)(2,1)S(1)} copy-done((bf16[1,256,1536]{2,1,0:T(8,128)(2,1)S(1)}, bf16[1,256,1536]{2,1,0:T(8,128)(2,1)}, u32[]{:S(2)}) %copy-start) | copy-done | bytes 786456
  15.2 4.8 %forward_inner.1 = (bf16[288,1536]{1,0:T(8,128)(2,1)S(1)}, f32[288,1536]{1,0:T(8,128)S(1)}, f32[288,128]{1,0:T(8,128)S(1)}) custom-call(s32[1]{0:T(128)S(6)} %copy.16.lengths, bf16[256,1536]{1,0:T(8,128)(2,1)S(1)} %bitcast.14, f32[33,1536]{1,0:T(8,128)S(1)} %pad_select_fusion.taps), custom_call_target="tpu_custom_call" | custom-call | flops 60000000 | bytes 4000000 | tf_op jit(solution)/shard_map/forward_inner/pallas_call | solution.py:180
  20.0 0.0 collective-permute-done.chips
  20.0 0.0 collective-permute-done.1.beside
  20.0 0.0 collective-permute-done.2.____.cot_other
  20.0 0.0 copy-start.2
  20.0 1.2 %forward_edge.1 = (bf16[288,1536]{1,0:T(8,128)(2,1)S(1)}, f32[288,1536]{1,0:T(8,128)S(1)}, f32[288,128]{1,0:T(8,128)S(1)}) custom-call(s32[1]{0:T(128)S(6)} %copy.16.lengths, bf16[256,1536]{1,0:T(8,128)(2,1)S(1)} %bitcast.15, bf16[256,1536]{1,0:T(8,128)(2,1)S(1)} %bitcast.16, ...), custom_call_target="tpu_custom_call", output_to_operand_aliasing={{0}: (6, {}), {1}: (7, {}), {2}: (8, {})} | custom-call | flops 8000000 | bytes 1000000 | tf_op jit(solution)/shard_map/forward_edge/pallas_call | solution.py:205
  21.2 0.6 collective-permute-start.3
  21.9 0.0 copy-start.3
  21.9 0.1 pad_maximum_fusion
  21.9 1.9 %collective-permute-done.3.hidden_other = bf16[288,1536]{1,0:T(8,128)(2,1)S(1)} collective-permute-done((bf16[288,1536]{1,0:T(8,128)(2,1)S(1)}, bf16[288,1536]{1,0:T(8,128)(2,1)S(1)}, u32[]{:S(2)}, u32[]{:S(2)}) %collective-permute-start.3) | collective-permute-done | bytes 884768 | tf_op jit(solution)/shard_map/ppermute | solution.py:40
  23.9 0.5 far_products.1
  24.4 0.1 collective-permute-start.5
  24.5 3.2 %collective-permute-start.6 = (bf16[384,384]{1,0:T(8,128)(2,1)S(1)}, bf16[384,384]{1,0:T(8,128)(2,1)S(1)}, u32[]{:S(2)}, u32[]{:S(2)}) collective-permute-start(bf16[384,384]{1,0:T(8,128)(2,1)S(1)} %get-tuple-element.60), channel_id=1, source_target_pairs={{0,12},{1,13},{2,14},{3,15},{4,0},{5,1},{6,2},{7,3},{8,4},{9,5},{1... | collective-permute-start | bytes 884744 | tf_op jit(solution)/shard_map/ppermute | solution.py:32
  27.7 1.6 %fusion._.upstream = f32[288,1536]{1,0:T(8,128)S(1)} fusion(bf16[288,1536]{1,0:T(8,128)(2,1)S(1)} %pad_maximum_fusion, bf16[1536,1536]{1,0:T(8,128)(2,1)S(1)} %copy-done.3), kind=kOutput, calls=%fused_computation.13 | convolution fusion | flops 1358954496 | bytes 7372800 | tf_op jit(solution)/shard_map/dot_general | solution.py:660
  29.3 1.1 %near_products.1 = (f32[384,384]{1,0:T(8,128)S(1)}, bf16[384,384]{1,0:T(8,128)(2,1)S(1)}, bf16[384,384]{1,0:T(8,128)(2,1)S(1)}, f32[384,384]{1,0:T(8,128)S(1)}, f32[384,768]{1,0:T(8,128)S(1)}) custom-call(bf16[288,1536]{1,0:T(8,128)(2,1)S(1)} %get-tuple-element.48.hidden, bf16[288,1536]{1,0:T(8,128)(2,1)S(1)} %collective-permute-done.3.hidden_other, ...), custom_call_target="tpu_custom_call" | custom-call | flops 500000 | bytes 1500000 | tf_op jit(solution)/shard_map/near_products/pallas_call | solution.py:430
  30.4 0.1 collective-permute-start.4
  30.5 2.0 %collective-permute-start.8 = (bf16[384,384]{1,0:T(8,128)(2,1)S(1)}, bf16[384,384]{1,0:T(8,128)(2,1)S(1)}, u32[]{:S(2)}, u32[]{:S(2)}) collective-permute-start(bf16[384,384]{1,0:T(8,128)(2,1)S(1)} %get-tuple-element.63), channel_id=1, source_target_pairs={{0,4},{1,5},{2,6},{3,7},{4,8},{5,9},{6,10},{7,11},{8,12},{9,13},{1... | collective-permute-start | bytes 884744 | tf_op jit(solution)/shard_map/ppermute | solution.py:32
  32.5 1.3 %backward.1 = (bf16[256,1536]{1,0:T(8,128)(2,1)S(1)}, f32[8,1536]{1,0:T(8,128)S(1)}) custom-call(s32[1]{0:T(128)S(6)} %copy.16.lengths, f32[288,1536]{1,0:T(8,128)S(1)} %fusion._.upstream, f32[288,1536]{1,0:T(8,128)S(1)} %get-tuple-element.52.standard, f32[288,128]{1,0:T(8,128)S(1)} %get-tuple-element.53.inverse, f32[33,1536]{1,0:T(8,128)S(1)} %pad_select_fusion.taps, ...), custom_call_target="tpu_custom_call" | custom-call | flops 10000000 | bytes 4000000 | tf_op jit(solution)/shard_map/backward/pallas_call | solution.py:272
  33.8 2.6 %kernel_grads_first.1._.first = f32[40,768]{1,0:T(8,128)S(1)} custom-call(s32[1]{0:T(128)S(6)} %copy.16.lengths, bf16[256,1536]{1,0:T(8,128)(2,1)S(1)} %bitcast.17, bf16[48,1536]{1,0:T(8,128)(2,1)S(1)} %collective-permute-done.chips, bf16[48,1536]{1,0:T(8,128)(2,1)S(1)} %collective-permute-done.1.beside, bf16[256,1536]{1,0:T(8,128)(2,1)S(1)} %get-tuple-element.55.conv_grad, ...), custom_call_target="tpu_custom_call" | custom-call | flops 25000000 | bytes 1000000 | tf_op jit(solution)/shard_map/kernel_grads_first/pallas_call | solution.py:377
  36.4 0.0 collective-permute-done.5.up_a
  36.4 0.1 seconds.1
  36.6 2.6 %collective-permute-start.9 = (bf16[384,384]{1,0:T(8,128)(2,1)S(1)}, bf16[384,384]{1,0:T(8,128)(2,1)S(1)}, u32[]{:S(2)}, u32[]{:S(2)}) collective-permute-start(bf16[384,384]{1,0:T(8,128)(2,1)S(1)} %get-tuple-element.64), channel_id=1, source_target_pairs={{0,12},{1,13},{2,14},{3,15},{4,0},{5,1},{6,2},{7,3},{8,4},{9,5},{1... | collective-permute-start | bytes 884744 | tf_op jit(solution)/shard_map/ppermute | solution.py:32
  39.2 2.6 %kernel_grads_other.1 = (f32[48,384]{1,0:T(8,128)S(1)}, bf16[48,384]{1,0:T(8,128)(2,1)S(1)}, bf16[48,384]{1,0:T(8,128)(2,1)S(1)}, bf16[48,384]{1,0:T(8,128)(2,1)S(1)}) custom-call(s32[1]{0:T(128)S(6)} %copy.16.lengths, bf16[256,1536]{1,0:T(8,128)(2,1)S(1)} %bitcast.18, bf16[48,1536]{1,0:T(8,128)(2,1)S(1)} %collective-permute-done.chips, ...), custom_call_target="tpu_custom_call" | custom-call | flops 25000000 | bytes 1000000 | tf_op jit(solution)/shard_map/kernel_grads_other/pallas_call | solution.py:390
  41.8 0.1 collective-permute-start.10
  41.9 0.0 collective-permute-done.4.down_a
  41.9 4.7 %collective-permute-start.11 = (bf16[48,384]{1,0:T(8,128)(2,1)S(1)}, bf16[48,384]{1,0:T(8,128)(2,1)S(1)}, u32[]{:S(2)}, u32[]{:S(2)}) collective-permute-start(bf16[48,384]{1,0:T(8,128)(2,1)S(1)} %get-tuple-element.67), channel_id=1, source_target_pairs={{0,8},{1,9},{2,10},{3,11},{4,12},{5,13},{6,14},{7,15},{8,0},{9,1},... | collective-permute-start | bytes 110600 | tf_op jit(solution)/shard_map/ppermute | solution.py:32
  46.6 0.0 collective-permute-done.8.up_b
  46.6 0.0 collective-permute-start.12
  46.6 2.6 %collective-permute-done.10.k1 = bf16[48,384]{1,0:T(8,128)(2,1)S(1)} collective-permute-done((bf16[48,384]{1,0:T(8,128)(2,1)S(1)}, bf16[48,384]{1,0:T(8,128)(2,1)S(1)}, u32[]{:S(2)}, u32[]{:S(2)}) %collective-permute-start.10) | collective-permute-done | bytes 36896 | tf_op jit(solution)/shard_map/ppermute | solution.py:32
  49.2 0.0 collective-permute-done.11.k2
  49.2 1.3 %collective-permute-done.12.k3 = bf16[48,384]{1,0:T(8,128)(2,1)S(1)} collective-permute-done((bf16[48,384]{1,0:T(8,128)(2,1)S(1)}, bf16[48,384]{1,0:T(8,128)(2,1)S(1)}, u32[]{:S(2)}, u32[]{:S(2)}) %collective-permute-start.12) | collective-permute-done | bytes 36896 | tf_op jit(solution)/shard_map/ppermute | solution.py:32
  50.5 0.0 collective-permute-done.9.down_b
  50.5 0.4 blocks.1
  50.9 0.1 collective-permute-start.13
  51.0 1.6 %collective-permute-done.13.other = bf16[208,768]{1,0:T(8,128)(2,1)S(1)} collective-permute-done((bf16[208,768]{1,0:T(8,128)(2,1)S(1)}, bf16[208,768]{1,0:T(8,128)(2,1)S(1)}, u32[]{:S(2)}, u32[]{:S(2)}) %collective-permute-start.13) | collective-permute-done | bytes 319520 | tf_op jit(solution)/shard_map/ppermute | solution.py:40
  52.6 0.1 chip_blocks.1
  52.8 4.1 %collective-permute-start.14 = (bf16[48,3200]{1,0:T(8,128)(2,1)S(1)}, bf16[48,3200]{1,0:T(8,128)(2,1)S(1)}, u32[]{:S(2)}, u32[]{:S(2)}) collective-permute-start(bf16[48,3200]{1,0:T(8,128)(2,1)S(1)} %get-tuple-element.71._), channel_id=1, source_target_pairs={{0,2},{1,3},{2,0},{3,1},{4,6},{5,7},{6,4},{7,5},{8,10},{9,11},{10,... | collective-permute-start | bytes 921608 | tf_op jit(solution)/shard_map/ppermute | solution.py:36
  56.9 1.3 %outer_grads.1.outer = bf16[32,1536]{1,0:T(8,128)(2,1)S(1)} custom-call(s32[1]{0:T(128)S(6)} %copy.16.lengths, bf16[256,1536]{1,0:T(8,128)(2,1)S(1)} %bitcast.19, bf16[48,1536]{1,0:T(8,128)(2,1)S(1)} %collective-permute-done.chips, bf16[48,1536]{1,0:T(8,128)(2,1)S(1)} %collective-permute-done.1.beside, f32[33,1536]{1,0:T(8,128)S(1)} %pad_select_fusion.taps, ...), custom_call_target="tpu_custom_call" | custom-call | flops 8000000 | bytes 1000000 | tf_op jit(solution)/shard_map/outer_grads/pallas_call | solution.py:301
  58.1 6.0 %input_grads.1 = (bf16[256,1536]{1,0:T(8,128)(2,1)}, f32[8,128]{1,0:T(8,128)S(1)}) custom-call(s32[1]{0:T(128)S(6)} %copy.16.lengths, bf16[256,1536]{1,0:T(8,128)(2,1)S(1)} %get-tuple-element.55.conv_grad, bf16[32,1536]{1,0:T(8,128)(2,1)S(1)} %outer_grads.1.outer, f32[33,1536]{1,0:T(8,128)S(1)} %pad_select_fusion.taps, bf16[48,3200]{1,0:T(8,128)(2,1)S(1)} %get-tuple-element.71._), custom_call_target="tpu_custom_call" | custom-call | flops 50000000 | bytes 2000000 | tf_op jit(solution)/shard_map/input_grads/pallas_call | solution.py:417
  64.1 7.4 %collective-permute-done.14.other = bf16[48,3200]{1,0:T(8,128)(2,1)S(1)} collective-permute-done((bf16[48,3200]{1,0:T(8,128)(2,1)S(1)}, bf16[48,3200]{1,0:T(8,128)(2,1)S(1)}, u32[]{:S(2)}, u32[]{:S(2)}) %collective-permute-start.14) | collective-permute-done | bytes 307232 | tf_op jit(solution)/shard_map/ppermute | solution.py:36
  71.5 0.2 squares.1
  71.7 0.6 collective-permute-start.15
  72.3 2.4 %collective-permute-start.16 = (bf16[112,384]{1,0:T(8,128)(2,1)S(1)}, bf16[112,384]{1,0:T(8,128)(2,1)S(1)}, u32[]{:S(2)}, u32[]{:S(2)}) collective-permute-start(bf16[112,384]{1,0:T(8,128)(2,1)S(1)} %get-tuple-element.77), channel_id=1, source_target_pairs={{0,128},{16,144},{32,160},{48,176},{64,192},{80,208},{96,224},{112... | collective-permute-start | bytes 258056 | tf_op jit(solution)/shard_map/ppermute | solution.py:44
  74.7 0.0 collective-permute-start.17
  74.7 1.7 %collective-permute-done.15.one = bf16[112,384]{1,0:T(8,128)(2,1)S(1)} collective-permute-done((bf16[112,384]{1,0:T(8,128)(2,1)S(1)}, bf16[112,384]{1,0:T(8,128)(2,1)S(1)}, u32[]{:S(2)}, u32[]{:S(2)}) %collective-permute-start.15) | collective-permute-done | bytes 86048 | tf_op jit(solution)/shard_map/ppermute | solution.py:44
  76.4 2.7 %collective-permute-done.16.two = bf16[112,384]{1,0:T(8,128)(2,1)S(1)} collective-permute-done((bf16[112,384]{1,0:T(8,128)(2,1)S(1)}, bf16[112,384]{1,0:T(8,128)(2,1)S(1)}, u32[]{:S(2)}, u32[]{:S(2)}) %collective-permute-start.16) | collective-permute-done | bytes 86048 | tf_op jit(solution)/shard_map/ppermute | solution.py:44
  79.0 1.4 %collective-permute-done.17.three = bf16[112,384]{1,0:T(8,128)(2,1)S(1)} collective-permute-done((bf16[112,384]{1,0:T(8,128)(2,1)S(1)}, bf16[112,384]{1,0:T(8,128)(2,1)S(1)}, u32[]{:S(2)}, u32[]{:S(2)}) %collective-permute-start.17) | collective-permute-done | bytes 86048 | tf_op jit(solution)/shard_map/ppermute | solution.py:44
  80.4 0.2 quarters.1
  80.6 2.3 %collective-permute-start.18 = (bf16[112,96]{1,0:T(8,128)(2,1)S(1)}, bf16[112,96]{1,0:T(8,128)(2,1)S(1)}, u32[]{:S(2)}, u32[]{:S(2)}) collective-permute-start(bf16[112,96]{1,0:T(8,128)(2,1)S(1)} %get-tuple-element.80), channel_id=1, source_target_pairs={{0,16},{16,32},{32,48},{48,0},{64,80},{80,96},{96,112},{112,64},{1... | collective-permute-start | bytes 64520 | tf_op jit(solution)/shard_map/ppermute | solution.py:48
  82.8 0.6 collective-permute-start.19
  83.4 2.8 %collective-permute-start.20 = (bf16[112,96]{1,0:T(8,128)(2,1)S(1)}, bf16[112,96]{1,0:T(8,128)(2,1)S(1)}, u32[]{:S(2)}, u32[]{:S(2)}) collective-permute-start(bf16[112,96]{1,0:T(8,128)(2,1)S(1)} %get-tuple-element.82), channel_id=1, source_target_pairs={{0,48},{16,0},{32,16},{48,32},{64,112},{80,64},{96,80},{112,96},{1... | collective-permute-start | bytes 64520 | tf_op jit(solution)/shard_map/ppermute | solution.py:48
  86.2 0.3 collective-permute-done.18.one
  86.5 1.0 %collective-permute-done.19.two = bf16[112,96]{1,0:T(8,128)(2,1)S(1)} collective-permute-done((bf16[112,96]{1,0:T(8,128)(2,1)S(1)}, bf16[112,96]{1,0:T(8,128)(2,1)S(1)}, u32[]{:S(2)}, u32[]{:S(2)}) %collective-permute-start.19) | collective-permute-done | bytes 21536 | tf_op jit(solution)/shard_map/ppermute | solution.py:48
  87.6 0.2 collective-permute-done.20.three
  87.8 0.6 means.1
  (9 shorter events, 0.0 us)
Async XLA Ops:
  0.6 19.4 %collective-permute-start.2 = (bf16[256,1536]{1,0:T(8,128)(2,1)}, bf16[256,1536]{1,0:T(8,128)(2,1)S(1)}, u32[]{:S(2)}, u32[]{:S(2)}) collective-permute-start(bf16[256,1536]{1,0:T(8,128)(2,1)} %bitcast.20), channel_id=1, source_target_pairs={{0,1},{1,0},{2,3},{3,2},{4,5},{5,4},{6,7},{7,6},{8,9},{9,8},{10,11... | collective-permute-start | bytes 2359304 | tf_op jit(solution)/shard_map/ppermute | solution.py:40
  2.6 17.4 %collective-permute-start = (bf16[48,1536]{1,0:T(8,128)(2,1)S(1)}, bf16[48,1536]{1,0:T(8,128)(2,1)S(1)}, u32[]{:S(2)}, u32[]{:S(2)}) collective-permute-start(bf16[48,1536]{1,0:T(8,128)(2,1)S(1)} %get-tuple-element.92), channel_id=1, source_target_pairs={{0,15},{1,2},{2,1},{3,4},{4,3},{5,6},{6,5},{7,8},{8,7},{9,10},{10,... | collective-permute-start | bytes 442376 | tf_op jit(solution)/shard_map/ppermute | solution.py:52
  12.4 7.6 %collective-permute-start.1 = (bf16[48,1536]{1,0:T(8,128)(2,1)S(1)}, bf16[48,1536]{1,0:T(8,128)(2,1)S(1)}, u32[]{:S(2)}, u32[]{:S(2)}) collective-permute-start(bf16[48,1536]{1,0:T(8,128)(2,1)S(1)} %get-tuple-element.93), channel_id=1, source_target_pairs={{0,1},{1,0},{2,3},{3,2},{4,5},{5,4},{6,7},{7,6},{8,9},{9,8},{10,11... | collective-permute-start | bytes 442376 | tf_op jit(solution)/shard_map/ppermute | solution.py:40
  14.1 1.1 %copy-start = (bf16[1,256,1536]{2,1,0:T(8,128)(2,1)S(1)}, bf16[1,256,1536]{2,1,0:T(8,128)(2,1)}, u32[]{:S(2)}) copy-start(bf16[1,256,1536]{2,1,0:T(8,128)(2,1)} %param.6) | copy-start | bytes 2359300
  20.0 1.8 %copy-start.2 = (bf16[1,256,1536]{2,1,0:T(8,128)(2,1)S(1)}, bf16[1,256,1536]{2,1,0:T(8,128)(2,1)}, u32[]{:S(2)}) copy-start(bf16[1,256,1536]{2,1,0:T(8,128)(2,1)} %param.7) | copy-start | bytes 2359300
  21.2 2.6 %collective-permute-start.3 = (bf16[288,1536]{1,0:T(8,128)(2,1)S(1)}, bf16[288,1536]{1,0:T(8,128)(2,1)S(1)}, u32[]{:S(2)}, u32[]{:S(2)}) collective-permute-start(bf16[288,1536]{1,0:T(8,128)(2,1)S(1)} %get-tuple-element.48.hidden), channel_id=1, source_target_pairs={{0,1},{1,0},{2,3},{3,2},{4,5},{5,4},{6,7},{7,6},{8,9},{9,8},{10,11... | collective-permute-start | bytes 2654216 | tf_op jit(solution)/shard_map/ppermute | solution.py:40
  21.9 5.9 %copy-start.3 = (bf16[1536,1536]{1,0:T(8,128)(2,1)S(1)}, bf16[1536,1536]{1,0:T(8,128)(2,1)}, u32[]{:S(2)}) copy-start(bf16[1536,1536]{1,0:T(8,128)(2,1)} %param.9) | copy-start | bytes 14155780
  24.4 12.0 %collective-permute-start.5 = (bf16[384,384]{1,0:T(8,128)(2,1)S(1)}, bf16[384,384]{1,0:T(8,128)(2,1)S(1)}, u32[]{:S(2)}, u32[]{:S(2)}) collective-permute-start(bf16[384,384]{1,0:T(8,128)(2,1)S(1)} %get-tuple-element.58), channel_id=1, source_target_pairs={{0,4},{1,5},{2,6},{3,7},{4,8},{5,9},{6,10},{7,11},{8,12},{9,13},{1... | collective-permute-start | bytes 884744 | tf_op jit(solution)/shard_map/ppermute | solution.py:32
  24.5 11.9 %collective-permute-start.6 = (bf16[384,384]{1,0:T(8,128)(2,1)S(1)}, bf16[384,384]{1,0:T(8,128)(2,1)S(1)}, u32[]{:S(2)}, u32[]{:S(2)}) collective-permute-start(bf16[384,384]{1,0:T(8,128)(2,1)S(1)} %get-tuple-element.60), channel_id=1, source_target_pairs={{0,12},{1,13},{2,14},{3,15},{4,0},{5,1},{6,2},{7,3},{8,4},{9,5},{1... | collective-permute-start | bytes 884744 | tf_op jit(solution)/shard_map/ppermute | solution.py:32
  30.4 11.5 %collective-permute-start.4 = (bf16[384,384]{1,0:T(8,128)(2,1)S(1)}, bf16[384,384]{1,0:T(8,128)(2,1)S(1)}, u32[]{:S(2)}, u32[]{:S(2)}) collective-permute-start(bf16[384,384]{1,0:T(8,128)(2,1)S(1)} %get-tuple-element.56), channel_id=1, source_target_pairs={{0,12},{1,13},{2,14},{3,15},{4,0},{5,1},{6,2},{7,3},{8,4},{9,5},{1... | collective-permute-start | bytes 884744 | tf_op jit(solution)/shard_map/ppermute | solution.py:32
  30.5 16.0 %collective-permute-start.8 = (bf16[384,384]{1,0:T(8,128)(2,1)S(1)}, bf16[384,384]{1,0:T(8,128)(2,1)S(1)}, u32[]{:S(2)}, u32[]{:S(2)}) collective-permute-start(bf16[384,384]{1,0:T(8,128)(2,1)S(1)} %get-tuple-element.63), channel_id=1, source_target_pairs={{0,4},{1,5},{2,6},{3,7},{4,8},{5,9},{6,10},{7,11},{8,12},{9,13},{1... | collective-permute-start | bytes 884744 | tf_op jit(solution)/shard_map/ppermute | solution.py:32
  32.5 1.3 %copy-start.1 = (bf16[1,256,1536]{2,1,0:T(8,128)(2,1)S(1)}, bf16[1,256,1536]{2,1,0:T(8,128)(2,1)}, u32[]{:S(2)}) copy-start(bf16[1,256,1536]{2,1,0:T(8,128)(2,1)} %param.6) | copy-start | bytes 2359300
  36.6 14.0 %collective-permute-start.9 = (bf16[384,384]{1,0:T(8,128)(2,1)S(1)}, bf16[384,384]{1,0:T(8,128)(2,1)S(1)}, u32[]{:S(2)}, u32[]{:S(2)}) collective-permute-start(bf16[384,384]{1,0:T(8,128)(2,1)S(1)} %get-tuple-element.64), channel_id=1, source_target_pairs={{0,12},{1,13},{2,14},{3,15},{4,0},{5,1},{6,2},{7,3},{8,4},{9,5},{1... | collective-permute-start | bytes 884744 | tf_op jit(solution)/shard_map/ppermute | solution.py:32
  39.2 11.3 %collective-permute-start.7 = (bf16[384,384]{1,0:T(8,128)(2,1)S(1)}, bf16[384,384]{1,0:T(8,128)(2,1)S(1)}, u32[]{:S(2)}, u32[]{:S(2)}) collective-permute-start(bf16[384,384]{1,0:T(8,128)(2,1)S(1)} %get-tuple-element.62._), channel_id=1, source_target_pairs={{0,4},{1,5},{2,6},{3,7},{4,8},{5,9},{6,10},{7,11},{8,12},{9,13},{1... | collective-permute-start | bytes 884744 | tf_op jit(solution)/shard_map/ppermute | solution.py:32
  41.8 7.4 %collective-permute-start.10 = (bf16[48,384]{1,0:T(8,128)(2,1)S(1)}, bf16[48,384]{1,0:T(8,128)(2,1)S(1)}, u32[]{:S(2)}, u32[]{:S(2)}) collective-permute-start(bf16[48,384]{1,0:T(8,128)(2,1)S(1)} %get-tuple-element.66), channel_id=1, source_target_pairs={{0,4},{1,5},{2,6},{3,7},{4,8},{5,9},{6,10},{7,11},{8,12},{9,13},{1... | collective-permute-start | bytes 110600 | tf_op jit(solution)/shard_map/ppermute | solution.py:32
  41.9 7.3 %collective-permute-start.11 = (bf16[48,384]{1,0:T(8,128)(2,1)S(1)}, bf16[48,384]{1,0:T(8,128)(2,1)S(1)}, u32[]{:S(2)}, u32[]{:S(2)}) collective-permute-start(bf16[48,384]{1,0:T(8,128)(2,1)S(1)} %get-tuple-element.67), channel_id=1, source_target_pairs={{0,8},{1,9},{2,10},{3,11},{4,12},{5,13},{6,14},{7,15},{8,0},{9,1},... | collective-permute-start | bytes 110600 | tf_op jit(solution)/shard_map/ppermute | solution.py:32
  46.6 4.0 %collective-permute-start.12 = (bf16[48,384]{1,0:T(8,128)(2,1)S(1)}, bf16[48,384]{1,0:T(8,128)(2,1)S(1)}, u32[]{:S(2)}, u32[]{:S(2)}) collective-permute-start(bf16[48,384]{1,0:T(8,128)(2,1)S(1)} %get-tuple-element.68), channel_id=1, source_target_pairs={{0,12},{1,13},{2,14},{3,15},{4,0},{5,1},{6,2},{7,3},{8,4},{9,5},{1... | collective-permute-start | bytes 110600 | tf_op jit(solution)/shard_map/ppermute | solution.py:32
  50.9 1.7 %collective-permute-start.13 = (bf16[208,768]{1,0:T(8,128)(2,1)S(1)}, bf16[208,768]{1,0:T(8,128)(2,1)S(1)}, u32[]{:S(2)}, u32[]{:S(2)}) collective-permute-start(bf16[208,768]{1,0:T(8,128)(2,1)S(1)} %get-tuple-element.70), channel_id=1, source_target_pairs={{0,1},{1,0},{2,3},{3,2},{4,5},{5,4},{6,7},{7,6},{8,9},{9,8},{10,11... | collective-permute-start | bytes 958472 | tf_op jit(solution)/shard_map/ppermute | solution.py:40
  52.8 18.7 %collective-permute-start.14 = (bf16[48,3200]{1,0:T(8,128)(2,1)S(1)}, bf16[48,3200]{1,0:T(8,128)(2,1)S(1)}, u32[]{:S(2)}, u32[]{:S(2)}) collective-permute-start(bf16[48,3200]{1,0:T(8,128)(2,1)S(1)} %get-tuple-element.71._), channel_id=1, source_target_pairs={{0,2},{1,3},{2,0},{3,1},{4,6},{5,7},{6,4},{7,5},{8,10},{9,11},{10,... | collective-permute-start | bytes 921608 | tf_op jit(solution)/shard_map/ppermute | solution.py:36
  71.7 4.7 %collective-permute-start.15 = (bf16[112,384]{1,0:T(8,128)(2,1)S(1)}, bf16[112,384]{1,0:T(8,128)(2,1)S(1)}, u32[]{:S(2)}, u32[]{:S(2)}) collective-permute-start(bf16[112,384]{1,0:T(8,128)(2,1)S(1)} %get-tuple-element.76), channel_id=1, source_target_pairs={{0,64},{16,80},{32,96},{48,112},{64,128},{80,144},{96,160},{112,17... | collective-permute-start | bytes 258056 | tf_op jit(solution)/shard_map/ppermute | solution.py:44
  72.3 6.8 %collective-permute-start.16 = (bf16[112,384]{1,0:T(8,128)(2,1)S(1)}, bf16[112,384]{1,0:T(8,128)(2,1)S(1)}, u32[]{:S(2)}, u32[]{:S(2)}) collective-permute-start(bf16[112,384]{1,0:T(8,128)(2,1)S(1)} %get-tuple-element.77), channel_id=1, source_target_pairs={{0,128},{16,144},{32,160},{48,176},{64,192},{80,208},{96,224},{112... | collective-permute-start | bytes 258056 | tf_op jit(solution)/shard_map/ppermute | solution.py:44
  74.7 5.7 %collective-permute-start.17 = (bf16[112,384]{1,0:T(8,128)(2,1)S(1)}, bf16[112,384]{1,0:T(8,128)(2,1)S(1)}, u32[]{:S(2)}, u32[]{:S(2)}) collective-permute-start(bf16[112,384]{1,0:T(8,128)(2,1)S(1)} %get-tuple-element.78), channel_id=1, source_target_pairs={{0,192},{16,208},{32,224},{48,240},{64,0},{80,16},{96,32},{112,48}... | collective-permute-start | bytes 258056 | tf_op jit(solution)/shard_map/ppermute | solution.py:44
  80.6 6.0 %collective-permute-start.18 = (bf16[112,96]{1,0:T(8,128)(2,1)S(1)}, bf16[112,96]{1,0:T(8,128)(2,1)S(1)}, u32[]{:S(2)}, u32[]{:S(2)}) collective-permute-start(bf16[112,96]{1,0:T(8,128)(2,1)S(1)} %get-tuple-element.80), channel_id=1, source_target_pairs={{0,16},{16,32},{32,48},{48,0},{64,80},{80,96},{96,112},{112,64},{1... | collective-permute-start | bytes 64520 | tf_op jit(solution)/shard_map/ppermute | solution.py:48
  82.8 4.8 %collective-permute-start.19 = (bf16[112,96]{1,0:T(8,128)(2,1)S(1)}, bf16[112,96]{1,0:T(8,128)(2,1)S(1)}, u32[]{:S(2)}, u32[]{:S(2)}) collective-permute-start(bf16[112,96]{1,0:T(8,128)(2,1)S(1)} %get-tuple-element.81), channel_id=1, source_target_pairs={{0,32},{16,48},{32,0},{48,16},{64,96},{80,112},{96,64},{112,80},{1... | collective-permute-start | bytes 64520 | tf_op jit(solution)/shard_map/ppermute | solution.py:48
  83.4 4.4 %collective-permute-start.20 = (bf16[112,96]{1,0:T(8,128)(2,1)S(1)}, bf16[112,96]{1,0:T(8,128)(2,1)S(1)}, u32[]{:S(2)}, u32[]{:S(2)}) collective-permute-start(bf16[112,96]{1,0:T(8,128)(2,1)S(1)} %get-tuple-element.82), channel_id=1, source_target_pairs={{0,48},{16,0},{32,16},{48,32},{64,112},{80,64},{96,80},{112,96},{1... | collective-permute-start | bytes 64520 | tf_op jit(solution)/shard_map/ppermute | solution.py:48

commit v6 on v5

--- a/solution.py
+++ b/solution.py
@@ -151,7 +151,7 @@
         standardise(conv, taps, refs, begin, 112, 2 * HALF + begin, first + HALF + begin, length)
 
 
-def edge_kernel(lengths, top, bottom, chips, beside, taps, _, __, ___, ____, hidden, standard, inverse, x, conv, h, s, i):
+def edge_kernel(lengths, top, bottom, chips, beside, taps, _, __, ___, hidden, standard, inverse, x, conv, h, s, i):
     where = where_of(lengths)
     first, length, core = where[0], where[1], where[2]
     end = first + ROWS
@@ -198,7 +198,7 @@
 KEPT = [pltpu.VMEM((2 * HALF, WIDTH), BF16), pltpu.VMEM((2 * HALF, WIDTH), F32), pltpu.VMEM((2 * HALF, LANES), F32)]
 
 
-def forward_edge(lengths, frames, chips, beside, taps, forward, after):
+def forward_edge(lengths, frames, chips, beside, taps, forward):
     def ends(i):
         return (1 + 15 * i, 0)
 
@@ -216,7 +216,6 @@
             ANY,
             ANY,
             ANY,
-            ANY,
         ],
         out_specs=(
             pl.BlockSpec((HALF, WIDTH), ends),
@@ -228,7 +227,7 @@
         compiler_params=LIMIT,
         cost_estimate=pl.CostEstimate(flops=8_000_000, bytes_accessed=1_000_000, transcendentals=100_000),
         name="forward_edge",
-    )(lengths, frames, frames, chips, beside, taps, *forward, after)
+    )(lengths, frames, frames, chips, beside, taps, *forward)
 
 
 def backward_rows(first, length, upstream, begin, standard, row, inverse, taps, conv_grad, out_row, size, scaled):
@@ -650,15 +649,15 @@
     beside = move_core(jnp.where(core == 0, end, begin))
     cot_other = move_core(cot)
     forward = forward_inner(lengths, frames, taps)
-    hidden, standard, inverse = forward_edge(lengths, frames, chips, beside, taps, forward, cot_other)
+    hidden, standard, inverse = forward_edge(lengths, frames, chips, beside, taps, forward)
     hidden_other = move_core(hidden)
     low = jnp.where(core == 0, chips[2 * HALF :], beside[2 * HALF :])
     high = jnp.where(core == 0, beside[2 * HALF :], chips[2 * HALF :])
+    late_cot, _ = lax.optimization_barrier((jnp.concatenate([low, cot, high], axis=0), hidden))
+    upstream = lax.dot_general(late_cot, out_weight, (((1,), (1,)), ((), ())), preferred_element_type=F32)
     operands = (hidden, hidden_other, cot, cot_other)
-    far_a, far_b = far_products(*operands, low)
-    late_cot, far_a, far_b = lax.optimization_barrier((jnp.concatenate([low, cot, high], axis=0), far_a, far_b))
-    upstream = lax.dot_general(late_cot, out_weight, (((1,), (1,)), ((), ())), preferred_element_type=F32)
-    above_a, above_b, below_a, below_b, own = near_products(*operands, upstream)
+    far_a, far_b = far_products(*operands, upstream)
+    above_a, above_b, below_a, below_b, own = near_products(*operands, far_a)
     up_a = move_y(far_a, 1)
     down_b = move_y(far_b, -1)
     up_b = move_y(above_b, 1)

time: 88.6 us -> 88 us (level)
  starting transfers between devices: 36.1 us -> 35.2 us
    ppermute x4, waiting for transfers between devices: 3.56 us -> 1.61 us  [move_core(): lax.ppermute(value, 'seq', [(seq_at(*p), seq_at(p[0], p[1], p[2] + 1)) fo...]
    ppermute x3, starting transfers between devices: 5.64 us -> 3.9 us  [move_z_lo(): lax.ppermute(value, 'dp', [(x * 4 + z, x * 4 + (z + step) % 4) for x, z i...]
    ppermute x3, waiting for transfers between devices: 1.56 us -> 2.71 us  [move_z_lo(): lax.ppermute(value, 'dp', [(x * 4 + z, x * 4 + (z + step) % 4) for x, z i...]
  transfers between devices with their start and end apart: 21 -> 21, of which waited for: 11 -> 10; matrix products, arithmetic and copies ran while one was open for 5% -> 3% of each run, Pallas kernels for 22% -> 24%
where the time goes in v6:
time: 88 us; the launch traced here: 87.7 us
  starting transfers between devices  35.2 us (40%)
  Pallas kernels  22.9 us (26%)
  waiting for transfers between devices  21.7 us (25%)
  local copies, waits for them, and re-layouts  3.61 us (4%)
  matrix products  1.56 us (2%)
  between operations  1.54 us (2%)
  other arithmetic  1.14 us (1%)
    ppermute x9, starting transfers between devices, move_y(): lax.ppermute(value, 'seq', [(seq_at(*p), seq_at(p[0] + step, p[1], p[2]))...  13.1 us
    ppermute x1, starting transfers between devices, move_neighbour(): lax.ppermute(value, 'seq', [(i, (i + 1) % 16 if i % 2 else (i - 1) % 16)...  9.74 us
    ppermute x1, waiting for transfers between devices, move_z_hi(): lax.ppermute(value, 'seq', [(seq_at(*p), seq_at(p[0], p[1] + 1, p[2])) fo...  7.61 us
    pallas_call x1, Pallas kernels, input_grads(): pl.pallas_call(input_grad_kernel, out_shape=(rows_of((ROWS, WIDTH), BF16)...  5.96 us
    ppermute x3, waiting for transfers between devices, move_x(): lax.ppermute(value, 'dp', [(x * 4 + z, (x + step) % 4 * 4 + z) for x, z i...  5.69 us
    pallas_call x1, Pallas kernels, forward_inner(): pl.pallas_call(inner_kernel, out_shape=FORWARD, in_specs=[SMEM, VMEM, VME...  4.77 us
    ppermute x1, starting transfers between devices, move_z_hi(): lax.ppermute(value, 'seq', [(seq_at(*p), seq_at(p[0], p[1] + 1, p[2])) fo...  4.68 us
    ppermute x9, waiting for transfers between devices, move_y(): lax.ppermute(value, 'seq', [(seq_at(*p), seq_at(p[0] + step, p[1], p[2]))...  4.11 us
  transfers between devices with their start and end apart: 21, of which 10 were waited for; matrix products, arithmetic and copies ran while one was open for 3% of the time, Pallas kernels for 24%

profile of v6, /device:TPU:6, one launch (start us, length us, event | category | flops | bytes accessed | tf_op | source)
XLA Modules:
  0.0 87.7 jit_solution(4970572754782573838)
XLA Ops:
  0.6 0.8 slice_bitcast_fusion.3
  1.5 1.0 %slice_bitcast_fusion.1 = (bf16[32,1536]{1,0:T(8,128)(2,1)S(1)}, bf16[32,1536]{1,0:T(8,128)(2,1)S(1)}) fusion(bf16[1,256,1536]{2,1,0:T(8,128)(2,1)} %param.6), kind=kLoop, calls=%fused_computation.7 | loop fusion | bytes 393216 | tf_op jit(solution)/shard_map/slice | solution.py:646
  2.4 0.1 broadcast_select_fusion.1
  2.5 0.1 collective-permute-start.1
  2.6 9.7 %collective-permute-start = (bf16[48,1536]{1,0:T(8,128)(2,1)S(1)}, bf16[48,1536]{1,0:T(8,128)(2,1)S(1)}, u32[]{:S(2)}, u32[]{:S(2)}) collective-permute-start(bf16[48,1536]{1,0:T(8,128)(2,1)S(1)} %get-tuple-element.88), channel_id=1, source_target_pairs={{0,15},{1,2},{2,1},{3,4},{4,3},{5,6},{6,5},{7,8},{8,7},{9,10},{10,... | collective-permute-start | bytes 442376 | tf_op jit(solution)/shard_map/ppermute | solution.py:52
  12.3 0.0 collective-permute-start.3
  12.3 1.0 %pad_select_fusion.taps = f32[33,1536]{1,0:T(8,128)S(1)} fusion(f32[32,1536]{1,0:T(8,128)} %param.10, f32[1536]{0:T(1024)} %param.11, pred[33]{0:T(512)(128)(4,1)S(1)} %iota_compare_fusion), kind=kLoop, calls=%fused_computation.1 | loop fusion | flops 50688 | bytes 405537 | tf_op jit(solution)/shard_map/jit(_where)/select_n | solution.py:645
  14.0 0.0 copy-start
  14.0 1.1 %copy-done = bf16[1,256,1536]{2,1,0:T(8,128)(2,1)S(1)} copy-done((bf16[1,256,1536]{2,1,0:T(8,128)(2,1)S(1)}, bf16[1,256,1536]{2,1,0:T(8,128)(2,1)}, u32[]{:S(2)}) %copy-start) | copy-done | bytes 786456
  15.1 4.8 %forward_inner.1 = (bf16[288,1536]{1,0:T(8,128)(2,1)S(1)}, f32[288,1536]{1,0:T(8,128)S(1)}, f32[288,128]{1,0:T(8,128)S(1)}) custom-call(s32[1]{0:T(128)S(6)} %copy.16.lengths, bf16[256,1536]{1,0:T(8,128)(2,1)S(1)} %bitcast.14, f32[33,1536]{1,0:T(8,128)S(1)} %pad_select_fusion.taps), custom_call_target="tpu_custom_call" | custom-call | flops 60000000 | bytes 4000000 | tf_op jit(solution)/shard_map/forward_inner/pallas_call | solution.py:180
  19.9 0.0 collective-permute-done.1.beside
  19.9 0.0 collective-permute-done.chips
  19.9 0.0 copy-start.2
  20.0 0.0 copy-start.3
  20.0 1.2 %forward_edge.1 = (bf16[288,1536]{1,0:T(8,128)(2,1)S(1)}, f32[288,1536]{1,0:T(8,128)S(1)}, f32[288,128]{1,0:T(8,128)S(1)}) custom-call(s32[1]{0:T(128)S(6)} %copy.16.lengths, bf16[256,1536]{1,0:T(8,128)(2,1)S(1)} %bitcast.15, bf16[256,1536]{1,0:T(8,128)(2,1)S(1)} %bitcast.16, ...), custom_call_target="tpu_custom_call", output_to_operand_aliasing={{0}: (6, {}), {1}: (7, {}), {2}: (8, {})} | custom-call | flops 8000000 | bytes 1000000 | tf_op jit(solution)/shard_map/forward_edge/pallas_call | solution.py:205
  21.2 0.6 collective-permute-start.2
  21.8 0.1 pad_maximum_fusion
  21.8 0.7 copy-done.3
  22.5 1.6 %fusion._.upstream = f32[288,1536]{1,0:T(8,128)S(1)} fusion(bf16[288,1536]{1,0:T(8,128)(2,1)S(1)} %pad_maximum_fusion, bf16[1536,1536]{1,0:T(8,128)(2,1)S(1)} %copy-done.3), kind=kOutput, calls=%fused_computation.13 | convolution fusion | flops 1358954496 | bytes 7372800 | tf_op jit(solution)/shard_map/dot_general | solution.py:657
  24.1 0.0 collective-permute-done.3.cot_other
  24.1 0.0 collective-permute-done.2.hidden_other
  24.1 0.5 far_products.1
  24.6 0.1 collective-permute-start.5
  24.7 3.2 %collective-permute-start.6 = (bf16[384,384]{1,0:T(8,128)(2,1)S(1)}, bf16[384,384]{1,0:T(8,128)(2,1)S(1)}, u32[]{:S(2)}, u32[]{:S(2)}) collective-permute-start(bf16[384,384]{1,0:T(8,128)(2,1)S(1)} %get-tuple-element.56), channel_id=1, source_target_pairs={{0,12},{1,13},{2,14},{3,15},{4,0},{5,1},{6,2},{7,3},{8,4},{9,5},{1... | collective-permute-start | bytes 884744 | tf_op jit(solution)/shard_map/ppermute | solution.py:32
  28.0 1.1 %near_products.1 = (f32[384,384]{1,0:T(8,128)S(1)}, bf16[384,384]{1,0:T(8,128)(2,1)S(1)}, bf16[384,384]{1,0:T(8,128)(2,1)S(1)}, f32[384,384]{1,0:T(8,128)S(1)}, f32[384,768]{1,0:T(8,128)S(1)}) custom-call(bf16[288,1536]{1,0:T(8,128)(2,1)S(1)} %get-tuple-element.46.hidden, bf16[288,1536]{1,0:T(8,128)(2,1)S(1)} %collective-permute-done.2.hidden_other, ...), custom_call_target="tpu_custom_call" | custom-call | flops 500000 | bytes 1500000 | tf_op jit(solution)/shard_map/near_products/pallas_call | solution.py:429
  29.1 0.1 collective-permute-start.4
  29.2 2.0 %collective-permute-start.8 = (bf16[384,384]{1,0:T(8,128)(2,1)S(1)}, bf16[384,384]{1,0:T(8,128)(2,1)S(1)}, u32[]{:S(2)}, u32[]{:S(2)}) collective-permute-start(bf16[384,384]{1,0:T(8,128)(2,1)S(1)} %get-tuple-element.59), channel_id=1, source_target_pairs={{0,4},{1,5},{2,6},{3,7},{4,8},{5,9},{6,10},{7,11},{8,12},{9,13},{1... | collective-permute-start | bytes 884744 | tf_op jit(solution)/shard_map/ppermute | solution.py:32
  31.2 1.3 %backward.1 = (bf16[256,1536]{1,0:T(8,128)(2,1)S(1)}, f32[8,1536]{1,0:T(8,128)S(1)}) custom-call(s32[1]{0:T(128)S(6)} %copy.16.lengths, f32[288,1536]{1,0:T(8,128)S(1)} %fusion._.upstream, f32[288,1536]{1,0:T(8,128)S(1)} %get-tuple-element.48.standard, f32[288,128]{1,0:T(8,128)S(1)} %get-tuple-element.49.inverse, f32[33,1536]{1,0:T(8,128)S(1)} %pad_select_fusion.taps, ...), custom_call_target="tpu_custom_call" | custom-call | flops 10000000 | bytes 4000000 | tf_op jit(solution)/shard_map/backward/pallas_call | solution.py:271
  32.5 2.6 %kernel_grads_first.1._.first = f32[40,768]{1,0:T(8,128)S(1)} custom-call(s32[1]{0:T(128)S(6)} %copy.16.lengths, bf16[256,1536]{1,0:T(8,128)(2,1)S(1)} %bitcast.17, bf16[48,1536]{1,0:T(8,128)(2,1)S(1)} %collective-permute-done.chips, bf16[48,1536]{1,0:T(8,128)(2,1)S(1)} %collective-permute-done.1.beside, bf16[256,1536]{1,0:T(8,128)(2,1)S(1)} %get-tuple-element.52.conv_grad, ...), custom_call_target="tpu_custom_call" | custom-call | flops 25000000 | bytes 1000000 | tf_op jit(solution)/shard_map/kernel_grads_first/pallas_call | solution.py:376
  35.1 0.7 collective-permute-done.5.up_a
  35.7 0.0 collective-permute-done.6.down_b
  35.7 0.1 seconds.1
  35.9 0.3 collective-permute-start.7
  36.1 3.3 %collective-permute-start.9 = (bf16[384,384]{1,0:T(8,128)(2,1)S(1)}, bf16[384,384]{1,0:T(8,128)(2,1)S(1)}, u32[]{:S(2)}, u32[]{:S(2)}) collective-permute-start(bf16[384,384]{1,0:T(8,128)(2,1)S(1)} %get-tuple-element.60), channel_id=1, source_target_pairs={{0,12},{1,13},{2,14},{3,15},{4,0},{5,1},{6,2},{7,3},{8,4},{9,5},{1... | collective-permute-start | bytes 884744 | tf_op jit(solution)/shard_map/ppermute | solution.py:32
  39.5 2.6 %kernel_grads_other.1 = (f32[48,384]{1,0:T(8,128)S(1)}, bf16[48,384]{1,0:T(8,128)(2,1)S(1)}, bf16[48,384]{1,0:T(8,128)(2,1)S(1)}, bf16[48,384]{1,0:T(8,128)(2,1)S(1)}) custom-call(s32[1]{0:T(128)S(6)} %copy.16.lengths, bf16[256,1536]{1,0:T(8,128)(2,1)S(1)} %bitcast.18, bf16[48,1536]{1,0:T(8,128)(2,1)S(1)} %collective-permute-done.chips, ...), custom_call_target="tpu_custom_call" | custom-call | flops 25000000 | bytes 1000000 | tf_op jit(solution)/shard_map/kernel_grads_other/pallas_call | solution.py:389
  42.1 0.1 collective-permute-start.10
  42.1 0.0 collective-permute-done.4.down_a
  42.2 3.4 %collective-permute-start.11 = (bf16[48,384]{1,0:T(8,128)(2,1)S(1)}, bf16[48,384]{1,0:T(8,128)(2,1)S(1)}, u32[]{:S(2)}, u32[]{:S(2)}) collective-permute-start(bf16[48,384]{1,0:T(8,128)(2,1)S(1)} %get-tuple-element.63), channel_id=1, source_target_pairs={{0,8},{1,9},{2,10},{3,11},{4,12},{5,13},{6,14},{7,15},{8,0},{9,1},... | collective-permute-start | bytes 110600 | tf_op jit(solution)/shard_map/ppermute | solution.py:32
  45.5 0.6 collective-permute-start.12
  46.1 3.4 %collective-permute-done.10.k1 = bf16[48,384]{1,0:T(8,128)(2,1)S(1)} collective-permute-done((bf16[48,384]{1,0:T(8,128)(2,1)S(1)}, bf16[48,384]{1,0:T(8,128)(2,1)S(1)}, u32[]{:S(2)}, u32[]{:S(2)}) %collective-permute-start.10) | collective-permute-done | bytes 36896 | tf_op jit(solution)/shard_map/ppermute | solution.py:32
  49.6 0.0 collective-permute-done.7.up_a
  49.6 0.0 collective-permute-done.9.down_b
  49.6 0.4 blocks.1
  50.0 0.1 collective-permute-start.13
  50.1 1.6 %collective-permute-done.13.other = bf16[208,768]{1,0:T(8,128)(2,1)S(1)} collective-permute-done((bf16[208,768]{1,0:T(8,128)(2,1)S(1)}, bf16[208,768]{1,0:T(8,128)(2,1)S(1)}, u32[]{:S(2)}, u32[]{:S(2)}) %collective-permute-start.13) | collective-permute-done | bytes 319520 | tf_op jit(solution)/shard_map/ppermute | solution.py:40
  51.7 0.1 chip_blocks.1
  51.9 4.7 %collective-permute-start.14 = (bf16[48,3200]{1,0:T(8,128)(2,1)S(1)}, bf16[48,3200]{1,0:T(8,128)(2,1)S(1)}, u32[]{:S(2)}, u32[]{:S(2)}) collective-permute-start(bf16[48,3200]{1,0:T(8,128)(2,1)S(1)} %get-tuple-element.67._), channel_id=1, source_target_pairs={{0,2},{1,3},{2,0},{3,1},{4,6},{5,7},{6,4},{7,5},{8,10},{9,11},{10,... | collective-permute-start | bytes 921608 | tf_op jit(solution)/shard_map/ppermute | solution.py:36
  56.5 1.3 %outer_grads.1.outer = bf16[32,1536]{1,0:T(8,128)(2,1)S(1)} custom-call(s32[1]{0:T(128)S(6)} %copy.16.lengths, bf16[256,1536]{1,0:T(8,128)(2,1)S(1)} %bitcast.19, bf16[48,1536]{1,0:T(8,128)(2,1)S(1)} %collective-permute-done.chips, bf16[48,1536]{1,0:T(8,128)(2,1)S(1)} %collective-permute-done.1.beside, f32[33,1536]{1,0:T(8,128)S(1)} %pad_select_fusion.taps, ...), custom_call_target="tpu_custom_call" | custom-call | flops 8000000 | bytes 1000000 | tf_op jit(solution)/shard_map/outer_grads/pallas_call | solution.py:300
  57.8 6.0 %input_grads.1 = (bf16[256,1536]{1,0:T(8,128)(2,1)}, f32[8,128]{1,0:T(8,128)S(1)}) custom-call(s32[1]{0:T(128)S(6)} %copy.16.lengths, bf16[256,1536]{1,0:T(8,128)(2,1)S(1)} %get-tuple-element.52.conv_grad, bf16[32,1536]{1,0:T(8,128)(2,1)S(1)} %outer_grads.1.outer, f32[33,1536]{1,0:T(8,128)S(1)} %pad_select_fusion.taps, bf16[48,3200]{1,0:T(8,128)(2,1)S(1)} %get-tuple-element.67._), custom_call_target="tpu_custom_call" | custom-call | flops 50000000 | bytes 2000000 | tf_op jit(solution)/shard_map/input_grads/pallas_call | solution.py:416
  63.8 7.6 %collective-permute-done.14.other = bf16[48,3200]{1,0:T(8,128)(2,1)S(1)} collective-permute-done((bf16[48,3200]{1,0:T(8,128)(2,1)S(1)}, bf16[48,3200]{1,0:T(8,128)(2,1)S(1)}, u32[]{:S(2)}, u32[]{:S(2)}) %collective-permute-start.14) | collective-permute-done | bytes 307232 | tf_op jit(solution)/shard_map/ppermute | solution.py:36
  71.4 0.2 squares.1
  71.6 0.6 collective-permute-start.15
  72.1 2.4 %collective-permute-start.16 = (bf16[112,384]{1,0:T(8,128)(2,1)S(1)}, bf16[112,384]{1,0:T(8,128)(2,1)S(1)}, u32[]{:S(2)}, u32[]{:S(2)}) collective-permute-start(bf16[112,384]{1,0:T(8,128)(2,1)S(1)} %get-tuple-element.73), channel_id=1, source_target_pairs={{0,128},{16,144},{32,160},{48,176},{64,192},{80,208},{96,224},{112... | collective-permute-start | bytes 258056 | tf_op jit(solution)/shard_map/ppermute | solution.py:44
  74.6 0.0 collective-permute-start.17
  74.6 1.6 %collective-permute-done.15.one = bf16[112,384]{1,0:T(8,128)(2,1)S(1)} collective-permute-done((bf16[112,384]{1,0:T(8,128)(2,1)S(1)}, bf16[112,384]{1,0:T(8,128)(2,1)S(1)}, u32[]{:S(2)}, u32[]{:S(2)}) %collective-permute-start.15) | collective-permute-done | bytes 86048 | tf_op jit(solution)/shard_map/ppermute | solution.py:44
  76.2 2.7 %collective-permute-done.16.two = bf16[112,384]{1,0:T(8,128)(2,1)S(1)} collective-permute-done((bf16[112,384]{1,0:T(8,128)(2,1)S(1)}, bf16[112,384]{1,0:T(8,128)(2,1)S(1)}, u32[]{:S(2)}, u32[]{:S(2)}) %collective-permute-start.16) | collective-permute-done | bytes 86048 | tf_op jit(solution)/shard_map/ppermute | solution.py:44
  78.8 1.4 %collective-permute-done.17.three = bf16[112,384]{1,0:T(8,128)(2,1)S(1)} collective-permute-done((bf16[112,384]{1,0:T(8,128)(2,1)S(1)}, bf16[112,384]{1,0:T(8,128)(2,1)S(1)}, u32[]{:S(2)}, u32[]{:S(2)}) %collective-permute-start.17) | collective-permute-done | bytes 86048 | tf_op jit(solution)/shard_map/ppermute | solution.py:44
  80.3 0.2 quarters.1
  80.4 1.4 %collective-permute-start.18 = (bf16[112,96]{1,0:T(8,128)(2,1)S(1)}, bf16[112,96]{1,0:T(8,128)(2,1)S(1)}, u32[]{:S(2)}, u32[]{:S(2)}) collective-permute-start(bf16[112,96]{1,0:T(8,128)(2,1)S(1)} %get-tuple-element.76), channel_id=1, source_target_pairs={{0,16},{16,32},{32,48},{48,0},{64,80},{80,96},{96,112},{112,64},{1... | collective-permute-start | bytes 64520 | tf_op jit(solution)/shard_map/ppermute | solution.py:48
  81.9 2.5 %collective-permute-start.20 = (bf16[112,96]{1,0:T(8,128)(2,1)S(1)}, bf16[112,96]{1,0:T(8,128)(2,1)S(1)}, u32[]{:S(2)}, u32[]{:S(2)}) collective-permute-start(bf16[112,96]{1,0:T(8,128)(2,1)S(1)} %get-tuple-element.78), channel_id=1, source_target_pairs={{0,48},{16,0},{32,16},{48,32},{64,112},{80,64},{96,80},{112,96},{1... | collective-permute-start | bytes 64520 | tf_op jit(solution)/shard_map/ppermute | solution.py:48
  84.4 1.8 %collective-permute-done.18.one = bf16[112,96]{1,0:T(8,128)(2,1)S(1)} collective-permute-done((bf16[112,96]{1,0:T(8,128)(2,1)S(1)}, bf16[112,96]{1,0:T(8,128)(2,1)S(1)}, u32[]{:S(2)}, u32[]{:S(2)}) %collective-permute-start.18) | collective-permute-done | bytes 21536 | tf_op jit(solution)/shard_map/ppermute | solution.py:48
  86.2 0.7 collective-permute-done.19.two
  86.9 0.1 collective-permute-done.20.three
  87.1 0.6 means.1
  (9 shorter events, 0.0 us)
Async XLA Ops:
  2.5 17.4 %collective-permute-start.1 = (bf16[48,1536]{1,0:T(8,128)(2,1)S(1)}, bf16[48,1536]{1,0:T(8,128)(2,1)S(1)}, u32[]{:S(2)}, u32[]{:S(2)}) collective-permute-start(bf16[48,1536]{1,0:T(8,128)(2,1)S(1)} %get-tuple-element.89), channel_id=1, source_target_pairs={{0,1},{1,0},{2,3},{3,2},{4,5},{5,4},{6,7},{7,6},{8,9},{9,8},{10,11... | collective-permute-start | bytes 442376 | tf_op jit(solution)/shard_map/ppermute | solution.py:40
  2.6 17.3 %collective-permute-start = (bf16[48,1536]{1,0:T(8,128)(2,1)S(1)}, bf16[48,1536]{1,0:T(8,128)(2,1)S(1)}, u32[]{:S(2)}, u32[]{:S(2)}) collective-permute-start(bf16[48,1536]{1,0:T(8,128)(2,1)S(1)} %get-tuple-element.88), channel_id=1, source_target_pairs={{0,15},{1,2},{2,1},{3,4},{4,3},{5,6},{6,5},{7,8},{8,7},{9,10},{10,... | collective-permute-start | bytes 442376 | tf_op jit(solution)/shard_map/ppermute | solution.py:52
  12.3 11.8 %collective-permute-start.3 = (bf16[256,1536]{1,0:T(8,128)(2,1)}, bf16[256,1536]{1,0:T(8,128)(2,1)S(1)}, u32[]{:S(2)}, u32[]{:S(2)}) collective-permute-start(bf16[256,1536]{1,0:T(8,128)(2,1)} %bitcast.20), channel_id=1, source_target_pairs={{0,1},{1,0},{2,3},{3,2},{4,5},{5,4},{6,7},{7,6},{8,9},{9,8},{10,11... | collective-permute-start | bytes 2359304 | tf_op jit(solution)/shard_map/ppermute | solution.py:40
  14.0 1.1 %copy-start = (bf16[1,256,1536]{2,1,0:T(8,128)(2,1)S(1)}, bf16[1,256,1536]{2,1,0:T(8,128)(2,1)}, u32[]{:S(2)}) copy-start(bf16[1,256,1536]{2,1,0:T(8,128)(2,1)} %param.6) | copy-start | bytes 2359300
  19.9 1.8 %copy-start.2 = (bf16[1,256,1536]{2,1,0:T(8,128)(2,1)S(1)}, bf16[1,256,1536]{2,1,0:T(8,128)(2,1)}, u32[]{:S(2)}) copy-start(bf16[1,256,1536]{2,1,0:T(8,128)(2,1)} %param.7) | copy-start | bytes 2359300
  20.0 2.6 %copy-start.3 = (bf16[1536,1536]{1,0:T(8,128)(2,1)S(1)}, bf16[1536,1536]{1,0:T(8,128)(2,1)}, u32[]{:S(2)}) copy-start(bf16[1536,1536]{1,0:T(8,128)(2,1)} %param.9) | copy-start | bytes 14155780
  21.2 3.0 %collective-permute-start.2 = (bf16[288,1536]{1,0:T(8,128)(2,1)S(1)}, bf16[288,1536]{1,0:T(8,128)(2,1)S(1)}, u32[]{:S(2)}, u32[]{:S(2)}) collective-permute-start(bf16[288,1536]{1,0:T(8,128)(2,1)S(1)} %get-tuple-element.46.hidden), channel_id=1, source_target_pairs={{0,1},{1,0},{2,3},{3,2},{4,5},{5,4},{6,7},{7,6},{8,9},{9,8},{10,11... | collective-permute-start | bytes 2654216 | tf_op jit(solution)/shard_map/ppermute | solution.py:40
  24.6 11.1 %collective-permute-start.5 = (bf16[384,384]{1,0:T(8,128)(2,1)S(1)}, bf16[384,384]{1,0:T(8,128)(2,1)S(1)}, u32[]{:S(2)}, u32[]{:S(2)}) collective-permute-start(bf16[384,384]{1,0:T(8,128)(2,1)S(1)} %get-tuple-element.50._), channel_id=1, source_target_pairs={{0,4},{1,5},{2,6},{3,7},{4,8},{5,9},{6,10},{7,11},{8,12},{9,13},{1... | collective-permute-start | bytes 884744 | tf_op jit(solution)/shard_map/ppermute | solution.py:32
  24.7 11.0 %collective-permute-start.6 = (bf16[384,384]{1,0:T(8,128)(2,1)S(1)}, bf16[384,384]{1,0:T(8,128)(2,1)S(1)}, u32[]{:S(2)}, u32[]{:S(2)}) collective-permute-start(bf16[384,384]{1,0:T(8,128)(2,1)S(1)} %get-tuple-element.56), channel_id=1, source_target_pairs={{0,12},{1,13},{2,14},{3,15},{4,0},{5,1},{6,2},{7,3},{8,4},{9,5},{1... | collective-permute-start | bytes 884744 | tf_op jit(solution)/shard_map/ppermute | solution.py:32
  29.1 13.1 %collective-permute-start.4 = (bf16[384,384]{1,0:T(8,128)(2,1)S(1)}, bf16[384,384]{1,0:T(8,128)(2,1)S(1)}, u32[]{:S(2)}, u32[]{:S(2)}) collective-permute-start(bf16[384,384]{1,0:T(8,128)(2,1)S(1)} %get-tuple-element.53), channel_id=1, source_target_pairs={{0,12},{1,13},{2,14},{3,15},{4,0},{5,1},{6,2},{7,3},{8,4},{9,5},{1... | collective-permute-start | bytes 884744 | tf_op jit(solution)/shard_map/ppermute | solution.py:32
  29.2 16.4 %collective-permute-start.8 = (bf16[384,384]{1,0:T(8,128)(2,1)S(1)}, bf16[384,384]{1,0:T(8,128)(2,1)S(1)}, u32[]{:S(2)}, u32[]{:S(2)}) collective-permute-start(bf16[384,384]{1,0:T(8,128)(2,1)S(1)} %get-tuple-element.59), channel_id=1, source_target_pairs={{0,4},{1,5},{2,6},{3,7},{4,8},{5,9},{6,10},{7,11},{8,12},{9,13},{1... | collective-permute-start | bytes 884744 | tf_op jit(solution)/shard_map/ppermute | solution.py:32
  31.2 1.3 %copy-start.1 = (bf16[1,256,1536]{2,1,0:T(8,128)(2,1)S(1)}, bf16[1,256,1536]{2,1,0:T(8,128)(2,1)}, u32[]{:S(2)}) copy-start(bf16[1,256,1536]{2,1,0:T(8,128)(2,1)} %param.6) | copy-start | bytes 2359300
  35.9 13.7 %collective-permute-start.7 = (bf16[384,384]{1,0:T(8,128)(2,1)S(1)}, bf16[384,384]{1,0:T(8,128)(2,1)S(1)}, u32[]{:S(2)}, u32[]{:S(2)}) collective-permute-start(bf16[384,384]{1,0:T(8,128)(2,1)S(1)} %get-tuple-element.58._), channel_id=1, source_target_pairs={{0,4},{1,5},{2,6},{3,7},{4,8},{5,9},{6,10},{7,11},{8,12},{9,13},{1... | collective-permute-start | bytes 884744 | tf_op jit(solution)/shard_map/ppermute | solution.py:32
  36.1 13.5 %collective-permute-start.9 = (bf16[384,384]{1,0:T(8,128)(2,1)S(1)}, bf16[384,384]{1,0:T(8,128)(2,1)S(1)}, u32[]{:S(2)}, u32[]{:S(2)}) collective-permute-start(bf16[384,384]{1,0:T(8,128)(2,1)S(1)} %get-tuple-element.60), channel_id=1, source_target_pairs={{0,12},{1,13},{2,14},{3,15},{4,0},{5,1},{6,2},{7,3},{8,4},{9,5},{1... | collective-permute-start | bytes 884744 | tf_op jit(solution)/shard_map/ppermute | solution.py:32
  42.1 7.5 %collective-permute-start.10 = (bf16[48,384]{1,0:T(8,128)(2,1)S(1)}, bf16[48,384]{1,0:T(8,128)(2,1)S(1)}, u32[]{:S(2)}, u32[]{:S(2)}) collective-permute-start(bf16[48,384]{1,0:T(8,128)(2,1)S(1)} %get-tuple-element.62), channel_id=1, source_target_pairs={{0,4},{1,5},{2,6},{3,7},{4,8},{5,9},{6,10},{7,11},{8,12},{9,13},{1... | collective-permute-start | bytes 110600 | tf_op jit(solution)/shard_map/ppermute | solution.py:32
  42.2 7.4 %collective-permute-start.11 = (bf16[48,384]{1,0:T(8,128)(2,1)S(1)}, bf16[48,384]{1,0:T(8,128)(2,1)S(1)}, u32[]{:S(2)}, u32[]{:S(2)}) collective-permute-start(bf16[48,384]{1,0:T(8,128)(2,1)S(1)} %get-tuple-element.63), channel_id=1, source_target_pairs={{0,8},{1,9},{2,10},{3,11},{4,12},{5,13},{6,14},{7,15},{8,0},{9,1},... | collective-permute-start | bytes 110600 | tf_op jit(solution)/shard_map/ppermute | solution.py:32
  45.5 4.0 %collective-permute-start.12 = (bf16[48,384]{1,0:T(8,128)(2,1)S(1)}, bf16[48,384]{1,0:T(8,128)(2,1)S(1)}, u32[]{:S(2)}, u32[]{:S(2)}) collective-permute-start(bf16[48,384]{1,0:T(8,128)(2,1)S(1)} %get-tuple-element.64), channel_id=1, source_target_pairs={{0,12},{1,13},{2,14},{3,15},{4,0},{5,1},{6,2},{7,3},{8,4},{9,5},{1... | collective-permute-start | bytes 110600 | tf_op jit(solution)/shard_map/ppermute | solution.py:32
  50.0 1.7 %collective-permute-start.13 = (bf16[208,768]{1,0:T(8,128)(2,1)S(1)}, bf16[208,768]{1,0:T(8,128)(2,1)S(1)}, u32[]{:S(2)}, u32[]{:S(2)}) collective-permute-start(bf16[208,768]{1,0:T(8,128)(2,1)S(1)} %get-tuple-element.66), channel_id=1, source_target_pairs={{0,1},{1,0},{2,3},{3,2},{4,5},{5,4},{6,7},{7,6},{8,9},{9,8},{10,11... | collective-permute-start | bytes 958472 | tf_op jit(solution)/shard_map/ppermute | solution.py:40
  51.9 19.5 %collective-permute-start.14 = (bf16[48,3200]{1,0:T(8,128)(2,1)S(1)}, bf16[48,3200]{1,0:T(8,128)(2,1)S(1)}, u32[]{:S(2)}, u32[]{:S(2)}) collective-permute-start(bf16[48,3200]{1,0:T(8,128)(2,1)S(1)} %get-tuple-element.67._), channel_id=1, source_target_pairs={{0,2},{1,3},{2,0},{3,1},{4,6},{5,7},{6,4},{7,5},{8,10},{9,11},{10,... | collective-permute-start | bytes 921608 | tf_op jit(solution)/shard_map/ppermute | solution.py:36
  71.6 4.6 %collective-permute-start.15 = (bf16[112,384]{1,0:T(8,128)(2,1)S(1)}, bf16[112,384]{1,0:T(8,128)(2,1)S(1)}, u32[]{:S(2)}, u32[]{:S(2)}) collective-permute-start(bf16[112,384]{1,0:T(8,128)(2,1)S(1)} %get-tuple-element.72), channel_id=1, source_target_pairs={{0,64},{16,80},{32,96},{48,112},{64,128},{80,144},{96,160},{112,17... | collective-permute-start | bytes 258056 | tf_op jit(solution)/shard_map/ppermute | solution.py:44
  72.1 6.7 %collective-permute-start.16 = (bf16[112,384]{1,0:T(8,128)(2,1)S(1)}, bf16[112,384]{1,0:T(8,128)(2,1)S(1)}, u32[]{:S(2)}, u32[]{:S(2)}) collective-permute-start(bf16[112,384]{1,0:T(8,128)(2,1)S(1)} %get-tuple-element.73), channel_id=1, source_target_pairs={{0,128},{16,144},{32,160},{48,176},{64,192},{80,208},{96,224},{112... | collective-permute-start | bytes 258056 | tf_op jit(solution)/shard_map/ppermute | solution.py:44
  74.6 5.7 %collective-permute-start.17 = (bf16[112,384]{1,0:T(8,128)(2,1)S(1)}, bf16[112,384]{1,0:T(8,128)(2,1)S(1)}, u32[]{:S(2)}, u32[]{:S(2)}) collective-permute-start(bf16[112,384]{1,0:T(8,128)(2,1)S(1)} %get-tuple-element.74), channel_id=1, source_target_pairs={{0,192},{16,208},{32,224},{48,240},{64,0},{80,16},{96,32},{112,48}... | collective-permute-start | bytes 258056 | tf_op jit(solution)/shard_map/ppermute | solution.py:44
  80.4 5.7 %collective-permute-start.18 = (bf16[112,96]{1,0:T(8,128)(2,1)S(1)}, bf16[112,96]{1,0:T(8,128)(2,1)S(1)}, u32[]{:S(2)}, u32[]{:S(2)}) collective-permute-start(bf16[112,96]{1,0:T(8,128)(2,1)S(1)} %get-tuple-element.76), channel_id=1, source_target_pairs={{0,16},{16,32},{32,48},{48,0},{64,80},{80,96},{96,112},{112,64},{1... | collective-permute-start | bytes 64520 | tf_op jit(solution)/shard_map/ppermute | solution.py:48
  81.9 5.0 %collective-permute-start.19 = (bf16[112,96]{1,0:T(8,128)(2,1)S(1)}, bf16[112,96]{1,0:T(8,128)(2,1)S(1)}, u32[]{:S(2)}, u32[]{:S(2)}) collective-permute-start(bf16[112,96]{1,0:T(8,128)(2,1)S(1)} %get-tuple-element.77), channel_id=1, source_target_pairs={{0,32},{16,48},{32,0},{48,16},{64,96},{80,112},{96,64},{112,80},{1... | collective-permute-start | bytes 64520 | tf_op jit(solution)/shard_map/ppermute | solution.py:48
  81.9 5.2 %collective-permute-start.20 = (bf16[112,96]{1,0:T(8,128)(2,1)S(1)}, bf16[112,96]{1,0:T(8,128)(2,1)S(1)}, u32[]{:S(2)}, u32[]{:S(2)}) collective-permute-start(bf16[112,96]{1,0:T(8,128)(2,1)S(1)} %get-tuple-element.78), channel_id=1, source_target_pairs={{0,48},{16,0},{32,16},{48,32},{64,112},{80,64},{96,80},{112,96},{1... | collective-permute-start | bytes 64520 | tf_op jit(solution)/shard_map/ppermute | solution.py:48
